TPU v7x, 32 devices: a whole 2x2x4 slice. The times are simulated.
32 devices in a mesh: group: 4 (over z), dom: 8 (over y, x, core).
Axes of the slice: x: 2, y: 2, z: 4, core: 2. Of those that a mesh axis runs over, the one named last changes fastest.
Arguments:
- query_rows: bfloat16 [24576, 256], P(('group', 'dom')), may hold values from -64 to 64
- key_rows: bfloat16 [24576, 256], P(('group', 'dom')), may hold values from -6 to 6
- value_rows: bfloat16 [24576, 256], P(('group', 'dom')), may hold values from -6 to 6
- out_weight: bfloat16 [256, 256], replicated, may hold values from -1.5 to 1.5
- grad_update: bfloat16 [24576, 256], P(('group', 'dom')), may hold values from -6 to 6
- expander_bias: float32 [8], replicated, may hold values from 1 to 5
- tile_block: int32 [32, 6, 8], P(('group', 'dom')), may hold values from 0 to 13, as said below
- tile_count: int32 [32, 6], P(('group', 'dom')), may hold values from 5 to 8, as said below
- send_block: int32 [32, 8], P(('group', 'dom')), may hold values from 0 to 5
- matching: int32 [32, 3, 768], P(('group', 'dom')), may hold values from 0 to 767, each once within a row
Outputs:
- update: bfloat16 [24576, 256], P(('group', 'dom'))
- query_grad: float32 [24576, 256], P(('group', 'dom'))
- key_grad: float32 [24576, 256], P(('group', 'dom'))
- value_grad: float32 [24576, 256], P(('group', 'dom'))
- weight_grad: float32 [256, 256], replicated
Inputs may be any that keep to these rules, and one draw needn't show every extreme that they name: `tile_block`: slot 0 of block b names entry b, the block itself. `tile_count`: some block has all 8 slots in use. `matching`: each row is a permutation of the 768 nodes.
All inputs are finite; a program needn't handle non-finite values.
Results may differ from a plain program's by a relative error of at most 0.035.
Values may be sent and summed in bfloat16 or wider, within the bound.
A program may use at most 128 MiB of HBM per device.

v0:
```python
import jax
import jax.numpy as jnp
from jax import lax
from jax.sharding import PartitionSpec as P


def from_partner(array, axis, apart):
    return lax.ppermute(array, axis, [(i, i ^ 1 << apart) for i in range(lax.axis_size(axis))])


def outgoing(key_rows, value_rows, send_block, block_rows):
    feature_width = key_rows.shape[1]
    key_blocks = key_rows.reshape(-1, block_rows, feature_width)[send_block]
    value_blocks = value_rows.reshape(-1, block_rows, feature_width)[send_block]
    return (key_blocks, value_blocks)


def block_table(own_rows, received, block_rows):
    feature_width = own_rows.shape[1]
    return jnp.concatenate([own_rows.reshape(-1, block_rows, feature_width), received], axis=0)


def pick_blocks(table, tile_block, slot_index, template):
    return table[tile_block[:, slot_index]].reshape(template.shape)


def tile_scores(query_heads, picked_keys, tile_count, slot_index, score_scale):
    scores = (
        jnp.einsum("bqhd,bkhd->bqhk", query_heads, picked_keys, preferred_element_type=jnp.float32)
        * score_scale
    )
    live_blocks = slot_index < tile_count
    return jnp.where(live_blocks[:, None, None, None], scores, -jnp.inf)


def shards(
    query_rows,
    key_rows,
    value_rows,
    out_weight,
    grad_update,
    expander_bias,
    tile_block,
    tile_count,
    send_block,
    matching,
):
    node_count, feature_width = query_rows.shape
    head_count = expander_bias.shape[0]
    head_dim = feature_width // head_count
    score_scale = head_dim ** (-0.5)
    tile_block = tile_block[0]
    tile_count = tile_count[0]
    send_block = send_block[0]
    matching = matching[0]
    block_count, slot_count = tile_block.shape
    block_rows = node_count // block_count
    devices = lax.axis_size(("group", "dom"))
    top_bit = devices.bit_length() - 1
    query_heads = query_rows.reshape(block_count, block_rows, head_count, head_dim)
    query_flat = query_rows.reshape(node_count, head_count, head_dim)
    sent_keys, sent_values = outgoing(key_rows, value_rows, send_block, block_rows)
    got_keys, got_values = (
        lax.all_to_all(sent_keys, "dom", split_axis=0, concat_axis=0, tiled=True),
        lax.all_to_all(sent_values, "dom", split_axis=0, concat_axis=0, tiled=True),
    )
    table_keys = block_table(key_rows, got_keys, block_rows)
    far_keys = []
    far_values = []
    for turn in range(3):
        moved_keys, moved_values = from_partner(
            (key_rows, value_rows), ("group", "dom"), top_bit - 1 - turn
        )
        far_keys.append(moved_keys[matching[turn]].reshape(node_count, head_count, head_dim))
        far_values.append(moved_values[matching[turn]].reshape(node_count, head_count, head_dim))
    far_keys = jnp.stack(far_keys)
    far_values = jnp.stack(far_values)
    edge_scores = (
        jnp.einsum("nhd,mnhd->nhm", query_flat, far_keys, preferred_element_type=jnp.float32)
        * score_scale
    )
    edge_scores = edge_scores + expander_bias[None, :, None]
    edge_top = edge_scores.max(axis=2)
    start_top = edge_top.reshape(block_count, block_rows, head_count)
    start_total = (
        jnp.exp(edge_scores - edge_top[..., None])
        .sum(axis=2)
        .reshape(block_count, block_rows, head_count)
    )

    def first_pass(slot_index, running):
        row_top, row_total = running
        picked_keys = pick_blocks(table_keys, tile_block, slot_index, query_heads)
        scores = tile_scores(query_heads, picked_keys, tile_count, slot_index, score_scale)
        newer = jnp.maximum(row_top, scores.max(axis=3))
        row_total = row_total * jnp.exp(row_top - newer) + jnp.exp(scores - newer[..., None]).sum(
            axis=3
        )
        return (newer, row_total)

    row_top, row_total = lax.fori_loop(0, slot_count, first_pass, (start_top, start_total))
    table_values = block_table(value_rows, got_values, block_rows)
    flat_top = row_top.reshape(node_count, head_count)
    flat_total = row_total.reshape(node_count, head_count)
    edge_prob = jnp.exp(edge_scores - flat_top[..., None]) / flat_total[..., None]
    edge_weight = edge_prob.astype(jnp.bfloat16)
    start_mix = jnp.einsum(
        "nhm,mnhd->nhd", edge_weight, far_values, preferred_element_type=jnp.float32
    )
    start_mix = start_mix.reshape(block_count, block_rows, head_count, head_dim)

    def second_pass(slot_index, accumulated):
        picked_keys = pick_blocks(table_keys, tile_block, slot_index, query_heads)
        picked_values = pick_blocks(table_values, tile_block, slot_index, query_heads)
        scores = tile_scores(query_heads, picked_keys, tile_count, slot_index, score_scale)
        weight = (jnp.exp(scores - row_top[..., None]) / row_total[..., None]).astype(jnp.bfloat16)
        return accumulated + jnp.einsum(
            "bqhk,bkhd->bqhd", weight, picked_values, preferred_element_type=jnp.float32
        )

    mixed = lax.fori_loop(0, slot_count, second_pass, start_mix)
    attended = mixed.reshape(node_count, feature_width).astype(jnp.bfloat16)
    update = jnp.dot(attended, out_weight, preferred_element_type=jnp.float32).astype(jnp.bfloat16)
    grad_attended = jnp.dot(grad_update, out_weight.T, preferred_element_type=jnp.float32).astype(
        jnp.bfloat16
    )
    weight_term = jnp.dot(attended.T, grad_update, preferred_element_type=jnp.float32)
    weight_grad = lax.psum(weight_term, ("group", "dom")) * (node_count * devices) ** (-0.5)
    grad_flat = grad_attended.reshape(node_count, head_count, head_dim)
    grad_heads = grad_attended.reshape(block_count, block_rows, head_count, head_dim)
    row_delta = jnp.sum(
        (grad_attended.astype(jnp.float32) * attended.astype(jnp.float32)).reshape(
            node_count, head_count, head_dim
        ),
        axis=2,
    )
    delta_heads = row_delta.reshape(block_count, block_rows, head_count)
    edge_gprob = jnp.einsum(
        "nhd,mnhd->nhm", grad_flat, far_values, preferred_element_type=jnp.float32
    )
    edge_gscore = (edge_prob * (edge_gprob - row_delta[..., None]) * score_scale).astype(
        jnp.bfloat16
    )
    edge_query_grad = jnp.einsum(
        "nhm,mnhd->nhd", edge_gscore, far_keys, preferred_element_type=jnp.float32
    )
    edge_kterms = jnp.einsum(
        "nhm,nhd->mnhd", edge_gscore, query_flat, preferred_element_type=jnp.float32
    )
    edge_vterms = jnp.einsum(
        "nhm,nhd->mnhd", edge_weight, grad_flat, preferred_element_type=jnp.float32
    )
    entries = block_count + send_block.shape[0]
    empty_table = jnp.zeros((entries, block_rows, feature_width), jnp.float32)
    empty_query = jnp.zeros((block_count, block_rows, head_count, head_dim), jnp.float32)

    def backward_slot(slot_index, running):
        query_accum, key_table, value_table = running
        picked_keys = pick_blocks(table_keys, tile_block, slot_index, query_heads)
        picked_values = pick_blocks(table_values, tile_block, slot_index, query_heads)
        scores = tile_scores(query_heads, picked_keys, tile_count, slot_index, score_scale)
        probability = jnp.exp(scores - row_top[..., None]) / row_total[..., None]
        weight = probability.astype(jnp.bfloat16)
        grad_prob = jnp.einsum(
            "bqhd,bkhd->bqhk", grad_heads, picked_values, preferred_element_type=jnp.float32
        )
        grad_score = (probability * (grad_prob - delta_heads[..., None]) * score_scale).astype(
            jnp.bfloat16
        )
        query_accum = query_accum + jnp.einsum(
            "bqhk,bkhd->bqhd", grad_score, picked_keys, preferred_element_type=jnp.float32
        )
        key_slot = jnp.einsum(
            "bqhk,bqhd->bkhd", grad_score, query_heads, preferred_element_type=jnp.float32
        )
        value_slot = jnp.einsum(
            "bqhk,bqhd->bkhd", weight, grad_heads, preferred_element_type=jnp.float32
        )
        targets = tile_block[:, slot_index]
        key_table = key_table.at[targets].add(
            key_slot.reshape(block_count, block_rows, feature_width)
        )
        value_table = value_table.at[targets].add(
            value_slot.reshape(block_count, block_rows, feature_width)
        )
        return (query_accum, key_table, value_table)

    query_accum, table_kgrad, table_vgrad = lax.fori_loop(
        0, slot_count, backward_slot, (empty_query, empty_table, empty_table)
    )
    return_key = table_kgrad[block_count:].astype(jnp.bfloat16)
    return_value = table_vgrad[block_count:].astype(jnp.bfloat16)
    home_key, home_value = (
        lax.all_to_all(return_key, "dom", split_axis=0, concat_axis=0, tiled=True),
        lax.all_to_all(return_value, "dom", split_axis=0, concat_axis=0, tiled=True),
    )
    key_grad = table_kgrad[:block_count].at[send_block].add(home_key.astype(jnp.float32))
    value_grad = table_vgrad[:block_count].at[send_block].add(home_value.astype(jnp.float32))
    key_grad = key_grad.reshape(node_count, feature_width)
    value_grad = value_grad.reshape(node_count, feature_width)
    for turn in range(3):
        placed_key = (
            jnp.zeros((node_count, feature_width), jnp.bfloat16)
            .at[matching[turn]]
            .set(edge_kterms[turn].reshape(node_count, feature_width).astype(jnp.bfloat16))
        )
        placed_value = (
            jnp.zeros((node_count, feature_width), jnp.bfloat16)
            .at[matching[turn]]
            .set(edge_vterms[turn].reshape(node_count, feature_width).astype(jnp.bfloat16))
        )
        owned_key, owned_value = from_partner(
            (placed_key, placed_value), ("group", "dom"), top_bit - 1 - turn
        )
        key_grad = key_grad + owned_key.astype(jnp.float32)
        value_grad = value_grad + owned_value.astype(jnp.float32)
    query_grad = query_accum.reshape(node_count, feature_width) + edge_query_grad.reshape(
        node_count, feature_width
    )
    return (update, query_grad, key_grad, value_grad, weight_grad)


def solution(mesh):
    in_specs = (
        P(("group", "dom"), None),
        P(("group", "dom"), None),
        P(("group", "dom"), None),
        P(),
        P(("group", "dom"), None),
        P(),
        P(("group", "dom"), None, None),
        P(("group", "dom"), None),
        P(("group", "dom"), None),
        P(("group", "dom"), None, None),
    )
    out_specs = (
        P(("group", "dom"), None),
        P(("group", "dom"), None),
        P(("group", "dom"), None),
        P(("group", "dom"), None),
        P(),
    )
    return jax.shard_map(shards, mesh=mesh, in_specs=in_specs, out_specs=out_specs, check_vma=False)
```

profile of v0, /device:TPU:0, one launch (start us, length us, event | category | flops | bytes accessed | tf_op | source)
XLA Modules:
  0.0 479.3 jit_solution(12892361956765676531)
XLA Ops:
  18.2 4.2 all-to-all-start
  23.1 5.6 %collective-permute-done.1 = bf16[768,256]{1,0:T(8,128)(2,1)S(1)} collective-permute-done((bf16[768,256]{1,0:T(8,128)(2,1)}, bf16[768,256]{1,0:T(8,128)(2,1)S(1)}, u32[]{:S(2)}, u32[]{:S(2)}) %collective-permute-start.1) | collective-permute-done | bytes 393248 | tf_op jit(solution)/shard_map/ppermute | solution.py:8
  40.1 3.3 gather_fusion.6
  58.9 3.3 gather_fusion.11
  65.8 4.2 all-to-all-start.1
  71.3 22.1 %while.46 = (s32[]{:T(128)}, f32[6,128,8]{1,2,0:T(8,128)S(1)}, f32[6,128,8]{1,2,0:T(8,128)S(1)}, s32[6]{0:T(128)S(1)}, s32[6,8]{0,1:T(8,128)S(1)}, /*index=5*/bf...) while((s32[]{:T(128)}, f32[6,128,8]{1,2,0:T(8,128)S(1)}, ...), condition=%wide.region_5.6_spmd, body=%wide.region_2.5_spmd.sunk | while | flops 55850008 | bytes 8974575 | solution.py:101
  98.1 51.3 %while.47 = (s32[]{:T(128)}, f32[6,128,8,32]{1,3,2,0:T(8,128)}, s32[6,8]{0,1:T(8,128)S(1)}, bf16[14,128,256]{2,1,0:T(8,128)(2,1)}, s32[6]{0:T(128)S(1)}, /*index...) while((s32[]{:T(128)}, f32[6,128,8,32]{1,3,2,0:T(8,128)}, ...), condition=%wide.region_7.8_spmd, body=%wide.region_6.7_spmd.sunk | while | flops 104793112 | bytes 5951761 | solution.py:121
  100.9 3.6 fusion.105
  107.3 3.6 fusion.105
  113.7 3.6 fusion.105
  120.1 3.6 fusion.105
  126.5 3.6 fusion.105
  133.0 3.6 fusion.105
  139.4 3.6 fusion.105
  145.8 3.6 fusion.105
  157.9 163.7 %while.48 = (s32[]{:T(128)}, f32[6,128,8,32]{1,3,2,0:T(8,128)}, f32[14,128,256]{2,1,0:T(8,128)}, f32[14,128,256]{2,1,0:T(8,128)}, s32[6,8]{0,1:T(8,128)S(1)}, /*...) while((s32[]{:T(128)}, f32[6,128,8,32]{1,3,2,0:T(8,128)}, ...), condition=%wide.region_12.0_spmd.clone, body=%wide.region_9.12_spmd.clone.sunk | while | flops 259523616 | bytes 45169084 | solution.py:188
  175.0 3.1 scatter_fusion.1
  215.9 3.1 scatter_fusion.1
  233.3 3.1 scatter_fusion
  236.4 3.1 scatter_fusion.1
  274.2 3.1 scatter_fusion
  277.3 3.1 scatter_fusion.1
  332.3 6.5 %scatter_custom_fusion.3 = bf16[768,256]{1,0:T(8,128)(2,1)} fusion(s32[768]{0:T(1024)S(1)} %get-tuple-element.645, bf16[768,256]{1,0:T(8,128)(2,1)} %copy.93, bf16[]{:T(256)} %constant.147.clone.1), kind=kCustom, calls=%fused_computation.100 | custom fusion | bytes 393728 | tf_op jit(solution)/shard_map/scatter | solution.py:205
  338.8 6.1 %scatter_custom_fusion.5 = bf16[768,256]{1,0:T(8,128)(2,1)} fusion(s32[768]{0:T(1024)S(1)} %get-tuple-element.646, bf16[768,256]{1,0:T(8,128)(2,1)S(1)} %copy.95, bf16[]{:T(256)} %constant.147.clone.1), kind=kCustom, calls=%fused_computation.96 | custom fusion | bytes 393218 | tf_op jit(solution)/shard_map/scatter | solution.py:205
  344.9 4.1 all-to-all-start.3
  353.4 6.5 %scatter_custom_fusion.7 = bf16[768,256]{1,0:T(8,128)(2,1)} fusion(s32[768]{0:T(1024)S(1)} %get-tuple-element.645, bf16[768,256]{1,0:T(8,128)(2,1)} %copy.96, bf16[]{:T(256)} %constant.147.clone.1), kind=kCustom, calls=%fused_computation.94 | custom fusion | bytes 393728 | tf_op jit(solution)/shard_map/scatter | solution.py:210
  361.8 6.8 %scatter_custom_fusion.9 = bf16[768,256]{1,0:T(8,128)(2,1)} fusion(s32[768]{0:T(1024)S(1)} %get-tuple-element.646, bf16[768,256]{1,0:T(8,128)(2,1)} %copy.98, bf16[]{:T(256)} %constant.147.clone.1), kind=kCustom, calls=%fused_computation.90 | custom fusion | bytes 393728 | tf_op jit(solution)/shard_map/scatter | solution.py:210
  370.5 6.5 %scatter_custom_fusion.8 = bf16[768,256]{1,0:T(8,128)(2,1)} fusion(s32[768]{0:T(1024)S(1)} %get-tuple-element.647, bf16[768,256]{1,0:T(8,128)(2,1)} %copy.97, bf16[]{:T(256)} %constant.147.clone.1), kind=kCustom, calls=%fused_computation.92 | custom fusion | bytes 393728 | tf_op jit(solution)/shard_map/scatter | solution.py:210
  378.9 6.5 %scatter_custom_fusion.4 = bf16[768,256]{1,0:T(8,128)(2,1)} fusion(s32[768]{0:T(1024)S(1)} %get-tuple-element.647, bf16[768,256]{1,0:T(8,128)(2,1)} %copy.94, bf16[]{:T(256)} %constant.147.clone.1), kind=kCustom, calls=%fused_computation.98 | custom fusion | bytes 393728 | tf_op jit(solution)/shard_map/scatter | solution.py:205
  393.2 4.1 all-to-all-start.2
  398.4 15.8 %collective-permute-done.10 = bf16[768,256]{1,0:T(8,128)(2,1)} collective-permute-done((bf16[768,256]{1,0:T(8,128)(2,1)}, bf16[768,256]{1,0:T(8,128)(2,1)}, u32[]{:S(2)}, u32[]{:S(2)}) %collective-permute-start.10) | collective-permute-done | bytes 393248 | tf_op jit(solution)/shard_map/ppermute | solution.py:8
  415.8 41.9 %all-reduce.2.cloned.1.call-done = f32[256,256]{1,0:T(8,128)} async-done(((f32[256,256]{1,0:T(8,128)}), f32[256,256]{1,0:T(8,128)}) %all-reduce.2.cloned.1.call-update) | async-done | bytes 262160 | tf_op jit(solution)/shard_map/psum | solution.py:128
  (633 shorter events, 288.3 us)
Async XLA Ops:
  7.2 143.7 %copy-start = (bf16[768,256]{1,0:T(8,128)(2,1)S(1)}, bf16[768,256]{1,0:T(8,128)(2,1)}, u32[]{:S(2)}) copy-start(bf16[768,256]{1,0:T(8,128)(2,1)} %param.20) | copy-start | bytes 1179652
  7.2 21.5 %collective-permute-start.1 = (bf16[768,256]{1,0:T(8,128)(2,1)}, bf16[768,256]{1,0:T(8,128)(2,1)S(1)}, u32[]{:S(2)}, u32[]{:S(2)}) collective-permute-start(bf16[768,256]{1,0:T(8,128)(2,1)} %param.17), channel_id=1, source_target_pairs={{0,8},{1,9},{2,10},{3,11},{4,12},{5,13},{6,14},{7,15},{8,0},{9,1},... | collective-permute-start | bytes 1179656 | tf_op jit(solution)/shard_map/ppermute | solution.py:8
  10.3 35.0 %collective-permute-start = (bf16[768,256]{1,0:T(8,128)(2,1)}, bf16[768,256]{1,0:T(8,128)(2,1)S(1)}, u32[]{:S(2)}, u32[]{:S(2)}) collective-permute-start(bf16[768,256]{1,0:T(8,128)(2,1)} %param.17), channel_id=1, source_target_pairs={{0,16},{1,17},{2,18},{3,19},{4,20},{5,21},{6,22},{7,23},{8,24},{9,... | collective-permute-start | bytes 1179656 | tf_op jit(solution)/shard_map/ppermute | solution.py:8
  12.9 36.0 %collective-permute-start.2 = (bf16[768,256]{1,0:T(8,128)(2,1)}, bf16[768,256]{1,0:T(8,128)(2,1)S(1)}, u32[]{:S(2)}, u32[]{:S(2)}) collective-permute-start(bf16[768,256]{1,0:T(8,128)(2,1)} %param.17), channel_id=1, source_target_pairs={{0,4},{1,5},{2,6},{3,7},{4,0},{5,1},{6,2},{7,3},{8,12},{9,13},{10,... | collective-permute-start | bytes 1179656 | tf_op jit(solution)/shard_map/ppermute | solution.py:8
  14.4 38.1 %collective-permute-start.4 = (bf16[768,256]{1,0:T(8,128)(2,1)}, bf16[768,256]{1,0:T(8,128)(2,1)S(1)}, u32[]{:S(2)}, u32[]{:S(2)}) collective-permute-start(bf16[768,256]{1,0:T(8,128)(2,1)} %param.18), channel_id=1, source_target_pairs={{0,8},{1,9},{2,10},{3,11},{4,12},{5,13},{6,14},{7,15},{8,0},{9,1},... | collective-permute-start | bytes 1179656 | tf_op jit(solution)/shard_map/ppermute | solution.py:8
  14.8 40.5 %collective-permute-start.3 = (bf16[768,256]{1,0:T(8,128)(2,1)}, bf16[768,256]{1,0:T(8,128)(2,1)S(1)}, u32[]{:S(2)}, u32[]{:S(2)}) collective-permute-start(bf16[768,256]{1,0:T(8,128)(2,1)} %param.18), channel_id=1, source_target_pairs={{0,16},{1,17},{2,18},{3,19},{4,20},{5,21},{6,22},{7,23},{8,24},{9,... | collective-permute-start | bytes 1179656 | tf_op jit(solution)/shard_map/ppermute | solution.py:8
  15.8 7.3 %copy-start.33 = (s32[8]{0:T(128)}, s32[8]{0:T(128)S(1)}, u32[]{:S(2)}) copy-start(s32[8]{0:T(128)S(1)} %fusion.49) | copy-start | bytes 100
  18.2 47.6 %all-to-all-start = ((bf16[8,128,256]{2,1,0:T(8,128)(2,1)}), bf16[8,128,256]{2,1,0:T(8,128)(2,1)}, u32[]{:S(2)}, u32[]{:S(2)}) async-start(bf16[8,128,256]{2,1,0:T(8,128)(2,1)} %gather_fusion.8), calls=%async_computation | async-start | bytes 1048576 | tf_op jit(solution)/shard_map/all_to_all | solution.py:64
  28.7 30.2 %collective-permute-start.5 = (bf16[768,256]{1,0:T(8,128)(2,1)}, bf16[768,256]{1,0:T(8,128)(2,1)S(1)}, u32[]{:S(2)}, u32[]{:S(2)}) collective-permute-start(bf16[768,256]{1,0:T(8,128)(2,1)} %param.18), channel_id=1, source_target_pairs={{0,4},{1,5},{2,6},{3,7},{4,0},{5,1},{6,2},{7,3},{8,12},{9,13},{10,... | collective-permute-start | bytes 1179656 | tf_op jit(solution)/shard_map/ppermute | solution.py:8
  55.3 38.2 %copy-start.14 = (bf16[768,256]{0,1:T(8,128)(2,1)}, bf16[768,256]{0,1:T(8,128)(2,1)S(1)}, u32[]{:S(2)}) copy-start(bf16[768,256]{0,1:T(8,128)(2,1)S(1)} %copy.83) | copy-start | bytes 1179652
  58.9 6.7 %copy-start.31 = (f32[8]{0:T(128)S(1)}, f32[8]{0:T(128)}, u32[]{:S(2)}) copy-start(f32[8]{0:T(128)} %param.21) | copy-start | bytes 100
  62.2 7.9 %copy-start.22 = (bf16[768,256]{1,0:T(8,128)(2,1)S(1)}, bf16[768,256]{1,0:T(8,128)(2,1)}, u32[]{:S(2)}) copy-start(bf16[768,256]{1,0:T(8,128)(2,1)} %param.17) | copy-start | bytes 1179652
  64.2 7.1 %copy-start.39 = (s32[1,6]{1,0:T(1,128)S(1)}, s32[1,6]{1,0:T(1,128)}, u32[]{:S(2)}) copy-start(s32[1,6]{1,0:T(1,128)} %param.23) | copy-start | bytes 76
  65.6 27.8 %copy-start.23 = (f32[768,8,3]{0,1,2:T(8,128)}, f32[768,8,3]{0,1,2:T(8,128)S(1)}, u32[]{:S(2)}) copy-start(f32[768,8,3]{0,1,2:T(8,128)S(1)} %multiply_reduce_fusion.3) | copy-start | bytes 221188
  65.8 30.1 %all-to-all-start.1 = ((bf16[8,128,256]{2,1,0:T(8,128)(2,1)}), bf16[8,128,256]{2,1,0:T(8,128)(2,1)}, u32[]{:S(2)}, u32[]{:S(2)}) async-start(bf16[8,128,256]{2,1,0:T(8,128)(2,1)} %gather_fusion.12), calls=%async_computation.1 | async-start | bytes 1048576 | tf_op jit(solution)/shard_map/all_to_all | solution.py:65
  69.9 387.8 %all-reduce.2.cloned.1.call-start = ((), (), s32[]{:S(2)}) async-start(), calls=%async_computation.4 | async-start | bytes 524288 | tf_op jit(solution)/shard_map/psum | solution.py:128
  71.3 22.2 %copy-start.16 = (bf16[768,256]{0,1:T(8,128)(2,1)S(1)}, bf16[768,256]{0,1:T(8,128)(2,1)}, u32[]{:S(2)}) copy-start(bf16[768,256]{0,1:T(8,128)(2,1)} %copy.82) | copy-start | bytes 1179652
  171.9 6.3 %copy-start.4 = (bf16[6,128,8,32]{1,3,2,0:T(8,128)(2,1)S(1)}, bf16[6,128,8,32]{1,3,2,0:T(8,128)(2,1)}, u32[]{:S(2)}) copy-start(bf16[6,128,8,32]{1,3,2,0:T(8,128)(2,1)} %copy-done.3) | copy-start | bytes 1179652 | tf_op jit(solution)/shard_map/while
  171.9 6.2 %copy-start.12 = (f32[6,128,8]{1,2,0:T(8,128)S(1)}, f32[6,128,8]{1,2,0:T(8,128)}, u32[]{:S(2)}) copy-start(f32[6,128,8]{1,2,0:T(8,128)} %copy-done.11) | copy-start | bytes 73732 | tf_op jit(solution)/shard_map/while
  233.2 6.2 %copy-start.4 = (bf16[6,128,8,32]{1,3,2,0:T(8,128)(2,1)S(1)}, bf16[6,128,8,32]{1,3,2,0:T(8,128)(2,1)}, u32[]{:S(2)}) copy-start(bf16[6,128,8,32]{1,3,2,0:T(8,128)(2,1)} %copy-done.3) | copy-start | bytes 1179652 | tf_op jit(solution)/shard_map/while
  274.2 6.3 %copy-start.4 = (bf16[6,128,8,32]{1,3,2,0:T(8,128)(2,1)S(1)}, bf16[6,128,8,32]{1,3,2,0:T(8,128)(2,1)}, u32[]{:S(2)}) copy-start(bf16[6,128,8,32]{1,3,2,0:T(8,128)(2,1)} %copy-done.3) | copy-start | bytes 1179652 | tf_op jit(solution)/shard_map/while
  274.2 6.3 %copy-start.12 = (f32[6,128,8]{1,2,0:T(8,128)S(1)}, f32[6,128,8]{1,2,0:T(8,128)}, u32[]{:S(2)}) copy-start(f32[6,128,8]{1,2,0:T(8,128)} %copy-done.11) | copy-start | bytes 73732 | tf_op jit(solution)/shard_map/while
  344.9 48.3 %all-to-all-start.3 = ((bf16[8,128,256]{2,1,0:T(8,128)(2,1)}), bf16[8,128,256]{2,1,0:T(8,128)(2,1)}, u32[]{:S(2)}, u32[]{:S(2)}) async-start(bf16[8,128,256]{2,1,0:T(8,128)(2,1)} %slice.111), calls=%async_computation.3 | async-start | bytes 1048576 | tf_op jit(solution)/shard_map/all_to_all | solution.py:195
  351.4 40.0 %copy-start.7 = (f32[6,128,8,32]{1,3,2,0:T(8,128)S(1)}, f32[6,128,8,32]{1,3,2,0:T(8,128)}, u32[]{:S(2)}) copy-start(f32[6,128,8,32]{1,3,2,0:T(8,128)} %get-tuple-element.503) | copy-start | bytes 2359300
  385.4 84.5 %collective-permute-start.7 = (bf16[768,256]{1,0:T(8,128)(2,1)}, bf16[768,256]{1,0:T(8,128)(2,1)}, u32[]{:S(2)}, u32[]{:S(2)}) collective-permute-start(bf16[768,256]{1,0:T(8,128)(2,1)} %scatter_custom_fusion.4), channel_id=1, source_target_pairs={{0,8},{1,9},{2,10},{3,11},{4,12},{5,13},{6,14},{7,15},{8,0},{9,1},... | collective-permute-start | bytes 1179656 | tf_op jit(solution)/shard_map/ppermute | solution.py:8
  385.4 28.8 %collective-permute-start.10 = (bf16[768,256]{1,0:T(8,128)(2,1)}, bf16[768,256]{1,0:T(8,128)(2,1)}, u32[]{:S(2)}, u32[]{:S(2)}) collective-permute-start(bf16[768,256]{1,0:T(8,128)(2,1)} %scatter_custom_fusion.8), channel_id=1, source_target_pairs={{0,8},{1,9},{2,10},{3,11},{4,12},{5,13},{6,14},{7,15},{8,0},{9,1},... | collective-permute-start | bytes 1179656 | tf_op jit(solution)/shard_map/ppermute | solution.py:8
  387.4 80.1 %collective-permute-start.11 = (bf16[768,256]{1,0:T(8,128)(2,1)}, bf16[768,256]{1,0:T(8,128)(2,1)}, u32[]{:S(2)}, u32[]{:S(2)}) collective-permute-start(bf16[768,256]{1,0:T(8,128)(2,1)} %scatter_custom_fusion.9), channel_id=1, source_target_pairs={{0,4},{1,5},{2,6},{3,7},{4,0},{5,1},{6,2},{7,3},{8,12},{9,13},{10,... | collective-permute-start | bytes 1179656 | tf_op jit(solution)/shard_map/ppermute | solution.py:8
  389.3 78.2 %collective-permute-start.9 = (bf16[768,256]{1,0:T(8,128)(2,1)}, bf16[768,256]{1,0:T(8,128)(2,1)}, u32[]{:S(2)}, u32[]{:S(2)}) collective-permute-start(bf16[768,256]{1,0:T(8,128)(2,1)} %scatter_custom_fusion.7), channel_id=1, source_target_pairs={{0,16},{1,17},{2,18},{3,19},{4,20},{5,21},{6,22},{7,23},{8,24},{9,... | collective-permute-start | bytes 1179656 | tf_op jit(solution)/shard_map/ppermute | solution.py:8
  391.2 78.6 %collective-permute-start.8 = (bf16[768,256]{1,0:T(8,128)(2,1)}, bf16[768,256]{1,0:T(8,128)(2,1)}, u32[]{:S(2)}, u32[]{:S(2)}) collective-permute-start(bf16[768,256]{1,0:T(8,128)(2,1)} %scatter_custom_fusion.5), channel_id=1, source_target_pairs={{0,4},{1,5},{2,6},{3,7},{4,0},{5,1},{6,2},{7,3},{8,12},{9,13},{10,... | collective-permute-start | bytes 1179656 | tf_op jit(solution)/shard_map/ppermute | solution.py:8
  393.2 68.3 %copy-start.34 = (s32[8]{0:T(128)S(1)}, s32[8]{0:T(128)}, u32[]{:S(2)}) copy-start(s32[8]{0:T(128)} %copy-done.33) | copy-start | bytes 100
  393.2 70.8 %all-to-all-start.2 = ((bf16[8,128,256]{2,1,0:T(8,128)(2,1)}), bf16[8,128,256]{2,1,0:T(8,128)(2,1)S(1)}, u32[]{:S(2)}, u32[]{:S(2)}) async-start(bf16[8,128,256]{2,1,0:T(8,128)(2,1)} %slice.112), calls=%async_computation.2 | async-start | bytes 1048576 | tf_op jit(solution)/shard_map/all_to_all | solution.py:194
  414.2 55.6 %collective-permute-start.6 = (bf16[768,256]{1,0:T(8,128)(2,1)}, bf16[768,256]{1,0:T(8,128)(2,1)S(1)}, u32[]{:S(2)}, u32[]{:S(2)}) collective-permute-start(bf16[768,256]{1,0:T(8,128)(2,1)} %scatter_custom_fusion.3), channel_id=1, source_target_pairs={{0,16},{1,17},{2,18},{3,19},{4,20},{5,21},{6,22},{7,23},{8,24},{9,... | collective-permute-start | bytes 1179656 | tf_op jit(solution)/shard_map/ppermute | solution.py:8
  (125 other events, 541.4 us)
Sparse Core Ops, SparseCore 0:
  326.2 131.4 all-reduce.1
where the time goes:
time: 489 us; the launch traced here: 479 us
  local copies, waits for them, and re-layouts  161 us (33%)
  matrix products  115 us (24%)
  other arithmetic  87.7 us (18%)
  waiting for transfers between devices  63.4 us (13%)
  starting transfers between devices  34.3 us (7%)
  between operations  15 us (3%)
    gather x80, local copies, waits for them, and re-layouts, pick_blocks(): return table[tile_block[:, slot_index]].reshape(template.shape)  59.6 us
    psum x1, waiting for transfers between devices, shards(): lax.psum(weight_term, ('group', 'dom')) * (node_count * devices) ** (-0.5)  41.9 us
    dot_general x8, matrix products, second_pass(): jnp.einsum('bqhk,bkhd->bqhd', weight, picked_values, preferred_element_ty...  28.7 us
    scatter-add x8, other arithmetic, backward_slot(): value_table.at[targets]  24.6 us
    scatter-add x8, other arithmetic, backward_slot(): key_table.at[targets]  24.6 us
    ppermute x12, waiting for transfers between devices, from_partner(): lax.ppermute(array, axis, [(i, i ^ 1 << apart) for i in range(lax.axis_si...  21.4 us
    dot_general x8, matrix products, backward_slot(): jnp.einsum('bqhk,bkhd->bqhd', grad_score, picked_keys, preferred_element_...  21.1 us
    scatter x3, local copies, waits for them, and re-layouts, shards(): placed_value = jnp.zeros((node_count, feature_width), jnp.bfloat16).at[ma...  19.8 us
  transfers between devices with their start and end apart: 17, of which 3 were waited for; matrix products, arithmetic and copies ran while one was open for 28% of the time, Pallas kernels for 0%

commit v1 on v0

v1 whole, which is shorter than its diff:
```python
import functools
import math

import jax
import jax.numpy as jnp
from jax import lax
from jax.experimental import pallas as pl
from jax.experimental.pallas import tpu as pltpu
from jax.sharding import PartitionSpec as P

LOG2E = math.log2(math.e)
VMEM = pl.BlockSpec(memory_space=pltpu.VMEM)
SMEM = pl.BlockSpec(memory_space=pltpu.SMEM)
F32 = jnp.float32
BF16 = jnp.bfloat16


def params(mib=48):
    return pltpu.CompilerParams(vmem_limit_bytes=mib * 1024 * 1024)


def cost(flops, moved):
    return pl.CostEstimate(flops=int(flops), bytes_accessed=int(moved), transcendentals=0)


def dot(left, right, left_dim=1, right_dim=0):
    return lax.dot_general(
        left, right, (((left_dim,), (right_dim,)), ((), ())), preferred_element_type=F32
    )


def spread(rows, width):
    heads, lanes = rows.shape
    return jnp.concatenate(
        [jnp.broadcast_to(rows[h : h + 1], (width, lanes)) for h in range(heads)], axis=0
    )


def head_sums(product, heads):
    features, lanes = product.shape
    return product.reshape(heads, features // heads, lanes).sum(axis=1)


def pick_kernel(send_ref, k_ref, v_ref, out_ref, *, block):
    def body(s, carry):
        rows = pl.ds(pl.multiple_of(send_ref[s] * block, block), block)
        out_ref[s, pl.ds(0, block), :] = k_ref[rows, :]
        out_ref[s, pl.ds(block, block), :] = v_ref[rows, :]
        return carry

    lax.fori_loop(0, out_ref.shape[0], body, 0)


def fwd_kernel(
    tb_ref, tc_ref, q_ref, k_ref, v_ref, got_ref,
    ot_ref, m_ref, l_ref,
    ktab, vttab, qx, acc, m_s, l_s,
    *, heads, block,
):
    nodes, feat = q_ref.shape
    blocks = nodes // block
    halo = got_ref.shape[0]
    width = feat // heads
    scale2 = width**-0.5 * LOG2E
    groups = heads // 2

    def fill_own(b, carry):
        rows = pl.ds(pl.multiple_of(b * block, block), block)
        ktab[b] = k_ref[rows, :]
        vttab[b] = v_ref[rows, :].T
        return carry

    def fill_halo(s, carry):
        ktab[blocks + s] = got_ref[s, pl.ds(0, block), :]
        vttab[blocks + s] = got_ref[s, pl.ds(block, block), :].T
        return carry

    lax.fori_loop(0, blocks, fill_own, 0)
    lax.fori_loop(0, halo, fill_halo, 0)
    qx[...] = jnp.zeros(qx.shape, qx.dtype)

    def do_block(b, carry):
        rows = pl.ds(pl.multiple_of(b * block, block), block)
        qt = q_ref[rows, :].T
        for h in range(heads):
            qx[h * width : (h + 1) * width, h * block : (h + 1) * block] = qt[
                h * width : (h + 1) * width
            ]
        m_s[...] = jnp.full(m_s.shape, -1e30, F32)
        l_s[...] = jnp.zeros(l_s.shape, F32)
        acc[...] = jnp.zeros(acc.shape, F32)

        def do_tile(t, inner):
            index = tb_ref[b, t]
            k = ktab[index]
            for g in range(groups):
                cols = slice(g * 2 * block, (g + 1) * 2 * block)
                s = dot(k, qx[:, cols])
                old = m_s[:, cols]
                top = jnp.maximum(old, s.max(axis=0, keepdims=True))
                p = jnp.exp2((s - top) * scale2)
                alpha = jnp.exp2((old - top) * scale2)
                m_s[:, cols] = top
                l_s[:, cols] = l_s[:, cols] * alpha + p.sum(axis=0, keepdims=True)
                feats = slice(g * 2 * width, (g + 1) * 2 * width)
                o = dot(vttab[index, feats, :], p.astype(BF16))
                acc[feats, :] = acc[feats, :] * jnp.concatenate(
                    [
                        jnp.broadcast_to(alpha[:, :block], (width, block)),
                        jnp.broadcast_to(alpha[:, block:], (width, block)),
                    ],
                    axis=0,
                ) + jnp.concatenate([o[:width, :block], o[width:, block:]], axis=0)
            return inner

        lax.fori_loop(0, tc_ref[b], do_tile, 0)
        ot_ref[:, rows] = acc[...]
        for h in range(heads):
            m_ref[h : h + 1, rows] = m_s[:, h * block : (h + 1) * block] * (width**-0.5)
            l_ref[h : h + 1, rows] = l_s[:, h * block : (h + 1) * block]
        return carry

    lax.fori_loop(0, blocks, do_block, 0)


def prep_kernel(q_ref, gu_ref, w_ref, qt_ref, gat_ref, ga_ref):
    qt_ref[...] = q_ref[...].T
    ga = dot(gu_ref[...], w_ref[...], 1, 1).astype(BF16)
    ga_ref[...] = ga
    gat_ref[...] = ga.T


def hot(match_row, nodes):
    return (lax.broadcasted_iota(jnp.int32, (nodes, nodes), 0) == match_row).astype(BF16)


def gather_kernel(match_ref, mk_ref, mv_ref, qt_ref, gat_ref, fk_ref, fv_ref, s_ref, dp_ref, *, heads):
    nodes = mk_ref.shape[0]
    onehot = hot(match_ref[...], nodes)
    fk = dot(mk_ref[...].T, onehot)
    fk_ref[...] = fk.astype(BF16)
    s_ref[...] = head_sums(fk * qt_ref[...].astype(F32), heads)
    fv = dot(mv_ref[...].T, onehot)
    fv_ref[...] = fv.astype(BF16)
    dp_ref[...] = head_sums(fv * gat_ref[...].astype(F32), heads)


def merge_kernel(*refs, heads):
    (bias_ref, ot_ref, m_ref, l_ref, gat_ref, gu_ref, w_ref) = refs[:7]
    far = refs[7:19]
    update_ref, term_ref, lse_ref, delta_ref, eq_ref = refs[19:24]
    out = refs[24:]
    feat = ot_ref.shape[0]
    width = feat // heads
    scale = width**-0.5
    scores = [far[4 * e + 2][...] * scale + bias_ref[...] for e in range(3)]
    old = m_ref[...]
    top = functools.reduce(jnp.maximum, scores, old)
    tile_factor = jnp.exp(old - top)
    edge = [jnp.exp(s - top) for s in scores]
    total = l_ref[...] * tile_factor + edge[0] + edge[1] + edge[2]
    probs = [e / total for e in edge]
    weights = [p.astype(BF16).astype(F32) for p in probs]
    mixed = ot_ref[...] * spread(tile_factor / total, width)
    for e in range(3):
        mixed = mixed + spread(weights[e], width) * far[4 * e + 1][...].astype(F32)
    att = mixed.astype(BF16)
    update_ref[...] = dot(att, w_ref[...], 0, 0).astype(BF16)
    term_ref[...] = dot(att, gu_ref[...])
    delta = head_sums(att.astype(F32) * gat_ref[...].astype(F32), heads)
    delta_ref[...] = delta
    lse_ref[...] = top * LOG2E + jnp.log2(total)
    query = None
    for e in range(3):
        ds = (probs[e] * (far[4 * e + 3][...] - delta) * scale).astype(BF16).astype(F32)
        out[2 * e][...] = ds
        out[2 * e + 1][...] = weights[e]
        part = spread(ds, width) * far[4 * e][...].astype(F32)
        query = part if query is None else query + part
    eq_ref[...] = query


def scatter_kernel(match_ref, qt_ref, gat_ref, ds_ref, wt_ref, pk_ref, pv_ref, *, heads):
    feat, nodes = qt_ref.shape
    width = feat // heads
    onehot = hot(match_ref[...], nodes)
    kt = (spread(ds_ref[...], width) * qt_ref[...].astype(F32)).astype(BF16)
    pk_ref[...] = dot(onehot, kt, 1, 1).astype(BF16)
    vt = (spread(wt_ref[...], width) * gat_ref[...].astype(F32)).astype(BF16)
    pv_ref[...] = dot(onehot, vt, 1, 1).astype(BF16)


def bwd_kernel(
    tb_ref, tc_ref, q_ref, k_ref, v_ref, got_ref, qt_ref, gat_ref, ga_ref,
    lse_ref, delta_ref, eq_ref,
    dq_ref, dk_ref, dv_ref, ret_ref,
    ktab, vtab, kttab, qxt, gxt, qx, gx, dkt, dvt, acc, lse_s, delta_s,
    *, heads, block,
):
    nodes, feat = q_ref.shape
    blocks = nodes // block
    halo = got_ref.shape[0]
    width = feat // heads
    scale = width**-0.5
    scale2 = scale * LOG2E
    groups = heads // 2

    def fill_own(b, carry):
        rows = pl.ds(pl.multiple_of(b * block, block), block)
        k = k_ref[rows, :]
        ktab[b] = k
        kttab[b] = k.T
        vtab[b] = v_ref[rows, :]
        return carry

    def fill_halo(s, carry):
        k = got_ref[s, pl.ds(0, block), :]
        ktab[blocks + s] = k
        kttab[blocks + s] = k.T
        vtab[blocks + s] = got_ref[s, pl.ds(block, block), :]
        return carry

    def clear(e, carry):
        dkt[e] = jnp.zeros((block, feat), F32)
        dvt[e] = jnp.zeros((block, feat), F32)
        return carry

    lax.fori_loop(0, blocks, fill_own, 0)
    lax.fori_loop(0, halo, fill_halo, 0)
    lax.fori_loop(0, blocks + halo, clear, 0)
    qxt[...] = jnp.zeros(qxt.shape, qxt.dtype)
    gxt[...] = jnp.zeros(gxt.shape, gxt.dtype)

    def do_block(b, carry):
        rows = pl.ds(pl.multiple_of(b * block, block), block)
        lanes = lax.broadcasted_iota(jnp.int32, (block, feat), 1) // width
        qf = q_ref[rows, :].astype(F32)
        gf = ga_ref[rows, :].astype(F32)
        qt = qt_ref[:, rows]
        gt = gat_ref[:, rows]
        for h in range(heads):
            hs, bs = slice(h * width, (h + 1) * width), slice(h * block, (h + 1) * block)
            qxt[hs, bs] = qt[hs]
            gxt[hs, bs] = gt[hs]
            qx[bs, :] = jnp.where(lanes == h, qf, 0.0).astype(BF16)
            gx[bs, :] = jnp.where(lanes == h, gf, 0.0).astype(BF16)
            lse_s[:, bs] = lse_ref[h : h + 1, rows]
            delta_s[:, bs] = delta_ref[h : h + 1, rows]
        acc[...] = jnp.zeros(acc.shape, F32)

        def do_tile(t, inner):
            index = tb_ref[b, t]
            k = ktab[index]
            v = vtab[index]
            ps, dss = [], []
            for g in range(groups):
                cols = slice(g * 2 * block, (g + 1) * 2 * block)
                s = dot(k, qxt[:, cols])
                p = jnp.exp2(s * scale2 - lse_s[:, cols])
                dp = dot(v, gxt[:, cols])
                ds = (p * (dp - delta_s[:, cols])).astype(BF16)
                ps.append(p.astype(BF16))
                dss.append(ds)
                feats = slice(g * 2 * width, (g + 1) * 2 * width)
                o = dot(kttab[index, feats, :], ds)
                acc[feats, :] += jnp.concatenate([o[:width, :block], o[width:, block:]], axis=0)
            dvt[index] += dot(jnp.concatenate(ps, axis=1), gx[...])
            dkt[index] += dot(jnp.concatenate(dss, axis=1), qx[...])
            return inner

        lax.fori_loop(0, tc_ref[b], do_tile, 0)
        dq_ref[rows, :] = (acc[...] * scale + eq_ref[:, rows]).T
        return carry

    lax.fori_loop(0, blocks, do_block, 0)

    def drain_own(b, carry):
        rows = pl.ds(pl.multiple_of(b * block, block), block)
        dk_ref[rows, :] = dkt[b] * scale
        dv_ref[rows, :] = dvt[b]
        return carry

    def drain_halo(s, carry):
        ret_ref[s, pl.ds(0, block), :] = (dkt[blocks + s] * scale).astype(BF16)
        ret_ref[s, pl.ds(block, block), :] = dvt[blocks + s].astype(BF16)
        return carry

    lax.fori_loop(0, blocks, drain_own, 0)
    lax.fori_loop(0, halo, drain_halo, 0)


def final_kernel(send_ref, dk_ref, dv_ref, home_ref, *refs, block):
    terms, (ok_ref, ov_ref) = refs[:6], refs[6:]
    ok_ref[...] = (
        dk_ref[...] + terms[0][...].astype(F32) + terms[2][...].astype(F32) + terms[4][...].astype(F32)
    )
    ov_ref[...] = (
        dv_ref[...] + terms[1][...].astype(F32) + terms[3][...].astype(F32) + terms[5][...].astype(F32)
    )

    def body(s, carry):
        rows = pl.ds(pl.multiple_of(send_ref[s] * block, block), block)
        ok_ref[rows, :] += home_ref[s, pl.ds(0, block), :].astype(F32)
        ov_ref[rows, :] += home_ref[s, pl.ds(block, block), :].astype(F32)
        return carry

    lax.fori_loop(0, home_ref.shape[0], body, 0)


def call(kernel, name, ins, outs, args, scratch=(), estimate=None, **static):
    return pl.pallas_call(
        functools.partial(kernel, **static),
        name=name,
        in_specs=ins,
        out_specs=[VMEM] * len(outs),
        out_shape=[jax.ShapeDtypeStruct(shape, dtype) for shape, dtype in outs],
        scratch_shapes=list(scratch),
        compiler_params=params(),
        cost_estimate=estimate,
    )(*args)


def from_partner(array, axis, apart):
    return lax.ppermute(array, axis, [(i, i ^ 1 << apart) for i in range(lax.axis_size(axis))])


def shards(
    query_rows, key_rows, value_rows, out_weight, grad_update, expander_bias,
    tile_block, tile_count, send_block, matching,
):
    nodes, feat = query_rows.shape
    heads = expander_bias.shape[0]
    tile_block = tile_block[0]
    tile_count = tile_count[0]
    send_block = send_block[0]
    matching = matching[0]
    blocks, slots = tile_block.shape
    block = nodes // blocks
    halo = send_block.shape[0]
    entries = blocks + halo
    axes = ("group", "dom")
    devices = lax.axis_size(axes)
    top_bit = devices.bit_length() - 1
    wide = heads * block
    tile_flops = 2 * wide * feat * block * blocks * slots

    moved = [
        from_partner((key_rows, value_rows), axes, top_bit - 1 - turn) for turn in range(3)
    ]
    (sent,) = call(
        pick_kernel, "pick", [SMEM, VMEM, VMEM], [((halo, 2 * block, feat), BF16)],
        (send_block, key_rows, value_rows), block=block,
        estimate=cost(0, 4 * halo * block * feat * 2),
    )
    got = lax.all_to_all(sent, "dom", split_axis=0, concat_axis=0, tiled=True)
    qt, gat, ga = call(
        prep_kernel, "prep", [VMEM] * 3,
        [((feat, nodes), BF16), ((feat, nodes), BF16), ((nodes, feat), BF16)],
        (query_rows, grad_update, out_weight),
        estimate=cost(2 * nodes * feat * feat, 10 * nodes * feat),
    )
    ot, top, total = call(
        fwd_kernel, "fwd_tiles", [SMEM, SMEM] + [VMEM] * 4,
        [((feat, nodes), F32), ((heads, nodes), F32), ((heads, nodes), F32)],
        (tile_block, tile_count, query_rows, key_rows, value_rows, got),
        scratch=[
            pltpu.VMEM((entries, block, feat), BF16),
            pltpu.VMEM((entries, feat, block), BF16),
            pltpu.VMEM((feat, wide), BF16),
            pltpu.VMEM((feat, block), F32),
            pltpu.VMEM((1, wide), F32),
            pltpu.VMEM((1, wide), F32),
        ],
        estimate=cost(4 * tile_flops, 8 * nodes * feat * 2),
        heads=heads, block=block,
    )
    rows = [matching[turn : turn + 1] for turn in range(3)]
    far = [None] * 3
    for turn in range(3):
        far[turn] = call(
            gather_kernel, f"gather{turn}", [VMEM] * 5,
            [((feat, nodes), BF16), ((feat, nodes), BF16), ((heads, nodes), F32), ((heads, nodes), F32)],
            (rows[turn], *moved[turn], qt, gat),
            estimate=cost(4 * nodes * nodes * feat, 12 * nodes * feat),
            heads=heads,
        )
    merged = call(
        merge_kernel, "merge", [VMEM] * 19,
        [
            ((nodes, feat), BF16), ((feat, feat), F32), ((heads, nodes), F32),
            ((heads, nodes), F32), ((feat, nodes), F32),
        ] + [((heads, nodes), F32)] * 6,
        (expander_bias.reshape(heads, 1), ot, top, total, gat, grad_update, out_weight,
         *far[0], *far[1], *far[2]),
        estimate=cost(4 * nodes * feat * feat, 24 * nodes * feat),
        heads=heads,
    )
    update, weight_term, lse, delta, edge_query = merged[:5]
    owned = []
    for turn in range(3):
        placed = call(
            scatter_kernel, f"scatter{turn}", [VMEM] * 5,
            [((nodes, feat), BF16), ((nodes, feat), BF16)],
            (rows[turn], qt, gat, merged[5 + 2 * turn], merged[6 + 2 * turn]),
            estimate=cost(4 * nodes * nodes * feat, 10 * nodes * feat),
            heads=heads,
        )
        owned.extend(from_partner(tuple(placed), axes, top_bit - 1 - turn))
    weight_grad = lax.psum(weight_term, axes) * (nodes * devices) ** (-0.5)
    query_grad, own_k, own_v, back = call(
        bwd_kernel, "bwd_tiles", [SMEM, SMEM] + [VMEM] * 10,
        [((nodes, feat), F32), ((nodes, feat), F32), ((nodes, feat), F32), ((halo, 2 * block, feat), BF16)],
        (tile_block, tile_count, query_rows, key_rows, value_rows, got, qt, gat, ga,
         lse, delta, edge_query),
        scratch=[
            pltpu.VMEM((entries, block, feat), BF16),
            pltpu.VMEM((entries, block, feat), BF16),
            pltpu.VMEM((entries, feat, block), BF16),
            pltpu.VMEM((feat, wide), BF16),
            pltpu.VMEM((feat, wide), BF16),
            pltpu.VMEM((wide, feat), BF16),
            pltpu.VMEM((wide, feat), BF16),
            pltpu.VMEM((entries, block, feat), F32),
            pltpu.VMEM((entries, block, feat), F32),
            pltpu.VMEM((feat, block), F32),
            pltpu.VMEM((1, wide), F32),
            pltpu.VMEM((1, wide), F32),
        ],
        estimate=cost(10 * tile_flops, 24 * nodes * feat * 2),
        heads=heads, block=block,
    )
    home = lax.all_to_all(back, "dom", split_axis=0, concat_axis=0, tiled=True)
    key_grad, value_grad = call(
        final_kernel, "final", [SMEM] + [VMEM] * 9,
        [((nodes, feat), F32), ((nodes, feat), F32)],
        (send_block, own_k, own_v, home, *owned),
        estimate=cost(0, 40 * nodes * feat),
        block=block,
    )
    return update, query_grad, key_grad, value_grad, weight_grad


def solution(mesh):
    split = P(("group", "dom"), None)
    split3 = P(("group", "dom"), None, None)
    in_specs = (split, split, split, P(), split, P(), split3, split, split, split3)
    out_specs = (split, split, split, split, P())
    return jax.shard_map(shards, mesh=mesh, in_specs=in_specs, out_specs=out_specs, check_vma=False)
```

time: 489 us -> 329 us (0.67); the launches traced: 479 us -> 331 us
  local copies, waits for them, and re-layouts: 161 us -> 9.12 us
  matrix products: 115 us -> 0 us
  Pallas kernels: 0 us -> 110 us
  waiting for transfers between devices: 63.4 us -> 169 us
  other arithmetic: 87.7 us -> 1.68 us
  starting transfers between devices: 34.3 us -> 26.5 us
    dot_general x59 -> x0, matrix products: 115 us -> none  [the longest x8 28.7 us: second_pass(): jnp.einsum('bqhk,bkhd->bqhd', weight, picked_values, preferred_element_ty...]
    pallas_call x0 -> x12, Pallas kernels: none -> 110 us  [call(): pl.pallas_call(functools.partial(kernel, **static), name=name, in_specs=i...]
    gather x94 -> x0, local copies, waits for them, and re-layouts: 88.4 us -> none  [the longest x80 59.6 us: pick_blocks(): return table[tile_block[:, slot_index]].reshape(template.shape)]
    psum x1, waiting for transfers between devices: 41.9 us -> 124 us  [shards(): weight_grad = lax.psum(weight_term, axes) * (nodes * devices) ** (-0.5)]
    scatter-add x18 -> x0, other arithmetic: 54.1 us -> none  [the longest x8 24.6 us: backward_slot(): value_table.at[targets]]
    scatter x6 -> x0, local copies, waits for them, and re-layouts: 38.8 us -> none  [the longest x3 19.8 us: shards(): placed_value = jnp.zeros((node_count, feature_width), jnp.bfloat16).at[ma...]
    ppermute x12, waiting for transfers between devices: 21.4 us -> 45.3 us  [from_partner(): lax.ppermute(array, axis, [(i, i ^ 1 << apart) for i in range(lax.axis_si...]
    convert_element_type x7 -> x0, local copies, waits for them, and re-layouts: 9.09 us -> none  [the longest x3 5.81 us: shards(): edge_vterms[turn].reshape(node_count, feature_width).astype(jnp.bfloat16)]
  transfers between devices with their start and end apart: 17 -> 15, of which waited for: 3 -> 4; matrix products, arithmetic and copies ran while one was open for 28% -> 1% of each run, Pallas kernels for 0% -> 3%
where the time goes in v1:
time: 329 us; the launch traced here: 331 us
  waiting for transfers between devices  169 us (51%)
  Pallas kernels  110 us (33%)
  starting transfers between devices  26.5 us (8%)
  between operations  14.3 us (4%)
  local copies, waits for them, and re-layouts  9.12 us (3%)
    psum x1, waiting for transfers between devices, shards(): weight_grad = lax.psum(weight_term, axes) * (nodes * devices) ** (-0.5)  124 us
    pallas_call x12, Pallas kernels, call(): pl.pallas_call(functools.partial(kernel, **static), name=name, in_specs=i...  110 us
    ppermute x12, waiting for transfers between devices, from_partner(): lax.ppermute(array, axis, [(i, i ^ 1 << apart) for i in range(lax.axis_si...  45.3 us
    ppermute x12, starting transfers between devices, from_partner(): lax.ppermute(array, axis, [(i, i ^ 1 << apart) for i in range(lax.axis_si...  17.5 us
    unnamed x61, local copies, waits for them, and re-layouts  9.03 us
  transfers between devices with their start and end apart: 15, of which 4 were waited for; matrix products, arithmetic and copies ran while one was open for 1% of the time, Pallas kernels for 3%

profile of v1, /device:TPU:0, one launch (start us, length us, event | category | flops | bytes accessed | tf_op | source)
XLA Modules:
  0.0 330.7 jit_solution(16190512664261454378)
XLA Ops:
  7.8 2.3 pick.1
  10.1 5.3 %all-to-all-start = ((bf16[8,256,256]{2,1,0:T(8,128)(2,1)}), bf16[8,256,256]{2,1,0:T(8,128)(2,1)S(1)}, u32[]{:S(2)}, u32[]{:S(2)}) async-start(bf16[8,256,256]{2,1,0:T(8,128)(2,1)} %pick.1), calls=%async_computation | async-start | bytes 2097152 | tf_op jit(solution)/shard_map/all_to_all | solution.py:355
  15.4 2.7 collective-permute-start
  18.4 1.6 collective-permute-start.2
  20.4 2.0 collective-permute-start.4
  22.4 23.1 %collective-permute-done.mk_ref = bf16[768,256]{1,0:T(8,128)(2,1)S(1)} collective-permute-done((bf16[768,256]{1,0:T(8,128)(2,1)}, bf16[768,256]{1,0:T(8,128)(2,1)S(1)}, u32[]{:S(2)}, u32[]{:S(2)}) %collective-permute-start) | collective-permute-done | bytes 393248 | tf_op jit(solution)/shard_map/ppermute | solution.py:324
  45.5 0.7 copy-done.20
  46.2 2.0 collective-permute-start.5
  48.7 0.8 copy-done.18
  49.5 3.9 %collective-permute-done.1.mv_ref = bf16[768,256]{1,0:T(8,128)(2,1)S(1)} collective-permute-done((bf16[768,256]{1,0:T(8,128)(2,1)}, bf16[768,256]{1,0:T(8,128)(2,1)S(1)}, u32[]{:S(2)}, u32[]{:S(2)}) %collective-permute-start.1) | collective-permute-done | bytes 393248 | tf_op jit(solution)/shard_map/ppermute | solution.py:324
  53.4 0.7 copy-done.22
  54.2 1.0 copy-done.23
  55.2 1.0 gather0.1
  56.2 2.1 gather1.1
  59.1 0.7 copy-done.6
  59.9 2.1 gather2.1
  62.7 0.7 copy-done.10
  64.1 40.1 %fwd_tiles.1 = (f32[256,768]{1,0:T(8,128)S(1)}, f32[8,768]{1,0:T(8,128)S(1)}, f32[8,768]{1,0:T(8,128)S(1)}) custom-call(s32[6,8]{1,0:T(8,128)S(1)} %bitcast.12, s32[6]{0:T(128)S(1)} %bitcast.16, bf16[768,256]{1,0:T(8,128)(2,1)S(1)} %copy-done.3, bf16[768,256]{1,0:T(8,128)(2,1)} %k_ref.5, bf16[768,256]{1,0:T(8,128)(2,1)} %v_ref.5, ...), custom_call_target="tpu_custom_call" | custom-call | flops 12884901888 | bytes 3145728 | tf_op jit(solution)/shard_map/fwd_tiles/pallas_call | solution.py:311
  104.4 2.1 merge.1
  107.1 51.7 %bwd_tiles.1 = (f32[768,256]{1,0:T(8,128)}, f32[768,256]{1,0:T(8,128)S(1)}, f32[768,256]{1,0:T(8,128)S(1)}, bf16[8,256,256]{2,1,0:T(8,128)(2,1)}) custom-call(s32[6,8]{1,0:T(8,128)S(1)} %bitcast.13, s32[6]{0:T(128)S(1)} %bitcast.17, bf16[768,256]{1,0:T(8,128)(2,1)S(1)} %copy-done.3, bf16[768,256]{1,0:T(8,128)(2,1)} %k_ref.5, bf16[768,256]{1,0:T(8,128)(2,1)} %v_ref.5, ...), custom_call_target="tpu_custom_call" | custom-call | flops 32212254720 | bytes 9437184 | tf_op jit(solution)/shard_map/bwd_tiles/pallas_call | solution.py:311
  158.9 3.7 %all-to-all-start.1 = ((bf16[8,256,256]{2,1,0:T(8,128)(2,1)}), bf16[8,256,256]{2,1,0:T(8,128)(2,1)S(1)}, u32[]{:S(2)}, u32[]{:S(2)}) async-start(bf16[8,256,256]{2,1,0:T(8,128)(2,1)} %get-tuple-element.71), calls=%async_computation.1 | async-start | bytes 2097152 | tf_op jit(solution)/shard_map/all_to_all | solution.py:432
  163.4 1.6 scatter0.1
  164.9 2.9 collective-permute-start.7
  167.9 1.7 scatter1.1
  169.6 2.0 collective-permute-start.9
  171.6 1.7 scatter2.1
  173.3 1.9 collective-permute-start.10
  175.2 18.3 %collective-permute-done.6.refs_0_ = bf16[768,256]{1,0:T(8,128)(2,1)S(1)} collective-permute-done((bf16[768,256]{1,0:T(8,128)(2,1)S(1)}, bf16[768,256]{1,0:T(8,128)(2,1)S(1)}, u32[]{:S(2)}, u32[]{:S(2)}) %collective-permute-start.6) | collective-permute-done | bytes 393248 | tf_op jit(solution)/shard_map/ppermute | solution.py:324
  193.5 1.7 collective-permute-start.11
  195.2 123.9 %all-reduce.2.cloned.1.call-done = f32[256,256]{1,0:T(8,128)} async-done(((f32[256,256]{1,0:T(8,128)}), f32[256,256]{1,0:T(8,128)}) %all-reduce.2.cloned.1.call-update) | async-done | bytes 262160 | tf_op jit(solution)/shard_map/psum | solution.py:409
  319.1 1.7 broadcast_multiply_fusion
  320.8 3.1 final.1
  (75 shorter events, 5.6 us)
Async XLA Ops:
  10.1 38.1 %copy-start.29 = (f32[8]{0:T(128)S(1)}, f32[8]{0:T(128)}, u32[]{:S(2)}) copy-start(f32[8]{0:T(128)} %param.15) | copy-start | bytes 100
  10.1 38.2 %copy-start = (bf16[768,256]{1,0:T(8,128)(2,1)S(1)}, bf16[768,256]{1,0:T(8,128)(2,1)}, u32[]{:S(2)}) copy-start(bf16[768,256]{1,0:T(8,128)(2,1)} %refs_5_.1) | copy-start | bytes 1179652
  10.1 38.2 %copy-start.2 = (bf16[256,256]{1,0:T(8,128)(2,1)S(1)}, bf16[256,256]{1,0:T(8,128)(2,1)}, u32[]{:S(2)}) copy-start(bf16[256,256]{1,0:T(8,128)(2,1)} %refs_6_.1) | copy-start | bytes 393220
  10.1 38.2 %copy-start.3 = (bf16[768,256]{1,0:T(8,128)(2,1)S(1)}, bf16[768,256]{1,0:T(8,128)(2,1)}, u32[]{:S(2)}) copy-start(bf16[768,256]{1,0:T(8,128)(2,1)} %q_ref.5) | copy-start | bytes 1179652
  10.1 53.4 %all-to-all-start = ((bf16[8,256,256]{2,1,0:T(8,128)(2,1)}), bf16[8,256,256]{2,1,0:T(8,128)(2,1)S(1)}, u32[]{:S(2)}, u32[]{:S(2)}) async-start(bf16[8,256,256]{2,1,0:T(8,128)(2,1)} %pick.1), calls=%async_computation | async-start | bytes 2097152 | tf_op jit(solution)/shard_map/all_to_all | solution.py:355
  15.4 32.9 %copy-start.28 = (s32[1,6,8]{2,0,1:T(1,128)S(1)}, s32[1,6,8]{2,0,1:T(1,128)}, u32[]{:S(2)}) copy-start(s32[1,6,8]{2,0,1:T(1,128)} %param.16) | copy-start | bytes 580
  15.4 30.1 %collective-permute-start = (bf16[768,256]{1,0:T(8,128)(2,1)}, bf16[768,256]{1,0:T(8,128)(2,1)S(1)}, u32[]{:S(2)}, u32[]{:S(2)}) collective-permute-start(bf16[768,256]{1,0:T(8,128)(2,1)} %k_ref.5), channel_id=1, source_target_pairs={{0,16},{1,17},{2,18},{3,19},{4,20},{5,21},{6,22},{7,23},{8,24},{9,... | collective-permute-start | bytes 1179656 | tf_op jit(solution)/shard_map/ppermute | solution.py:324
  18.1 35.4 %collective-permute-start.1 = (bf16[768,256]{1,0:T(8,128)(2,1)}, bf16[768,256]{1,0:T(8,128)(2,1)S(1)}, u32[]{:S(2)}, u32[]{:S(2)}) collective-permute-start(bf16[768,256]{1,0:T(8,128)(2,1)} %v_ref.5), channel_id=1, source_target_pairs={{0,16},{1,17},{2,18},{3,19},{4,20},{5,21},{6,22},{7,23},{8,24},{9,... | collective-permute-start | bytes 1179656 | tf_op jit(solution)/shard_map/ppermute | solution.py:324
  18.4 37.8 %collective-permute-start.2 = (bf16[768,256]{1,0:T(8,128)(2,1)}, bf16[768,256]{1,0:T(8,128)(2,1)}, u32[]{:S(2)}, u32[]{:S(2)}) collective-permute-start(bf16[768,256]{1,0:T(8,128)(2,1)} %k_ref.5), channel_id=1, source_target_pairs={{0,8},{1,9},{2,10},{3,11},{4,12},{5,13},{6,14},{7,15},{8,0},{9,1},... | collective-permute-start | bytes 1179656 | tf_op jit(solution)/shard_map/ppermute | solution.py:324
  20.0 36.2 %collective-permute-start.3 = (bf16[768,256]{1,0:T(8,128)(2,1)}, bf16[768,256]{1,0:T(8,128)(2,1)}, u32[]{:S(2)}, u32[]{:S(2)}) collective-permute-start(bf16[768,256]{1,0:T(8,128)(2,1)} %v_ref.5), channel_id=1, source_target_pairs={{0,8},{1,9},{2,10},{3,11},{4,12},{5,13},{6,14},{7,15},{8,0},{9,1},... | collective-permute-start | bytes 1179656 | tf_op jit(solution)/shard_map/ppermute | solution.py:324
  20.4 39.4 %collective-permute-start.4 = (bf16[768,256]{1,0:T(8,128)(2,1)}, bf16[768,256]{1,0:T(8,128)(2,1)}, u32[]{:S(2)}, u32[]{:S(2)}) collective-permute-start(bf16[768,256]{1,0:T(8,128)(2,1)} %k_ref.5), channel_id=1, source_target_pairs={{0,4},{1,5},{2,6},{3,7},{4,0},{5,1},{6,2},{7,3},{8,12},{9,13},{10,... | collective-permute-start | bytes 1179656 | tf_op jit(solution)/shard_map/ppermute | solution.py:324
  46.2 13.6 %collective-permute-start.5 = (bf16[768,256]{1,0:T(8,128)(2,1)}, bf16[768,256]{1,0:T(8,128)(2,1)}, u32[]{:S(2)}, u32[]{:S(2)}) collective-permute-start(bf16[768,256]{1,0:T(8,128)(2,1)} %v_ref.5), channel_id=1, source_target_pairs={{0,4},{1,5},{2,6},{3,7},{4,0},{5,1},{6,2},{7,3},{8,12},{9,13},{10,... | collective-permute-start | bytes 1179656 | tf_op jit(solution)/shard_map/ppermute | solution.py:324
  48.3 5.9 %copy-start.21 = (bf16[768,256]{1,0:T(8,128)(2,1)S(1)}, bf16[768,256]{1,0:T(8,128)(2,1)}, u32[]{:S(2)}) copy-start(bf16[768,256]{1,0:T(8,128)(2,1)} %copy-done.20) | copy-start | bytes 1179652
  49.5 10.4 %copy-start.14 = (bf16[256,768]{1,0:T(8,128)(2,1)}, bf16[256,768]{1,0:T(8,128)(2,1)S(1)}, u32[]{:S(2)}) copy-start(bf16[256,768]{1,0:T(8,128)(2,1)S(1)} %get-tuple-element.50.qt_ref) | copy-start | bytes 1179652
  63.5 40.8 %copy-start.1 = (bf16[8,256,256]{2,1,0:T(8,128)(2,1)}, bf16[8,256,256]{2,1,0:T(8,128)(2,1)S(1)}, u32[]{:S(2)}) copy-start(bf16[8,256,256]{2,1,0:T(8,128)(2,1)S(1)} %all-to-all-done.got_ref) | copy-start | bytes 3145732
  64.1 40.2 %copy-start.5 = (bf16[256,768]{1,0:T(8,128)(2,1)S(1)}, bf16[256,768]{1,0:T(8,128)(2,1)}, u32[]{:S(2)}) copy-start(bf16[256,768]{1,0:T(8,128)(2,1)} %copy-done.4) | copy-start | bytes 1179652
  64.1 40.2 %copy-start.7 = (bf16[256,768]{1,0:T(8,128)(2,1)S(1)}, bf16[256,768]{1,0:T(8,128)(2,1)}, u32[]{:S(2)}) copy-start(bf16[256,768]{1,0:T(8,128)(2,1)} %copy-done.6) | copy-start | bytes 1179652
  64.1 40.2 %copy-start.9 = (bf16[256,768]{1,0:T(8,128)(2,1)S(1)}, bf16[256,768]{1,0:T(8,128)(2,1)}, u32[]{:S(2)}) copy-start(bf16[256,768]{1,0:T(8,128)(2,1)} %copy-done.8) | copy-start | bytes 1179652
  64.1 40.2 %copy-start.11 = (bf16[256,768]{1,0:T(8,128)(2,1)S(1)}, bf16[256,768]{1,0:T(8,128)(2,1)}, u32[]{:S(2)}) copy-start(bf16[256,768]{1,0:T(8,128)(2,1)} %copy-done.10) | copy-start | bytes 1179652
  104.3 2.8 copy-start.15
  104.4 2.8 copy-start.19
  107.1 51.7 %copy-start.24 = (f32[8,768]{1,0:T(8,128)}, f32[8,768]{1,0:T(8,128)S(1)}, u32[]{:S(2)}) copy-start(f32[8,768]{1,0:T(8,128)S(1)} %get-tuple-element.73.wt_ref) | copy-start | bytes 73732
  158.9 3.7 %copy-start.16 = (bf16[256,768]{1,0:T(8,128)(2,1)S(1)}, bf16[256,768]{1,0:T(8,128)(2,1)}, u32[]{:S(2)}) copy-start(bf16[256,768]{1,0:T(8,128)(2,1)} %copy-done.14) | copy-start | bytes 1179652
  158.9 162.0 %all-to-all-start.1 = ((bf16[8,256,256]{2,1,0:T(8,128)(2,1)}), bf16[8,256,256]{2,1,0:T(8,128)(2,1)S(1)}, u32[]{:S(2)}, u32[]{:S(2)}) async-start(bf16[8,256,256]{2,1,0:T(8,128)(2,1)} %get-tuple-element.71), calls=%async_computation.1 | async-start | bytes 2097152 | tf_op jit(solution)/shard_map/all_to_all | solution.py:432
  162.6 156.5 %all-reduce.2.cloned.1.call-start = ((), (), s32[]{:S(2)}) async-start(), calls=%async_computation.2 | async-start | bytes 524288 | tf_op jit(solution)/shard_map/psum | solution.py:409
  163.4 4.5 %copy-start.17 = (bf16[256,768]{1,0:T(8,128)(2,1)S(1)}, bf16[256,768]{1,0:T(8,128)(2,1)}, u32[]{:S(2)}) copy-start(bf16[256,768]{1,0:T(8,128)(2,1)} %copy-done.14) | copy-start | bytes 1179652
  164.9 28.6 %collective-permute-start.6 = (bf16[768,256]{1,0:T(8,128)(2,1)S(1)}, bf16[768,256]{1,0:T(8,128)(2,1)S(1)}, u32[]{:S(2)}, u32[]{:S(2)}) collective-permute-start(bf16[768,256]{1,0:T(8,128)(2,1)S(1)} %get-tuple-element.74), channel_id=1, source_target_pairs={{0,16},{1,17},{2,18},{3,19},{4,20},{5,21},{6,22},{7,23},{8,24},{9,... | collective-permute-start | bytes 1179656 | tf_op jit(solution)/shard_map/ppermute | solution.py:324
  164.9 155.9 %collective-permute-start.7 = (bf16[768,256]{1,0:T(8,128)(2,1)}, bf16[768,256]{1,0:T(8,128)(2,1)}, u32[]{:S(2)}, u32[]{:S(2)}) collective-permute-start(bf16[768,256]{1,0:T(8,128)(2,1)} %get-tuple-element.75), channel_id=1, source_target_pairs={{0,16},{1,17},{2,18},{3,19},{4,20},{5,21},{6,22},{7,23},{8,24},{9,... | collective-permute-start | bytes 1179656 | tf_op jit(solution)/shard_map/ppermute | solution.py:324
  169.6 151.2 %collective-permute-start.8 = (bf16[768,256]{1,0:T(8,128)(2,1)}, bf16[768,256]{1,0:T(8,128)(2,1)}, u32[]{:S(2)}, u32[]{:S(2)}) collective-permute-start(bf16[768,256]{1,0:T(8,128)(2,1)} %get-tuple-element.78), channel_id=1, source_target_pairs={{0,8},{1,9},{2,10},{3,11},{4,12},{5,13},{6,14},{7,15},{8,0},{9,1},... | collective-permute-start | bytes 1179656 | tf_op jit(solution)/shard_map/ppermute | solution.py:324
  169.6 151.2 %collective-permute-start.9 = (bf16[768,256]{1,0:T(8,128)(2,1)}, bf16[768,256]{1,0:T(8,128)(2,1)}, u32[]{:S(2)}, u32[]{:S(2)}) collective-permute-start(bf16[768,256]{1,0:T(8,128)(2,1)} %get-tuple-element.79), channel_id=1, source_target_pairs={{0,8},{1,9},{2,10},{3,11},{4,12},{5,13},{6,14},{7,15},{8,0},{9,1},... | collective-permute-start | bytes 1179656 | tf_op jit(solution)/shard_map/ppermute | solution.py:324
  173.3 147.5 %collective-permute-start.10 = (bf16[768,256]{1,0:T(8,128)(2,1)}, bf16[768,256]{1,0:T(8,128)(2,1)S(1)}, u32[]{:S(2)}, u32[]{:S(2)}) collective-permute-start(bf16[768,256]{1,0:T(8,128)(2,1)} %get-tuple-element.82), channel_id=1, source_target_pairs={{0,4},{1,5},{2,6},{3,7},{4,0},{5,1},{6,2},{7,3},{8,12},{9,13},{10,... | collective-permute-start | bytes 1179656 | tf_op jit(solution)/shard_map/ppermute | solution.py:324
  193.5 127.3 %collective-permute-start.11 = (bf16[768,256]{1,0:T(8,128)(2,1)}, bf16[768,256]{1,0:T(8,128)(2,1)}, u32[]{:S(2)}, u32[]{:S(2)}) collective-permute-start(bf16[768,256]{1,0:T(8,128)(2,1)} %get-tuple-element.83), channel_id=1, source_target_pairs={{0,4},{1,5},{2,6},{3,7},{4,0},{5,1},{6,2},{7,3},{8,12},{9,13},{10,... | collective-permute-start | bytes 1179656 | tf_op jit(solution)/shard_map/ppermute | solution.py:324
  (13 other events, 10.2 us)
Sparse Core Ops, SparseCore 0:
  195.3 123.7 all-reduce.1

commit v2 on v1

--- a/solution.py
+++ b/solution.py
@@ -9,7 +9,9 @@
 from jax.sharding import PartitionSpec as P
 
 LOG2E = math.log2(math.e)
+LEAST = 5
 VMEM = pl.BlockSpec(memory_space=pltpu.VMEM)
+ANY = pl.BlockSpec(memory_space=pl.ANY)
 SMEM = pl.BlockSpec(memory_space=pltpu.SMEM)
 F32 = jnp.float32
 BF16 = jnp.bfloat16
@@ -54,7 +56,7 @@
 def fwd_kernel(
     tb_ref, tc_ref, q_ref, k_ref, v_ref, got_ref,
     ot_ref, m_ref, l_ref,
-    ktab, vttab, qx, acc, m_s, l_s,
+    ktab, vttab, kcat, vtcat, qx, m_s, l_s,
     *, heads, block,
 ):
     nodes, feat = q_ref.shape
@@ -63,6 +65,7 @@
     width = feat // heads
     scale2 = width**-0.5 * LOG2E
     groups = heads // 2
+    slots = tb_ref.shape[1]
 
     def fill_own(b, carry):
         rows = pl.ds(pl.multiple_of(b * block, block), block)
@@ -86,35 +89,28 @@
             qx[h * width : (h + 1) * width, h * block : (h + 1) * block] = qt[
                 h * width : (h + 1) * width
             ]
-        m_s[...] = jnp.full(m_s.shape, -1e30, F32)
-        l_s[...] = jnp.zeros(l_s.shape, F32)
-        acc[...] = jnp.zeros(acc.shape, F32)
-
-        def do_tile(t, inner):
+        count = tc_ref[b]
+        for t in range(slots):
             index = tb_ref[b, t]
-            k = ktab[index]
-            for g in range(groups):
-                cols = slice(g * 2 * block, (g + 1) * 2 * block)
-                s = dot(k, qx[:, cols])
-                old = m_s[:, cols]
-                top = jnp.maximum(old, s.max(axis=0, keepdims=True))
-                p = jnp.exp2((s - top) * scale2)
-                alpha = jnp.exp2((old - top) * scale2)
-                m_s[:, cols] = top
-                l_s[:, cols] = l_s[:, cols] * alpha + p.sum(axis=0, keepdims=True)
-                feats = slice(g * 2 * width, (g + 1) * 2 * width)
-                o = dot(vttab[index, feats, :], p.astype(BF16))
-                acc[feats, :] = acc[feats, :] * jnp.concatenate(
-                    [
-                        jnp.broadcast_to(alpha[:, :block], (width, block)),
-                        jnp.broadcast_to(alpha[:, block:], (width, block)),
-                    ],
-                    axis=0,
-                ) + jnp.concatenate([o[:width, :block], o[width:, block:]], axis=0)
-            return inner
-
-        lax.fori_loop(0, tc_ref[b], do_tile, 0)
-        ot_ref[:, rows] = acc[...]
+            kcat[t * block : (t + 1) * block, :] = ktab[index]
+            vtcat[:, t * block : (t + 1) * block] = vttab[index]
+        for g in range(groups):
+            cols = slice(g * 2 * block, (g + 1) * 2 * block)
+            feats = slice(g * 2 * width, (g + 1) * 2 * width)
+            s = dot(kcat[...], qx[:, cols])
+            live = [
+                s[t * block : (t + 1) * block]
+                if t < LEAST
+                else jnp.where(t < count, s[t * block : (t + 1) * block], -1e30)
+                for t in range(slots)
+            ]
+            s = jnp.concatenate(live, axis=0)
+            top = s.max(axis=0, keepdims=True)
+            p = jnp.exp2((s - top) * scale2)
+            m_s[:, cols] = top
+            l_s[:, cols] = p.sum(axis=0, keepdims=True)
+            o = dot(vtcat[feats, :], p.astype(BF16))
+            ot_ref[feats, rows] = jnp.concatenate([o[:width, :block], o[width:, block:]], axis=0)
         for h in range(heads):
             m_ref[h : h + 1, rows] = m_s[:, h * block : (h + 1) * block] * (width**-0.5)
             l_ref[h : h + 1, rows] = l_s[:, h * block : (h + 1) * block]
@@ -134,13 +130,13 @@
     return (lax.broadcasted_iota(jnp.int32, (nodes, nodes), 0) == match_row).astype(BF16)
 
 
-def gather_kernel(match_ref, mk_ref, mv_ref, qt_ref, gat_ref, fk_ref, fv_ref, s_ref, dp_ref, *, heads):
-    nodes = mk_ref.shape[0]
+def gather_kernel(match_ref, moved_ref, qt_ref, gat_ref, after_ref, fk_ref, fv_ref, s_ref, dp_ref, *, heads):
+    nodes = qt_ref.shape[1]
     onehot = hot(match_ref[...], nodes)
-    fk = dot(mk_ref[...].T, onehot)
+    fk = dot(moved_ref[:nodes, :].T, onehot)
     fk_ref[...] = fk.astype(BF16)
     s_ref[...] = head_sums(fk * qt_ref[...].astype(F32), heads)
-    fv = dot(mv_ref[...].T, onehot)
+    fv = dot(moved_ref[nodes:, :].T, onehot)
     fv_ref[...] = fv.astype(BF16)
     dp_ref[...] = head_sums(fv * gat_ref[...].astype(F32), heads)
 
@@ -180,19 +176,19 @@
     eq_ref[...] = query
 
 
-def scatter_kernel(match_ref, qt_ref, gat_ref, ds_ref, wt_ref, pk_ref, pv_ref, *, heads):
+def scatter_kernel(match_ref, qt_ref, gat_ref, ds_ref, wt_ref, placed_ref, *, heads):
     feat, nodes = qt_ref.shape
     width = feat // heads
     onehot = hot(match_ref[...], nodes)
     kt = (spread(ds_ref[...], width) * qt_ref[...].astype(F32)).astype(BF16)
-    pk_ref[...] = dot(onehot, kt, 1, 1).astype(BF16)
+    placed_ref[:nodes, :] = dot(onehot, kt, 1, 1).astype(BF16)
     vt = (spread(wt_ref[...], width) * gat_ref[...].astype(F32)).astype(BF16)
-    pv_ref[...] = dot(onehot, vt, 1, 1).astype(BF16)
+    placed_ref[nodes:, :] = dot(onehot, vt, 1, 1).astype(BF16)
 
 
 def bwd_kernel(
     tb_ref, tc_ref, q_ref, k_ref, v_ref, got_ref, qt_ref, gat_ref, ga_ref,
-    lse_ref, delta_ref, eq_ref,
+    lse_ref, delta_ref, eq_ref, after0_ref, after1_ref, after2_ref,
     dq_ref, dk_ref, dv_ref, ret_ref,
     ktab, vtab, kttab, qxt, gxt, qx, gx, dkt, dvt, acc, lse_s, delta_s,
     *, heads, block,
@@ -248,27 +244,36 @@
             delta_s[:, bs] = delta_ref[h : h + 1, rows]
         acc[...] = jnp.zeros(acc.shape, F32)
 
-        def do_tile(t, inner):
-            index = tb_ref[b, t]
-            k = ktab[index]
-            v = vtab[index]
+        count = tc_ref[b]
+
+        def do_pair(pair, inner):
+            first, second = tb_ref[b, 2 * pair], tb_ref[b, 2 * pair + 1]
+            live = 2 * pair + 1 < count
+            k = jnp.concatenate([ktab[first], ktab[second]], axis=0)
+            v = jnp.concatenate([vtab[first], vtab[second]], axis=0)
             ps, dss = [], []
             for g in range(groups):
                 cols = slice(g * 2 * block, (g + 1) * 2 * block)
+                feats = slice(g * 2 * width, (g + 1) * 2 * width)
                 s = dot(k, qxt[:, cols])
                 p = jnp.exp2(s * scale2 - lse_s[:, cols])
+                p = jnp.concatenate([p[:block], jnp.where(live, p[block:], 0.0)], axis=0)
                 dp = dot(v, gxt[:, cols])
                 ds = (p * (dp - delta_s[:, cols])).astype(BF16)
                 ps.append(p.astype(BF16))
                 dss.append(ds)
-                feats = slice(g * 2 * width, (g + 1) * 2 * width)
-                o = dot(kttab[index, feats, :], ds)
+                kt = jnp.concatenate([kttab[first, feats, :], kttab[second, feats, :]], axis=1)
+                o = dot(kt, ds)
                 acc[feats, :] += jnp.concatenate([o[:width, :block], o[width:, block:]], axis=0)
-            dvt[index] += dot(jnp.concatenate(ps, axis=1), gx[...])
-            dkt[index] += dot(jnp.concatenate(dss, axis=1), qx[...])
+            dv = dot(jnp.concatenate(ps, axis=1), gx[...])
+            dk = dot(jnp.concatenate(dss, axis=1), qx[...])
+            dvt[first] += dv[:block]
+            dvt[second] += dv[block:]
+            dkt[first] += dk[:block]
+            dkt[second] += dk[block:]
             return inner
 
-        lax.fori_loop(0, tc_ref[b], do_tile, 0)
+        lax.fori_loop(0, (count + 1) // 2, do_pair, 0)
         dq_ref[rows, :] = (acc[...] * scale + eq_ref[:, rows]).T
         return carry
 
@@ -290,13 +295,10 @@
 
 
 def final_kernel(send_ref, dk_ref, dv_ref, home_ref, *refs, block):
-    terms, (ok_ref, ov_ref) = refs[:6], refs[6:]
-    ok_ref[...] = (
-        dk_ref[...] + terms[0][...].astype(F32) + terms[2][...].astype(F32) + terms[4][...].astype(F32)
-    )
-    ov_ref[...] = (
-        dv_ref[...] + terms[1][...].astype(F32) + terms[3][...].astype(F32) + terms[5][...].astype(F32)
-    )
+    terms, (ok_ref, ov_ref) = refs[:3], refs[3:]
+    nodes = dk_ref.shape[0]
+    ok_ref[...] = dk_ref[...] + sum(term[:nodes, :].astype(F32) for term in terms)
+    ov_ref[...] = dv_ref[...] + sum(term[nodes:, :].astype(F32) for term in terms)
 
     def body(s, carry):
         rows = pl.ds(pl.multiple_of(send_ref[s] * block, block), block)
@@ -322,6 +324,15 @@
 
 def from_partner(array, axis, apart):
     return lax.ppermute(array, axis, [(i, i ^ 1 << apart) for i in range(lax.axis_size(axis))])
+
+
+def reduce_everywhere(term, axes):
+    devices = lax.axis_size(axes)
+    rows, columns = term.shape
+    parts = term.reshape(devices, rows // devices, columns)
+    mine = lax.all_to_all(parts, axes, split_axis=0, concat_axis=0, tiled=True).sum(axis=0)
+    copies = jnp.broadcast_to(mine[None], parts.shape)
+    return lax.all_to_all(copies, axes, split_axis=0, concat_axis=0, tiled=True).reshape(rows, columns)
 
 
 def shards(
@@ -344,9 +355,8 @@
     wide = heads * block
     tile_flops = 2 * wide * feat * block * blocks * slots
 
-    moved = [
-        from_partner((key_rows, value_rows), axes, top_bit - 1 - turn) for turn in range(3)
-    ]
+    both = jnp.concatenate([key_rows, value_rows], axis=0)
+    moved = [from_partner(both, axes, top_bit - 1 - turn) for turn in range(3)]
     (sent,) = call(
         pick_kernel, "pick", [SMEM, VMEM, VMEM], [((halo, 2 * block, feat), BF16)],
         (send_block, key_rows, value_rows), block=block,
@@ -366,21 +376,22 @@
         scratch=[
             pltpu.VMEM((entries, block, feat), BF16),
             pltpu.VMEM((entries, feat, block), BF16),
+            pltpu.VMEM((slots * block, feat), BF16),
+            pltpu.VMEM((feat, slots * block), BF16),
             pltpu.VMEM((feat, wide), BF16),
-            pltpu.VMEM((feat, block), F32),
             pltpu.VMEM((1, wide), F32),
             pltpu.VMEM((1, wide), F32),
         ],
-        estimate=cost(4 * tile_flops, 8 * nodes * feat * 2),
+        estimate=cost(8 * tile_flops, 8 * nodes * feat * 2),
         heads=heads, block=block,
     )
     rows = [matching[turn : turn + 1] for turn in range(3)]
     far = [None] * 3
     for turn in range(3):
         far[turn] = call(
-            gather_kernel, f"gather{turn}", [VMEM] * 5,
+            gather_kernel, f"gather{turn}", [VMEM] * 4 + [ANY],
             [((feat, nodes), BF16), ((feat, nodes), BF16), ((heads, nodes), F32), ((heads, nodes), F32)],
-            (rows[turn], *moved[turn], qt, gat),
+            (rows[turn], moved[turn], qt, gat, top),
             estimate=cost(4 * nodes * nodes * feat, 12 * nodes * feat),
             heads=heads,
         )
@@ -396,22 +407,23 @@
         heads=heads,
     )
     update, weight_term, lse, delta, edge_query = merged[:5]
-    owned = []
+    owned, ready = [], []
     for turn in range(3):
-        placed = call(
+        (placed,) = call(
             scatter_kernel, f"scatter{turn}", [VMEM] * 5,
-            [((nodes, feat), BF16), ((nodes, feat), BF16)],
+            [((2 * nodes, feat), BF16)],
             (rows[turn], qt, gat, merged[5 + 2 * turn], merged[6 + 2 * turn]),
             estimate=cost(4 * nodes * nodes * feat, 10 * nodes * feat),
             heads=heads,
         )
-        owned.extend(from_partner(tuple(placed), axes, top_bit - 1 - turn))
-    weight_grad = lax.psum(weight_term, axes) * (nodes * devices) ** (-0.5)
+        ready.append(placed)
+        owned.append(from_partner(placed, axes, top_bit - 1 - turn))
+    weight_grad = reduce_everywhere(weight_term, axes) * (nodes * devices) ** (-0.5)
     query_grad, own_k, own_v, back = call(
-        bwd_kernel, "bwd_tiles", [SMEM, SMEM] + [VMEM] * 10,
+        bwd_kernel, "bwd_tiles", [SMEM, SMEM] + [VMEM] * 10 + [ANY] * 3,
         [((nodes, feat), F32), ((nodes, feat), F32), ((nodes, feat), F32), ((halo, 2 * block, feat), BF16)],
         (tile_block, tile_count, query_rows, key_rows, value_rows, got, qt, gat, ga,
-         lse, delta, edge_query),
+         lse, delta, edge_query, *ready),
         scratch=[
             pltpu.VMEM((entries, block, feat), BF16),
             pltpu.VMEM((entries, block, feat), BF16),
@@ -426,12 +438,12 @@
             pltpu.VMEM((1, wide), F32),
             pltpu.VMEM((1, wide), F32),
         ],
-        estimate=cost(10 * tile_flops, 24 * nodes * feat * 2),
+        estimate=cost(12 * tile_flops, 24 * nodes * feat * 2),
         heads=heads, block=block,
     )
     home = lax.all_to_all(back, "dom", split_axis=0, concat_axis=0, tiled=True)
     key_grad, value_grad = call(
-        final_kernel, "final", [SMEM] + [VMEM] * 9,
+        final_kernel, "final", [SMEM] + [VMEM] * 6,
         [((nodes, feat), F32), ((nodes, feat), F32)],
         (send_block, own_k, own_v, home, *owned),
         estimate=cost(0, 40 * nodes * feat),

time: 329 us -> 155 us (0.47)
  waiting for transfers between devices: 169 us -> 44.7 us
  Pallas kernels: 110 us -> 66.4 us
  between operations: 14.3 us -> 0.9 us
  starting transfers between devices: 26.5 us -> 30.7 us
    psum x1 -> x0, waiting for transfers between devices: 124 us -> none  [shards(): weight_grad = lax.psum(weight_term, axes) * (nodes * devices) ** (-0.5)]
    pallas_call x12, Pallas kernels: 110 us -> 66.4 us  [call(): pl.pallas_call(functools.partial(kernel, **static), name=name, in_specs=i...]
    ppermute x12 -> x6, waiting for transfers between devices: 45.3 us -> 27 us  [from_partner(): lax.ppermute(array, axis, [(i, i ^ 1 << apart) for i in range(lax.axis_si...]
    all_to_all x1, waiting for transfers between devices: 0.01 us -> 12.2 us  [shards(): home = lax.all_to_all(back, 'dom', split_axis=0, concat_axis=0, tiled=True)]
    ppermute x12 -> x6, starting transfers between devices: 17.5 us -> 8.49 us  [from_partner(): lax.ppermute(array, axis, [(i, i ^ 1 << apart) for i in range(lax.axis_si...]
    all_to_all x0 -> x2, starting transfers between devices: none -> 7.15 us  [the longest x1 3.84 us: reduce_everywhere(): lax.all_to_all(parts, axes, split_axis=0, concat_axis=0, tiled=True)]
    all_to_all x1, starting transfers between devices: 3.69 us -> 9.71 us  [shards(): home = lax.all_to_all(back, 'dom', split_axis=0, concat_axis=0, tiled=True)]
    all_to_all x1, waiting for transfers between devices: 0.01 us -> 5.39 us  [shards(): got = lax.all_to_all(sent, 'dom', split_axis=0, concat_axis=0, tiled=True)]
  transfers between devices with their start and end apart: 15 -> 10, of which waited for: 4 -> 7; matrix products, arithmetic and copies ran while one was open for 1% -> 2% of each run, Pallas kernels for 3% -> 39%
where the time goes in v2:
time: 155 us; the launch traced here: 156 us
  Pallas kernels  66.4 us (43%)
  waiting for transfers between devices  44.7 us (29%)
  starting transfers between devices  30.7 us (20%)
  local copies, waits for them, and re-layouts  10.5 us (7%)
  other arithmetic  2.66 us (2%)
    pallas_call x12, Pallas kernels, call(): pl.pallas_call(functools.partial(kernel, **static), name=name, in_specs=i...  66.4 us
    ppermute x6, waiting for transfers between devices, from_partner(): lax.ppermute(array, axis, [(i, i ^ 1 << apart) for i in range(lax.axis_si...  27 us
    all_to_all x1, waiting for transfers between devices, shards(): home = lax.all_to_all(back, 'dom', split_axis=0, concat_axis=0, tiled=True)  12.2 us
    all_to_all x1, starting transfers between devices, shards(): home = lax.all_to_all(back, 'dom', split_axis=0, concat_axis=0, tiled=True)  9.71 us
    unnamed x56, local copies, waits for them, and re-layouts  8.92 us
    ppermute x6, starting transfers between devices, from_partner(): lax.ppermute(array, axis, [(i, i ^ 1 << apart) for i in range(lax.axis_si...  8.49 us
    all_to_all x1, waiting for transfers between devices, shards(): got = lax.all_to_all(sent, 'dom', split_axis=0, concat_axis=0, tiled=True)  5.39 us
    all_to_all x1, starting transfers between devices, shards(): got = lax.all_to_all(sent, 'dom', split_axis=0, concat_axis=0, tiled=True)  5.3 us
  transfers between devices with their start and end apart: 10, of which 7 were waited for; matrix products, arithmetic and copies ran while one was open for 2% of the time, Pallas kernels for 39%

profile of v2, /device:TPU:0, one launch (start us, length us, event | category | flops | bytes accessed | tf_op | source)
XLA Modules:
  0.0 155.8 jit_solution(13356034202654397273)
XLA Ops:
  1.3 1.0 copy-done.1
  2.3 1.0 copy-done.3
  3.3 1.7 %pick.1 = bf16[8,256,256]{2,1,0:T(8,128)(2,1)} custom-call(s32[8]{0:T(128)S(1)} %bitcast.17, bf16[768,256]{1,0:T(8,128)(2,1)S(1)} %copy-done.1, bf16[768,256]{1,0:T(8,128)(2,1)S(1)} %copy-done.3), custom_call_target="tpu_custom_call" | custom-call | bytes 2097152 | tf_op jit(solution)/shard_map/pick/pallas_call | solution.py:313
  4.9 5.3 %all-to-all-start = ((bf16[8,256,256]{2,1,0:T(8,128)(2,1)}), bf16[8,256,256]{2,1,0:T(8,128)(2,1)S(1)}, u32[]{:S(2)}, u32[]{:S(2)}) async-start(bf16[8,256,256]{2,1,0:T(8,128)(2,1)} %pick.1), calls=%async_computation | async-start | bytes 2097152 | tf_op jit(solution)/shard_map/all_to_all | solution.py:365
  10.3 0.8 constant_dynamic-update-slice_fusion.1
  12.2 2.0 %collective-permute-start.2 = (bf16[1536,256]{1,0:T(8,128)(2,1)}, bf16[1536,256]{1,0:T(8,128)(2,1)}, u32[]{:S(2)}, u32[]{:S(2)}) collective-permute-start(bf16[1536,256]{1,0:T(8,128)(2,1)} %constant_dynamic-update-slice_fusion), channel_id=1, source_target_pairs={{0,4},{1,5},{2,6},{3,7},{4,0},{5,1},{6,2},{7,3},{8,12},{9,13},{10,... | collective-permute-start | bytes 2359304 | tf_op jit(solution)/shard_map/ppermute | solution.py:326
  14.2 1.6 %collective-permute-start.1 = (bf16[1536,256]{1,0:T(8,128)(2,1)}, bf16[1536,256]{1,0:T(8,128)(2,1)}, u32[]{:S(2)}, u32[]{:S(2)}) collective-permute-start(bf16[1536,256]{1,0:T(8,128)(2,1)} %constant_dynamic-update-slice_fusion), channel_id=1, source_target_pairs={{0,8},{1,9},{2,10},{3,11},{4,12},{5,13},{6,14},{7,15},{8,0},{9,1},... | collective-permute-start | bytes 2359304 | tf_op jit(solution)/shard_map/ppermute | solution.py:326
  15.8 2.6 %collective-permute-start = (bf16[1536,256]{1,0:T(8,128)(2,1)}, bf16[1536,256]{1,0:T(8,128)(2,1)}, u32[]{:S(2)}, u32[]{:S(2)}) collective-permute-start(bf16[1536,256]{1,0:T(8,128)(2,1)} %constant_dynamic-update-slice_fusion), channel_id=1, source_target_pairs={{0,16},{1,17},{2,18},{3,19},{4,20},{5,21},{6,22},{7,23},{8,24},{9,... | collective-permute-start | bytes 2359304 | tf_op jit(solution)/shard_map/ppermute | solution.py:326
  20.4 5.4 %all-to-all-done.got_ref = bf16[8,256,256]{2,1,0:T(8,128)(2,1)S(1)} async-done(((bf16[8,256,256]{2,1,0:T(8,128)(2,1)}), bf16[8,256,256]{2,1,0:T(8,128)(2,1)S(1)}, u32[]{:S(2)}, u32[]{:S(2)}) %all-to-all-start) | async-done | bytes 1048608 | tf_op jit(solution)/shard_map/all_to_all | solution.py:365
  26.4 19.2 %fwd_tiles.1 = (f32[256,768]{1,0:T(8,128)S(1)}, f32[8,768]{1,0:T(8,128)S(1)}, f32[8,768]{1,0:T(8,128)S(1)}) custom-call(s32[6,8]{1,0:T(8,128)S(1)} %bitcast.15, s32[6]{0:T(128)S(1)} %bitcast.19, bf16[768,256]{1,0:T(8,128)(2,1)S(1)} %copy-done.7, bf16[768,256]{1,0:T(8,128)(2,1)S(1)} %copy-done.2, bf16[768,256]{1,0:T(8,128)(2,1)S(1)} %copy-done.4, ...), custom_call_target="tpu_custom_call" | custom-call | flops 25769803776 | bytes 3145728 | tf_op jit(solution)/shard_map/fwd_tiles/pallas_call | solution.py:313
  45.7 2.1 %gather2.1 = (bf16[256,768]{1,0:T(8,128)(2,1)S(1)}, bf16[256,768]{1,0:T(8,128)(2,1)S(1)}, f32[8,768]{1,0:T(8,128)S(1)}, f32[8,768]{1,0:T(8,128)S(1)}) custom-call(s32[1,768]{1,0:T(1,128)S(1)} %get-tuple-element.75.match_ref, bf16[1536,256]{1,0:T(8,128)(2,1)} %collective-permute-done.2.moved_ref, bf16[256,768]{1,0:T(8,128)(2,1)S(1)} %copy-done.15, ...), custom_call_target="tpu_custom_call" | custom-call | flops 603979776 | bytes 2359296 | tf_op jit(solution)/shard_map/gather2/pallas_call | solution.py:313
  47.8 2.7 %collective-permute-done.1.moved_ref = bf16[1536,256]{1,0:T(8,128)(2,1)} collective-permute-done((bf16[1536,256]{1,0:T(8,128)(2,1)}, bf16[1536,256]{1,0:T(8,128)(2,1)}, u32[]{:S(2)}, u32[]{:S(2)}) %collective-permute-start.1) | collective-permute-done | bytes 786464 | tf_op jit(solution)/shard_map/ppermute | solution.py:326
  50.5 2.1 %gather1.1 = (bf16[256,768]{1,0:T(8,128)(2,1)S(1)}, bf16[256,768]{1,0:T(8,128)(2,1)S(1)}, f32[8,768]{1,0:T(8,128)S(1)}, f32[8,768]{1,0:T(8,128)S(1)}) custom-call(s32[1,768]{1,0:T(1,128)S(1)} %get-tuple-element.77.match_ref, bf16[1536,256]{1,0:T(8,128)(2,1)} %collective-permute-done.1.moved_ref, bf16[256,768]{1,0:T(8,128)(2,1)S(1)} %copy-done.15, ...), custom_call_target="tpu_custom_call" | custom-call | flops 603979776 | bytes 2359296 | tf_op jit(solution)/shard_map/gather1/pallas_call | solution.py:313
  52.9 2.1 %gather0.1 = (bf16[256,768]{1,0:T(8,128)(2,1)S(1)}, bf16[256,768]{1,0:T(8,128)(2,1)S(1)}, f32[8,768]{1,0:T(8,128)S(1)}, f32[8,768]{1,0:T(8,128)S(1)}) custom-call(s32[1,768]{1,0:T(1,128)S(1)} %get-tuple-element.76.match_ref, bf16[1536,256]{1,0:T(8,128)(2,1)} %collective-permute-done.moved_ref, bf16[256,768]{1,0:T(8,128)(2,1)S(1)} %copy-done.15, ...), custom_call_target="tpu_custom_call" | custom-call | flops 603979776 | bytes 2359296 | tf_op jit(solution)/shard_map/gather0/pallas_call | solution.py:313
  55.1 2.1 %merge.1 = (bf16[768,256]{1,0:T(8,128)(2,1)}, f32[256,256]{1,0:T(8,128)}, f32[8,768]{1,0:T(8,128)S(1)}, f32[8,768]{1,0:T(8,128)S(1)}, f32[256,768]{1,0:T(8,128)S...) custom-call(f32[8,1]{1,0:T(8,128)S(1)} %copy.15.refs_0_, ...), custom_call_target="tpu_custom_call" | custom-call | flops 201326592 | bytes 4718592 | tf_op jit(solution)/shard_map/merge/pallas_call | solution.py:313
  57.1 0.9 copy-done.12
  59.2 3.8 %all-to-all-start.2 = ((f32[32,8,256]{2,1,0:T(8,128)}), f32[32,8,256]{2,1,0:T(8,128)}, u32[]{:S(2)}, u32[]{:S(2)}) async-start(f32[32,8,256]{2,1,0:T(8,128)} %bitcast.6), calls=%async_computation.2 | async-start | bytes 524288 | tf_op jit(solution)/shard_map/all_to_all | solution.py:333
  63.1 0.8 scatter0.1.after0_ref
  63.9 0.8 scatter1.1.after1_ref
  64.8 0.8 scatter2.1.after2_ref
  65.7 0.9 copy-done.11
  66.6 31.2 %bwd_tiles.1 = (f32[768,256]{1,0:T(8,128)}, f32[768,256]{1,0:T(8,128)S(1)}, f32[768,256]{1,0:T(8,128)S(1)}, bf16[8,256,256]{2,1,0:T(8,128)(2,1)}) custom-call(s32[6,8]{1,0:T(8,128)S(1)} %bitcast.16, s32[6]{0:T(128)S(1)} %bitcast.20, bf16[768,256]{1,0:T(8,128)(2,1)S(1)} %copy-done.7, bf16[768,256]{1,0:T(8,128)(2,1)S(1)} %copy-done.2, ...), custom_call_target="tpu_custom_call" | custom-call | flops 38654705664 | bytes 9437184 | tf_op jit(solution)/shard_map/bwd_tiles/pallas_call | solution.py:313
  97.8 9.7 %all-to-all-start.1 = ((bf16[8,256,256]{2,1,0:T(8,128)(2,1)}), bf16[8,256,256]{2,1,0:T(8,128)(2,1)S(1)}, u32[]{:S(2)}, u32[]{:S(2)}) async-start(bf16[8,256,256]{2,1,0:T(8,128)(2,1)} %get-tuple-element.71), calls=%async_computation.1 | async-start | bytes 2097152 | tf_op jit(solution)/shard_map/all_to_all | solution.py:444
  107.5 2.3 %collective-permute-start.5 = (bf16[1536,256]{1,0:T(8,128)(2,1)}, bf16[1536,256]{1,0:T(8,128)(2,1)S(1)}, u32[]{:S(2)}, u32[]{:S(2)}) collective-permute-start(bf16[1536,256]{1,0:T(8,128)(2,1)} %copy-done.11), channel_id=1, source_target_pairs={{0,4},{1,5},{2,6},{3,7},{4,0},{5,1},{6,2},{7,3},{8,12},{9,13},{10,... | collective-permute-start | bytes 2359304 | tf_op jit(solution)/shard_map/ppermute | solution.py:326
  109.8 1.0 reduce_sum.9
  110.8 12.2 %all-to-all-done.1.home_ref = bf16[8,256,256]{2,1,0:T(8,128)(2,1)S(1)} async-done(((bf16[8,256,256]{2,1,0:T(8,128)(2,1)}), bf16[8,256,256]{2,1,0:T(8,128)(2,1)S(1)}, u32[]{:S(2)}, u32[]{:S(2)}) %all-to-all-start.1) | async-done | bytes 1048608 | tf_op jit(solution)/shard_map/all_to_all | solution.py:444
  123.7 3.3 %all-to-all-start.3 = ((f32[32,8,256]{2,1,0:T(8,128)}), f32[32,8,256]{2,1,0:T(8,128)}, u32[]{:S(2)}, u32[]{:S(2)}) async-start(f32[32,8,256]{2,1,0:T(8,128)} %broadcast_in_dim.2), calls=%async_computation.3 | async-start | bytes 524288 | tf_op jit(solution)/shard_map/all_to_all | solution.py:335
  127.0 12.3 %collective-permute-done.5.refs_2_ = bf16[1536,256]{1,0:T(8,128)(2,1)S(1)} collective-permute-done((bf16[1536,256]{1,0:T(8,128)(2,1)}, bf16[1536,256]{1,0:T(8,128)(2,1)S(1)}, u32[]{:S(2)}, u32[]{:S(2)}) %collective-permute-start.5) | collective-permute-done | bytes 786464 | tf_op jit(solution)/shard_map/ppermute | solution.py:326
  139.3 5.5 %collective-permute-done.4.refs_1_ = bf16[1536,256]{1,0:T(8,128)(2,1)} collective-permute-done((bf16[1536,256]{1,0:T(8,128)(2,1)}, bf16[1536,256]{1,0:T(8,128)(2,1)}, u32[]{:S(2)}, u32[]{:S(2)}) %collective-permute-start.4) | collective-permute-done | bytes 786464 | tf_op jit(solution)/shard_map/ppermute | solution.py:326
  144.8 6.3 %collective-permute-done.3.refs_0_ = bf16[1536,256]{1,0:T(8,128)(2,1)} collective-permute-done((bf16[1536,256]{1,0:T(8,128)(2,1)}, bf16[1536,256]{1,0:T(8,128)(2,1)}, u32[]{:S(2)}, u32[]{:S(2)}) %collective-permute-start.3) | collective-permute-done | bytes 786464 | tf_op jit(solution)/shard_map/ppermute | solution.py:326
  151.1 3.0 %final.1 = (f32[768,256]{1,0:T(8,128)}, f32[768,256]{1,0:T(8,128)}) custom-call(s32[8]{0:T(128)S(1)} %bitcast.18, f32[768,256]{1,0:T(8,128)S(1)} %get-tuple-element.69.dk_ref, f32[768,256]{1,0:T(8,128)S(1)} %get-tuple-element.70.dv_ref, bf16[8,256,256]{2,1,0:T(8,128)(2,1)S(1)} %all-to-all-done.1.home_ref, bf16[1536,256]{1,0:T(8,128)(2,1)} %collective-permute-done.3.refs_0_, ...), custom_call_target="tpu_custom_call" | custom-call | bytes 7864320 | tf_op jit(solution)/shard_map/final/pallas_call | solution.py:313
  154.2 1.7 %multiply_bitcast_fusion = f32[256,256]{1,0:T(8,128)} fusion(f32[32,8,256]{2,1,0:T(8,128)} %all-to-all-done.3), kind=kLoop, calls=%fused_computation | loop fusion | flops 65536 | bytes 524288 | tf_op jit(solution)/shard_map/mul | solution.py:421
  (62 shorter events, 6.6 us)
Async XLA Ops:
  1.3 1.0 copy-start.1
  2.3 1.0 copy-start.3
  4.9 5.3 %copy-start.2 = (bf16[768,256]{1,0:T(8,128)(2,1)S(1)}, bf16[768,256]{1,0:T(8,128)(2,1)}, u32[]{:S(2)}) copy-start(bf16[768,256]{1,0:T(8,128)(2,1)} %k_ref.5) | copy-start | bytes 1179652
  4.9 20.8 %all-to-all-start = ((bf16[8,256,256]{2,1,0:T(8,128)(2,1)}), bf16[8,256,256]{2,1,0:T(8,128)(2,1)S(1)}, u32[]{:S(2)}, u32[]{:S(2)}) async-start(bf16[8,256,256]{2,1,0:T(8,128)(2,1)} %pick.1), calls=%async_computation | async-start | bytes 2097152 | tf_op jit(solution)/shard_map/all_to_all | solution.py:365
  10.2 1.1 copy-start.4
  10.3 8.2 %copy-start.7 = (bf16[768,256]{1,0:T(8,128)(2,1)S(1)}, bf16[768,256]{1,0:T(8,128)(2,1)}, u32[]{:S(2)}) copy-start(bf16[768,256]{1,0:T(8,128)(2,1)} %q_ref.5) | copy-start | bytes 1179652
  11.4 7.0 %copy-start.26 = (f32[8]{0:T(128)S(1)}, f32[8]{0:T(128)}, u32[]{:S(2)}) copy-start(f32[8]{0:T(128)} %param.15) | copy-start | bytes 100
  11.4 7.1 %copy-start = (bf16[768,256]{1,0:T(8,128)(2,1)S(1)}, bf16[768,256]{1,0:T(8,128)(2,1)}, u32[]{:S(2)}) copy-start(bf16[768,256]{1,0:T(8,128)(2,1)} %refs_5_.1) | copy-start | bytes 1179652
  11.4 7.1 %copy-start.6 = (bf16[256,256]{1,0:T(8,128)(2,1)S(1)}, bf16[256,256]{1,0:T(8,128)(2,1)}, u32[]{:S(2)}) copy-start(bf16[256,256]{1,0:T(8,128)(2,1)} %refs_6_.1) | copy-start | bytes 393220
  12.2 6.3 %copy-start.25 = (s32[1,6,8]{2,0,1:T(1,128)S(1)}, s32[1,6,8]{2,0,1:T(1,128)}, u32[]{:S(2)}) copy-start(s32[1,6,8]{2,0,1:T(1,128)} %param.16) | copy-start | bytes 580
  12.2 33.5 %collective-permute-start.2 = (bf16[1536,256]{1,0:T(8,128)(2,1)}, bf16[1536,256]{1,0:T(8,128)(2,1)}, u32[]{:S(2)}, u32[]{:S(2)}) collective-permute-start(bf16[1536,256]{1,0:T(8,128)(2,1)} %constant_dynamic-update-slice_fusion), channel_id=1, source_target_pairs={{0,4},{1,5},{2,6},{3,7},{4,0},{5,1},{6,2},{7,3},{8,12},{9,13},{10,... | collective-permute-start | bytes 2359304 | tf_op jit(solution)/shard_map/ppermute | solution.py:326
  14.2 36.4 %collective-permute-start.1 = (bf16[1536,256]{1,0:T(8,128)(2,1)}, bf16[1536,256]{1,0:T(8,128)(2,1)}, u32[]{:S(2)}, u32[]{:S(2)}) collective-permute-start(bf16[1536,256]{1,0:T(8,128)(2,1)} %constant_dynamic-update-slice_fusion), channel_id=1, source_target_pairs={{0,8},{1,9},{2,10},{3,11},{4,12},{5,13},{6,14},{7,15},{8,0},{9,1},... | collective-permute-start | bytes 2359304 | tf_op jit(solution)/shard_map/ppermute | solution.py:326
  15.8 37.2 %collective-permute-start = (bf16[1536,256]{1,0:T(8,128)(2,1)}, bf16[1536,256]{1,0:T(8,128)(2,1)}, u32[]{:S(2)}, u32[]{:S(2)}) collective-permute-start(bf16[1536,256]{1,0:T(8,128)(2,1)} %constant_dynamic-update-slice_fusion), channel_id=1, source_target_pairs={{0,16},{1,17},{2,18},{3,19},{4,20},{5,21},{6,22},{7,23},{8,24},{9,... | collective-permute-start | bytes 2359304 | tf_op jit(solution)/shard_map/ppermute | solution.py:326
  18.5 1.9 %copy-start.24 = (s32[1,3,768]{2,0,1:T(1,128)S(1)}, s32[1,3,768]{2,0,1:T(1,128)}, u32[]{:S(2)}) copy-start(s32[1,3,768]{2,0,1:T(1,128)} %param.19) | copy-start | bytes 27652
  18.9 0.7 copy-start.14
  25.8 19.9 %copy-start.5 = (bf16[8,256,256]{2,1,0:T(8,128)(2,1)}, bf16[8,256,256]{2,1,0:T(8,128)(2,1)S(1)}, u32[]{:S(2)}) copy-start(bf16[8,256,256]{2,1,0:T(8,128)(2,1)S(1)} %all-to-all-done.got_ref) | copy-start | bytes 3145732
  26.4 19.3 %copy-start.15 = (bf16[256,768]{1,0:T(8,128)(2,1)S(1)}, bf16[256,768]{1,0:T(8,128)(2,1)}, u32[]{:S(2)}) copy-start(bf16[256,768]{1,0:T(8,128)(2,1)} %copy-done.14) | copy-start | bytes 1179652
  57.1 0.9 copy-start.12
  59.2 3.9 %copy-start.16 = (bf16[256,768]{1,0:T(8,128)(2,1)S(1)}, bf16[256,768]{1,0:T(8,128)(2,1)}, u32[]{:S(2)}) copy-start(bf16[256,768]{1,0:T(8,128)(2,1)} %copy-done.14) | copy-start | bytes 1179652
  59.2 38.5 %all-to-all-start.2 = ((f32[32,8,256]{2,1,0:T(8,128)}), f32[32,8,256]{2,1,0:T(8,128)}, u32[]{:S(2)}, u32[]{:S(2)}) async-start(f32[32,8,256]{2,1,0:T(8,128)} %bitcast.6), calls=%async_computation.2 | async-start | bytes 524288 | tf_op jit(solution)/shard_map/all_to_all | solution.py:333
  63.9 2.6 %copy-start.9 = (bf16[1536,256]{1,0:T(8,128)(2,1)}, bf16[1536,256]{1,0:T(8,128)(2,1)S(1)}, u32[]{:S(2)}) copy-start(bf16[1536,256]{1,0:T(8,128)(2,1)S(1)} %scatter0.1.after0_ref) | copy-start | bytes 2359300
  64.8 0.9 copy-start.10
  64.8 1.8 %copy-start.13 = (f32[256,768]{1,0:T(8,128)S(1)}, f32[256,768]{1,0:T(8,128)}, u32[]{:S(2)}) copy-start(f32[256,768]{1,0:T(8,128)} %copy-done.12) | copy-start | bytes 2359300
  64.8 1.8 %copy-start.18 = (bf16[768,256]{1,0:T(8,128)(2,1)S(1)}, bf16[768,256]{1,0:T(8,128)(2,1)}, u32[]{:S(2)}) copy-start(bf16[768,256]{1,0:T(8,128)(2,1)} %copy-done.17) | copy-start | bytes 1179652
  64.8 1.8 %copy-start.20 = (f32[8,768]{1,0:T(8,128)S(1)}, f32[8,768]{1,0:T(8,128)}, u32[]{:S(2)}) copy-start(f32[8,768]{1,0:T(8,128)} %copy-done.19) | copy-start | bytes 73732
  64.8 1.7 %copy-start.22 = (f32[8,768]{1,0:T(8,128)S(1)}, f32[8,768]{1,0:T(8,128)}, u32[]{:S(2)}) copy-start(f32[8,768]{1,0:T(8,128)} %copy-done.21) | copy-start | bytes 73732
  65.6 0.9 copy-start.11
  97.8 25.2 %all-to-all-start.1 = ((bf16[8,256,256]{2,1,0:T(8,128)(2,1)}), bf16[8,256,256]{2,1,0:T(8,128)(2,1)S(1)}, u32[]{:S(2)}, u32[]{:S(2)}) async-start(bf16[8,256,256]{2,1,0:T(8,128)(2,1)} %get-tuple-element.71), calls=%async_computation.1 | async-start | bytes 2097152 | tf_op jit(solution)/shard_map/all_to_all | solution.py:444
  107.5 31.8 %collective-permute-start.5 = (bf16[1536,256]{1,0:T(8,128)(2,1)}, bf16[1536,256]{1,0:T(8,128)(2,1)S(1)}, u32[]{:S(2)}, u32[]{:S(2)}) collective-permute-start(bf16[1536,256]{1,0:T(8,128)(2,1)} %copy-done.11), channel_id=1, source_target_pairs={{0,4},{1,5},{2,6},{3,7},{4,0},{5,1},{6,2},{7,3},{8,12},{9,13},{10,... | collective-permute-start | bytes 2359304 | tf_op jit(solution)/shard_map/ppermute | solution.py:326
  109.8 35.0 %collective-permute-start.4 = (bf16[1536,256]{1,0:T(8,128)(2,1)}, bf16[1536,256]{1,0:T(8,128)(2,1)}, u32[]{:S(2)}, u32[]{:S(2)}) collective-permute-start(bf16[1536,256]{1,0:T(8,128)(2,1)} %copy-done.10), channel_id=1, source_target_pairs={{0,8},{1,9},{2,10},{3,11},{4,12},{5,13},{6,14},{7,15},{8,0},{9,1},... | collective-permute-start | bytes 2359304 | tf_op jit(solution)/shard_map/ppermute | solution.py:326
  109.8 41.3 %collective-permute-start.3 = (bf16[1536,256]{1,0:T(8,128)(2,1)}, bf16[1536,256]{1,0:T(8,128)(2,1)}, u32[]{:S(2)}, u32[]{:S(2)}) collective-permute-start(bf16[1536,256]{1,0:T(8,128)(2,1)} %copy-done.9), channel_id=1, source_target_pairs={{0,16},{1,17},{2,18},{3,19},{4,20},{5,21},{6,22},{7,23},{8,24},{9,... | collective-permute-start | bytes 2359304 | tf_op jit(solution)/shard_map/ppermute | solution.py:326
  123.7 30.4 %all-to-all-start.3 = ((f32[32,8,256]{2,1,0:T(8,128)}), f32[32,8,256]{2,1,0:T(8,128)}, u32[]{:S(2)}, u32[]{:S(2)}) async-start(f32[32,8,256]{2,1,0:T(8,128)} %broadcast_in_dim.2), calls=%async_computation.3 | async-start | bytes 524288 | tf_op jit(solution)/shard_map/all_to_all | solution.py:335
  (5 other events, 3.3 us)

commit v3 on v2

--- a/solution.py
+++ b/solution.py
@@ -43,11 +43,13 @@
     return product.reshape(heads, features // heads, lanes).sum(axis=1)
 
 
-def pick_kernel(send_ref, k_ref, v_ref, out_ref, *, block):
+def pick_kernel(send_ref, both_ref, out_ref, *, block):
+    nodes = both_ref.shape[0] // 2
+
     def body(s, carry):
-        rows = pl.ds(pl.multiple_of(send_ref[s] * block, block), block)
-        out_ref[s, pl.ds(0, block), :] = k_ref[rows, :]
-        out_ref[s, pl.ds(block, block), :] = v_ref[rows, :]
+        start = pl.multiple_of(send_ref[s] * block, block)
+        out_ref[s, pl.ds(0, block), :] = both_ref[pl.ds(start, block), :]
+        out_ref[s, pl.ds(block, block), :] = both_ref[pl.ds(nodes + start, block), :]
         return carry
 
     lax.fori_loop(0, out_ref.shape[0], body, 0)
@@ -190,7 +192,7 @@
     tb_ref, tc_ref, q_ref, k_ref, v_ref, got_ref, qt_ref, gat_ref, ga_ref,
     lse_ref, delta_ref, eq_ref, after0_ref, after1_ref, after2_ref,
     dq_ref, dk_ref, dv_ref, ret_ref,
-    ktab, vtab, kttab, qxt, gxt, qx, gx, dkt, dvt, acc, lse_s, delta_s,
+    ktab, vtab, kttab, kcat, vcat, ktcat, pbuf, dsbuf, qxt, gxt, qx, gx, dkt, dvt, acc, lse_s, delta_s,
     *, heads, block,
 ):
     nodes, feat = q_ref.shape
@@ -200,6 +202,7 @@
     scale = width**-0.5
     scale2 = scale * LOG2E
     groups = heads // 2
+    slots = tb_ref.shape[1]
 
     def fill_own(b, carry):
         rows = pl.ds(pl.multiple_of(b * block, block), block)
@@ -242,38 +245,42 @@
             gx[bs, :] = jnp.where(lanes == h, gf, 0.0).astype(BF16)
             lse_s[:, bs] = lse_ref[h : h + 1, rows]
             delta_s[:, bs] = delta_ref[h : h + 1, rows]
-        acc[...] = jnp.zeros(acc.shape, F32)
 
         count = tc_ref[b]
 
-        def do_pair(pair, inner):
-            first, second = tb_ref[b, 2 * pair], tb_ref[b, 2 * pair + 1]
-            live = 2 * pair + 1 < count
-            k = jnp.concatenate([ktab[first], ktab[second]], axis=0)
-            v = jnp.concatenate([vtab[first], vtab[second]], axis=0)
-            ps, dss = [], []
-            for g in range(groups):
-                cols = slice(g * 2 * block, (g + 1) * 2 * block)
-                feats = slice(g * 2 * width, (g + 1) * 2 * width)
-                s = dot(k, qxt[:, cols])
-                p = jnp.exp2(s * scale2 - lse_s[:, cols])
-                p = jnp.concatenate([p[:block], jnp.where(live, p[block:], 0.0)], axis=0)
-                dp = dot(v, gxt[:, cols])
-                ds = (p * (dp - delta_s[:, cols])).astype(BF16)
-                ps.append(p.astype(BF16))
-                dss.append(ds)
-                kt = jnp.concatenate([kttab[first, feats, :], kttab[second, feats, :]], axis=1)
-                o = dot(kt, ds)
-                acc[feats, :] += jnp.concatenate([o[:width, :block], o[width:, block:]], axis=0)
-            dv = dot(jnp.concatenate(ps, axis=1), gx[...])
-            dk = dot(jnp.concatenate(dss, axis=1), qx[...])
-            dvt[first] += dv[:block]
-            dvt[second] += dv[block:]
-            dkt[first] += dk[:block]
-            dkt[second] += dk[block:]
-            return inner
-
-        lax.fori_loop(0, (count + 1) // 2, do_pair, 0)
+        for t in range(slots):
+            index = tb_ref[b, t]
+            part = slice(t * block, (t + 1) * block)
+            kcat[part, :] = ktab[index]
+            vcat[part, :] = vtab[index]
+            ktcat[:, part] = kttab[index]
+        for g in range(groups):
+            cols = slice(g * 2 * block, (g + 1) * 2 * block)
+            feats = slice(g * 2 * width, (g + 1) * 2 * width)
+            s = dot(kcat[...], qxt[:, cols])
+            p = jnp.exp2(s * scale2 - lse_s[:, cols])
+            p = jnp.concatenate(
+                [
+                    p[t * block : (t + 1) * block]
+                    if t < LEAST
+                    else jnp.where(t < count, p[t * block : (t + 1) * block], 0.0)
+                    for t in range(slots)
+                ],
+                axis=0,
+            )
+            dp = dot(vcat[...], gxt[:, cols])
+            ds = (p * (dp - delta_s[:, cols])).astype(BF16)
+            pbuf[:, cols] = p.astype(BF16)
+            dsbuf[:, cols] = ds
+            o = dot(ktcat[feats, :], ds)
+            acc[feats, :] = jnp.concatenate([o[:width, :block], o[width:, block:]], axis=0)
+        dv = dot(pbuf[...], gx[...])
+        dk = dot(dsbuf[...], qx[...])
+        for t in range(slots):
+            index = tb_ref[b, t]
+            part = slice(t * block, (t + 1) * block)
+            dvt[index] += dv[part]
+            dkt[index] += dk[part]
         dq_ref[rows, :] = (acc[...] * scale + eq_ref[:, rows]).T
         return carry
 
@@ -292,6 +299,10 @@
 
     lax.fori_loop(0, blocks, drain_own, 0)
     lax.fori_loop(0, halo, drain_halo, 0)
+
+
+def pass_kernel(back_ref, *refs):
+    pass
 
 
 def final_kernel(send_ref, dk_ref, dv_ref, home_ref, *refs, block):
@@ -358,8 +369,8 @@
     both = jnp.concatenate([key_rows, value_rows], axis=0)
     moved = [from_partner(both, axes, top_bit - 1 - turn) for turn in range(3)]
     (sent,) = call(
-        pick_kernel, "pick", [SMEM, VMEM, VMEM], [((halo, 2 * block, feat), BF16)],
-        (send_block, key_rows, value_rows), block=block,
+        pick_kernel, "pick", [SMEM, VMEM], [((halo, 2 * block, feat), BF16)],
+        (send_block, both), block=block,
         estimate=cost(0, 4 * halo * block * feat * 2),
     )
     got = lax.all_to_all(sent, "dom", split_axis=0, concat_axis=0, tiled=True)
@@ -382,7 +393,7 @@
             pltpu.VMEM((1, wide), F32),
             pltpu.VMEM((1, wide), F32),
         ],
-        estimate=cost(8 * tile_flops, 8 * nodes * feat * 2),
+        estimate=cost(tile_flops / 2, nodes * feat),
         heads=heads, block=block,
     )
     rows = [matching[turn : turn + 1] for turn in range(3)]
@@ -428,6 +439,11 @@
             pltpu.VMEM((entries, block, feat), BF16),
             pltpu.VMEM((entries, block, feat), BF16),
             pltpu.VMEM((entries, feat, block), BF16),
+            pltpu.VMEM((slots * block, feat), BF16),
+            pltpu.VMEM((slots * block, feat), BF16),
+            pltpu.VMEM((feat, slots * block), BF16),
+            pltpu.VMEM((slots * block, wide), BF16),
+            pltpu.VMEM((slots * block, wide), BF16),
             pltpu.VMEM((feat, wide), BF16),
             pltpu.VMEM((feat, wide), BF16),
             pltpu.VMEM((wide, feat), BF16),
@@ -438,9 +454,18 @@
             pltpu.VMEM((1, wide), F32),
             pltpu.VMEM((1, wide), F32),
         ],
-        estimate=cost(12 * tile_flops, 24 * nodes * feat * 2),
+        estimate=cost(tile_flops / 2, nodes * feat),
         heads=heads, block=block,
     )
+    back = pl.pallas_call(
+        pass_kernel,
+        name="after_terms",
+        in_specs=[ANY] * 4,
+        out_specs=ANY,
+        out_shape=jax.ShapeDtypeStruct(back.shape, back.dtype),
+        input_output_aliases={0: 0},
+        cost_estimate=cost(0, 0),
+    )(back, *owned)
     home = lax.all_to_all(back, "dom", split_axis=0, concat_axis=0, tiled=True)
     key_grad, value_grad = call(
         final_kernel, "final", [SMEM] + [VMEM] * 6,

time: 155 us -> 137 us (0.88); the launches traced: 156 us -> 136 us
  waiting for transfers between devices: 44.7 us -> 25.7 us
  local copies, waits for them, and re-layouts: 10.5 us -> 19.3 us
  Pallas kernels: 66.4 us -> 59.8 us
  starting transfers between devices: 30.7 us -> 28.3 us
    ppermute x6, waiting for transfers between devices: 27 us -> 4.28 us  [from_partner(): lax.ppermute(array, axis, [(i, i ^ 1 << apart) for i in range(lax.axis_si...]
    unnamed x56 -> x78, local copies, waits for them, and re-layouts: 8.92 us -> 17.9 us
    pallas_call x12, Pallas kernels: 66.4 us -> 59.8 us  [call(): pl.pallas_call(functools.partial(kernel, **static), name=name, in_specs=i...]
    all_to_all x1, starting transfers between devices: 9.71 us -> 3.69 us  [shards(): home = lax.all_to_all(back, 'dom', split_axis=0, concat_axis=0, tiled=True)]
    ppermute x6, starting transfers between devices: 8.49 us -> 11.9 us  [from_partner(): lax.ppermute(array, axis, [(i, i ^ 1 << apart) for i in range(lax.axis_si...]
  transfers between devices with their start and end apart: 10 -> 10, of which waited for: 7 -> 4; matrix products, arithmetic and copies ran while one was open for 2% -> 2% of each run, Pallas kernels for 39% -> 38%
where the time goes in v3:
time: 137 us; the launch traced here: 136 us
  Pallas kernels  59.8 us (44%)
  starting transfers between devices  28.3 us (21%)
  waiting for transfers between devices  25.7 us (19%)
  local copies, waits for them, and re-layouts  19.3 us (14%)
  other arithmetic  1.71 us (1%)
    pallas_call x12, Pallas kernels, call(): pl.pallas_call(functools.partial(kernel, **static), name=name, in_specs=i...  59.8 us
    unnamed x78, local copies, waits for them, and re-layouts  17.9 us
    all_to_all x1, waiting for transfers between devices, shards(): home = lax.all_to_all(back, 'dom', split_axis=0, concat_axis=0, tiled=True)  13.7 us
    ppermute x6, starting transfers between devices, from_partner(): lax.ppermute(array, axis, [(i, i ^ 1 << apart) for i in range(lax.axis_si...  11.9 us
    all_to_all x1, waiting for transfers between devices, shards(): got = lax.all_to_all(sent, 'dom', split_axis=0, concat_axis=0, tiled=True)  6.67 us
    all_to_all x1, starting transfers between devices, shards(): got = lax.all_to_all(sent, 'dom', split_axis=0, concat_axis=0, tiled=True)  5.31 us
    ppermute x6, waiting for transfers between devices, from_partner(): lax.ppermute(array, axis, [(i, i ^ 1 << apart) for i in range(lax.axis_si...  4.28 us
    all_to_all x1, starting transfers between devices, reduce_everywhere(): lax.all_to_all(parts, axes, split_axis=0, concat_axis=0, tiled=True)  3.97 us
  transfers between devices with their start and end apart: 10, of which 4 were waited for; matrix products, arithmetic and copies ran while one was open for 2% of the time, Pallas kernels for 38%

profile of v3, /device:TPU:0, one launch (start us, length us, event | category | flops | bytes accessed | tf_op | source)
XLA Modules:
  0.0 135.7 jit_solution(17195778744841298385)
XLA Ops:
  0.6 1.1 constant_dynamic-update-slice_fusion.1
  2.4 1.6 %pick.1 = bf16[8,256,256]{2,1,0:T(8,128)(2,1)} custom-call(s32[8]{0:T(128)S(1)} %bitcast.17, bf16[1536,256]{1,0:T(8,128)(2,1)S(1)} %constant_dynamic-update-slice_fusion.both_ref), custom_call_target="tpu_custom_call" | custom-call | bytes 2097152 | tf_op jit(solution)/shard_map/pick/pallas_call | solution.py:324
  4.1 5.3 %all-to-all-start = ((bf16[8,256,256]{2,1,0:T(8,128)(2,1)}), bf16[8,256,256]{2,1,0:T(8,128)(2,1)S(1)}, u32[]{:S(2)}, u32[]{:S(2)}) async-start(bf16[8,256,256]{2,1,0:T(8,128)(2,1)} %pick.1), calls=%async_computation | async-start | bytes 2097152 | tf_op jit(solution)/shard_map/all_to_all | solution.py:376
  9.4 2.0 %collective-permute-start.2 = (bf16[1536,256]{1,0:T(8,128)(2,1)S(1)}, bf16[1536,256]{1,0:T(8,128)(2,1)}, u32[]{:S(2)}, u32[]{:S(2)}) collective-permute-start(bf16[1536,256]{1,0:T(8,128)(2,1)S(1)} %constant_dynamic-update-slice_fusion.both_ref), channel_id=1, source_target_pairs={{0,4},{1,5},{2,6},{3,7},{4,0},{5,1},{6,2},{7,3},{8,12},{9,13},{10,... | collective-permute-start | bytes 2359304 | tf_op jit(solution)/shard_map/ppermute | solution.py:337
  11.4 1.6 %collective-permute-start.1 = (bf16[1536,256]{1,0:T(8,128)(2,1)S(1)}, bf16[1536,256]{1,0:T(8,128)(2,1)}, u32[]{:S(2)}, u32[]{:S(2)}) collective-permute-start(bf16[1536,256]{1,0:T(8,128)(2,1)S(1)} %constant_dynamic-update-slice_fusion.both_ref), channel_id=1, source_target_pairs={{0,8},{1,9},{2,10},{3,11},{4,12},{5,13},{6,14},{7,15},{8,0},{9,1},... | collective-permute-start | bytes 2359304 | tf_op jit(solution)/shard_map/ppermute | solution.py:337
  13.0 2.6 %collective-permute-start = (bf16[1536,256]{1,0:T(8,128)(2,1)S(1)}, bf16[1536,256]{1,0:T(8,128)(2,1)}, u32[]{:S(2)}, u32[]{:S(2)}) collective-permute-start(bf16[1536,256]{1,0:T(8,128)(2,1)S(1)} %constant_dynamic-update-slice_fusion.both_ref), channel_id=1, source_target_pairs={{0,16},{1,17},{2,18},{3,19},{4,20},{5,21},{6,22},{7,23},{8,24},{9,... | collective-permute-start | bytes 2359304 | tf_op jit(solution)/shard_map/ppermute | solution.py:337
  18.2 6.7 %all-to-all-done.got_ref = bf16[8,256,256]{2,1,0:T(8,128)(2,1)S(1)} async-done(((bf16[8,256,256]{2,1,0:T(8,128)(2,1)}), bf16[8,256,256]{2,1,0:T(8,128)(2,1)S(1)}, u32[]{:S(2)}, u32[]{:S(2)}) %all-to-all-start) | async-done | bytes 1048608 | tf_op jit(solution)/shard_map/all_to_all | solution.py:376
  25.5 1.0 copy-done.15
  26.5 19.2 %fwd_tiles.1 = (f32[256,768]{1,0:T(8,128)S(1)}, f32[8,768]{1,0:T(8,128)S(1)}, f32[8,768]{1,0:T(8,128)S(1)}) custom-call(s32[6,8]{1,0:T(8,128)S(1)} %bitcast.15, s32[6]{0:T(128)S(1)} %bitcast.19, bf16[768,256]{1,0:T(8,128)(2,1)S(1)} %copy-done.8, bf16[768,256]{1,0:T(8,128)(2,1)S(1)} %copy-done.12, bf16[768,256]{1,0:T(8,128)(2,1)S(1)} %copy-done.15, ...), custom_call_target="tpu_custom_call" | custom-call | flops 1610612736 | bytes 196608 | tf_op jit(solution)/shard_map/fwd_tiles/pallas_call | solution.py:324
  46.5 2.1 %gather2.1 = (bf16[256,768]{1,0:T(8,128)(2,1)S(1)}, bf16[256,768]{1,0:T(8,128)(2,1)S(1)}, f32[8,768]{1,0:T(8,128)S(1)}, f32[8,768]{1,0:T(8,128)S(1)}) custom-call(s32[1,768]{1,0:T(1,128)S(1)} %copy-done.30, bf16[1536,256]{1,0:T(8,128)(2,1)} %collective-permute-done.2.moved_ref, bf16[256,768]{1,0:T(8,128)(2,1)S(1)} %copy-done.25, ...), custom_call_target="tpu_custom_call" | custom-call | flops 603979776 | bytes 2359296 | tf_op jit(solution)/shard_map/gather2/pallas_call | solution.py:324
  48.7 2.1 %gather1.1 = (bf16[256,768]{1,0:T(8,128)(2,1)S(1)}, bf16[256,768]{1,0:T(8,128)(2,1)S(1)}, f32[8,768]{1,0:T(8,128)S(1)}, f32[8,768]{1,0:T(8,128)S(1)}) custom-call(s32[1,768]{1,0:T(1,128)S(1)} %get-tuple-element.77.match_ref, bf16[1536,256]{1,0:T(8,128)(2,1)} %collective-permute-done.1.moved_ref, bf16[256,768]{1,0:T(8,128)(2,1)S(1)} %copy-done.25, ...), custom_call_target="tpu_custom_call" | custom-call | flops 603979776 | bytes 2359296 | tf_op jit(solution)/shard_map/gather1/pallas_call | solution.py:324
  50.8 2.1 %gather0.1 = (bf16[256,768]{1,0:T(8,128)(2,1)S(1)}, bf16[256,768]{1,0:T(8,128)(2,1)S(1)}, f32[8,768]{1,0:T(8,128)S(1)}, f32[8,768]{1,0:T(8,128)S(1)}) custom-call(s32[1,768]{1,0:T(1,128)S(1)} %get-tuple-element.76.match_ref, bf16[1536,256]{1,0:T(8,128)(2,1)} %collective-permute-done.moved_ref, bf16[256,768]{1,0:T(8,128)(2,1)S(1)} %copy-done.25, ...), custom_call_target="tpu_custom_call" | custom-call | flops 603979776 | bytes 2359296 | tf_op jit(solution)/shard_map/gather0/pallas_call | solution.py:324
  53.0 2.1 %merge.1 = (bf16[768,256]{1,0:T(8,128)(2,1)}, f32[256,256]{1,0:T(8,128)}, f32[8,768]{1,0:T(8,128)S(1)}, f32[8,768]{1,0:T(8,128)S(1)}, f32[256,768]{1,0:T(8,128)S...) custom-call(f32[8,1]{1,0:T(8,128)S(1)} %copy.16.refs_0_, ...), custom_call_target="tpu_custom_call" | custom-call | flops 201326592 | bytes 4718592 | tf_op jit(solution)/shard_map/merge/pallas_call | solution.py:324
  55.9 4.0 %all-to-all-start.2 = ((f32[32,8,256]{2,1,0:T(8,128)}), f32[32,8,256]{2,1,0:T(8,128)S(1)}, u32[]{:S(2)}, u32[]{:S(2)}) async-start(f32[32,8,256]{2,1,0:T(8,128)} %bitcast.6), calls=%async_computation.2 | async-start | bytes 524288 | tf_op jit(solution)/shard_map/all_to_all | solution.py:344
  59.9 1.7 %scatter2.1.after2_ref = bf16[1536,256]{1,0:T(8,128)(2,1)} custom-call(s32[1,768]{1,0:T(1,128)S(1)} %copy-done.30, bf16[256,768]{1,0:T(8,128)(2,1)S(1)} %copy-done.26, bf16[256,768]{1,0:T(8,128)(2,1)S(1)} %get-tuple-element.43.gat_ref.refs_4_, f32[8,768]{1,0:T(8,128)S(1)} %get-tuple-element.66.ds_ref, f32[8,768]{1,0:T(8,128)S(1)} %get-tuple-element.67.wt_ref), custom_call_target="tpu_custom_call" | custom-call | flops 603979776 | bytes 1966080 | tf_op jit(solution)/shard_map/scatter2/pallas_call | solution.py:324
  61.6 1.8 %collective-permute-start.5 = (bf16[1536,256]{1,0:T(8,128)(2,1)}, bf16[1536,256]{1,0:T(8,128)(2,1)S(1)}, u32[]{:S(2)}, u32[]{:S(2)}) collective-permute-start(bf16[1536,256]{1,0:T(8,128)(2,1)} %scatter2.1.after2_ref), channel_id=1, source_target_pairs={{0,4},{1,5},{2,6},{3,7},{4,0},{5,1},{6,2},{7,3},{8,12},{9,13},{10,... | collective-permute-start | bytes 2359304 | tf_op jit(solution)/shard_map/ppermute | solution.py:337
  63.4 1.7 %scatter1.1.after1_ref = bf16[1536,256]{1,0:T(8,128)(2,1)} custom-call(s32[1,768]{1,0:T(1,128)S(1)} %get-tuple-element.77.match_ref, bf16[256,768]{1,0:T(8,128)(2,1)S(1)} %copy-done.26, bf16[256,768]{1,0:T(8,128)(2,1)S(1)} %get-tuple-element.43.gat_ref.refs_4_, f32[8,768]{1,0:T(8,128)S(1)} %get-tuple-element.64.ds_ref, f32[8,768]{1,0:T(8,128)S(1)} %get-tuple-element.65.wt_ref), custom_call_target="tpu_custom_call" | custom-call | flops 603979776 | bytes 1966080 | tf_op jit(solution)/shard_map/scatter1/pallas_call | solution.py:324
  65.1 1.5 %collective-permute-start.4 = (bf16[1536,256]{1,0:T(8,128)(2,1)}, bf16[1536,256]{1,0:T(8,128)(2,1)S(1)}, u32[]{:S(2)}, u32[]{:S(2)}) collective-permute-start(bf16[1536,256]{1,0:T(8,128)(2,1)} %scatter1.1.after1_ref), channel_id=1, source_target_pairs={{0,8},{1,9},{2,10},{3,11},{4,12},{5,13},{6,14},{7,15},{8,0},{9,1},... | collective-permute-start | bytes 2359304 | tf_op jit(solution)/shard_map/ppermute | solution.py:337
  66.6 1.7 %scatter0.1.after0_ref = bf16[1536,256]{1,0:T(8,128)(2,1)} custom-call(s32[1,768]{1,0:T(1,128)S(1)} %get-tuple-element.76.match_ref, bf16[256,768]{1,0:T(8,128)(2,1)S(1)} %copy-done.26, bf16[256,768]{1,0:T(8,128)(2,1)S(1)} %get-tuple-element.43.gat_ref.refs_4_, f32[8,768]{1,0:T(8,128)S(1)} %get-tuple-element.62.ds_ref, f32[8,768]{1,0:T(8,128)S(1)} %get-tuple-element.63.wt_ref), custom_call_target="tpu_custom_call" | custom-call | flops 603979776 | bytes 1966080 | tf_op jit(solution)/shard_map/scatter0/pallas_call | solution.py:324
  68.3 2.4 %collective-permute-start.3 = (bf16[1536,256]{1,0:T(8,128)(2,1)}, bf16[1536,256]{1,0:T(8,128)(2,1)S(1)}, u32[]{:S(2)}, u32[]{:S(2)}) collective-permute-start(bf16[1536,256]{1,0:T(8,128)(2,1)} %scatter0.1.after0_ref), channel_id=1, source_target_pairs={{0,16},{1,17},{2,18},{3,19},{4,20},{5,21},{6,22},{7,23},{8,24},{9,... | collective-permute-start | bytes 2359304 | tf_op jit(solution)/shard_map/ppermute | solution.py:337
  71.5 3.5 %all-to-all-start.3 = ((f32[32,8,256]{2,1,0:T(8,128)}), f32[32,8,256]{2,1,0:T(8,128)}, u32[]{:S(2)}, u32[]{:S(2)}) async-start(f32[32,8,256]{2,1,0:T(8,128)} %broadcast_in_dim.2), calls=%async_computation.3 | async-start | bytes 524288 | tf_op jit(solution)/shard_map/all_to_all | solution.py:346
  75.7 1.0 copy-done.13
  77.7 1.1 copy-done.18
  80.8 22.6 %bwd_tiles.1 = (f32[768,256]{1,0:T(8,128)}, f32[768,256]{1,0:T(8,128)S(1)}, f32[768,256]{1,0:T(8,128)S(1)}, bf16[8,256,256]{2,1,0:T(8,128)(2,1)}) custom-call(s32[6,8]{1,0:T(8,128)S(1)} %bitcast.16, s32[6]{0:T(128)S(1)} %bitcast.20, bf16[768,256]{1,0:T(8,128)(2,1)S(1)} %copy-done.9, bf16[768,256]{1,0:T(8,128)(2,1)S(1)} %copy-done.13, ...), custom_call_target="tpu_custom_call" | custom-call | flops 1610612736 | bytes 196608 | tf_op jit(solution)/shard_map/bwd_tiles/pallas_call | solution.py:324
  105.3 4.3 %collective-permute-done.3.refs_0_ = bf16[1536,256]{1,0:T(8,128)(2,1)S(1)} collective-permute-done((bf16[1536,256]{1,0:T(8,128)(2,1)}, bf16[1536,256]{1,0:T(8,128)(2,1)S(1)}, u32[]{:S(2)}, u32[]{:S(2)}) %collective-permute-start.3) | collective-permute-done | bytes 786464 | tf_op jit(solution)/shard_map/ppermute | solution.py:337
  110.4 1.1 all-to-all-done.3
  111.5 3.7 %all-to-all-start.1 = ((bf16[8,256,256]{2,1,0:T(8,128)(2,1)}), bf16[8,256,256]{2,1,0:T(8,128)(2,1)S(1)}, u32[]{:S(2)}, u32[]{:S(2)}) async-start(bf16[8,256,256]{2,1,0:T(8,128)(2,1)} %after_terms.1), calls=%async_computation.1 | async-start | bytes 2097152 | tf_op jit(solution)/shard_map/all_to_all | solution.py:469
  115.2 1.7 %multiply_bitcast_fusion = f32[256,256]{1,0:T(8,128)} fusion(f32[32,8,256]{2,1,0:T(8,128)} %all-to-all-done.3), kind=kLoop, calls=%fused_computation | loop fusion | flops 65536 | bytes 524288 | tf_op jit(solution)/shard_map/mul | solution.py:432
  116.9 13.7 %all-to-all-done.1.home_ref = bf16[8,256,256]{2,1,0:T(8,128)(2,1)S(1)} async-done(((bf16[8,256,256]{2,1,0:T(8,128)(2,1)}), bf16[8,256,256]{2,1,0:T(8,128)(2,1)S(1)}, u32[]{:S(2)}, u32[]{:S(2)}) %all-to-all-start.1) | async-done | bytes 1048608 | tf_op jit(solution)/shard_map/all_to_all | solution.py:469
  131.2 1.1 copy-done.20
  132.3 1.1 copy-done.22
  133.5 2.3 %final.1 = (f32[768,256]{1,0:T(8,128)}, f32[768,256]{1,0:T(8,128)}) custom-call(s32[8]{0:T(128)S(1)} %bitcast.18, f32[768,256]{1,0:T(8,128)S(1)} %copy-done.20, f32[768,256]{1,0:T(8,128)S(1)} %copy-done.22, bf16[8,256,256]{2,1,0:T(8,128)(2,1)S(1)} %all-to-all-done.1.home_ref, bf16[1536,256]{1,0:T(8,128)(2,1)S(1)} %copy-done.6, ...), custom_call_target="tpu_custom_call" | custom-call | bytes 7864320 | tf_op jit(solution)/shard_map/final/pallas_call | solution.py:324
  (85 shorter events, 13.3 us)
Async XLA Ops:
  0.6 1.1 copy-start.14
  4.0 11.5 %copy-start.37 = (f32[8]{0:T(128)S(1)}, f32[8]{0:T(128)}, u32[]{:S(2)}) copy-start(f32[8]{0:T(128)} %param.15) | copy-start | bytes 100
  4.0 11.6 %copy-start.7 = (bf16[768,256]{1,0:T(8,128)(2,1)S(1)}, bf16[768,256]{1,0:T(8,128)(2,1)}, u32[]{:S(2)}) copy-start(bf16[768,256]{1,0:T(8,128)(2,1)} %refs_5_.1) | copy-start | bytes 1179652
  4.1 11.6 %copy-start.8 = (bf16[768,256]{1,0:T(8,128)(2,1)S(1)}, bf16[768,256]{1,0:T(8,128)(2,1)}, u32[]{:S(2)}) copy-start(bf16[768,256]{1,0:T(8,128)(2,1)} %q_ref.5) | copy-start | bytes 1179652
  4.1 11.6 %copy-start.23 = (bf16[256,256]{1,0:T(8,128)(2,1)S(1)}, bf16[256,256]{1,0:T(8,128)(2,1)}, u32[]{:S(2)}) copy-start(bf16[256,256]{1,0:T(8,128)(2,1)} %refs_6_.1) | copy-start | bytes 393220
  4.1 20.8 %all-to-all-start = ((bf16[8,256,256]{2,1,0:T(8,128)(2,1)}), bf16[8,256,256]{2,1,0:T(8,128)(2,1)S(1)}, u32[]{:S(2)}, u32[]{:S(2)}) async-start(bf16[8,256,256]{2,1,0:T(8,128)(2,1)} %pick.1), calls=%async_computation | async-start | bytes 2097152 | tf_op jit(solution)/shard_map/all_to_all | solution.py:376
  9.4 6.3 %copy-start.36 = (s32[1,6,8]{2,0,1:T(1,128)S(1)}, s32[1,6,8]{2,0,1:T(1,128)}, u32[]{:S(2)}) copy-start(s32[1,6,8]{2,0,1:T(1,128)} %param.16) | copy-start | bytes 580
  9.4 36.4 %collective-permute-start.2 = (bf16[1536,256]{1,0:T(8,128)(2,1)S(1)}, bf16[1536,256]{1,0:T(8,128)(2,1)}, u32[]{:S(2)}, u32[]{:S(2)}) collective-permute-start(bf16[1536,256]{1,0:T(8,128)(2,1)S(1)} %constant_dynamic-update-slice_fusion.both_ref), channel_id=1, source_target_pairs={{0,4},{1,5},{2,6},{3,7},{4,0},{5,1},{6,2},{7,3},{8,12},{9,13},{10,... | collective-permute-start | bytes 2359304 | tf_op jit(solution)/shard_map/ppermute | solution.py:337
  11.4 37.2 %collective-permute-start.1 = (bf16[1536,256]{1,0:T(8,128)(2,1)S(1)}, bf16[1536,256]{1,0:T(8,128)(2,1)}, u32[]{:S(2)}, u32[]{:S(2)}) collective-permute-start(bf16[1536,256]{1,0:T(8,128)(2,1)S(1)} %constant_dynamic-update-slice_fusion.both_ref), channel_id=1, source_target_pairs={{0,8},{1,9},{2,10},{3,11},{4,12},{5,13},{6,14},{7,15},{8,0},{9,1},... | collective-permute-start | bytes 2359304 | tf_op jit(solution)/shard_map/ppermute | solution.py:337
  13.0 37.8 %collective-permute-start = (bf16[1536,256]{1,0:T(8,128)(2,1)S(1)}, bf16[1536,256]{1,0:T(8,128)(2,1)}, u32[]{:S(2)}, u32[]{:S(2)}) collective-permute-start(bf16[1536,256]{1,0:T(8,128)(2,1)S(1)} %constant_dynamic-update-slice_fusion.both_ref), channel_id=1, source_target_pairs={{0,16},{1,17},{2,18},{3,19},{4,20},{5,21},{6,22},{7,23},{8,24},{9,... | collective-permute-start | bytes 2359304 | tf_op jit(solution)/shard_map/ppermute | solution.py:337
  15.7 1.9 %copy-start.35 = (s32[1,3,768]{2,0,1:T(1,128)S(1)}, s32[1,3,768]{2,0,1:T(1,128)}, u32[]{:S(2)}) copy-start(s32[1,3,768]{2,0,1:T(1,128)} %param.19) | copy-start | bytes 27652
  15.7 9.2 %copy-start.12 = (bf16[768,256]{1,0:T(8,128)(2,1)S(1)}, bf16[768,256]{1,0:T(8,128)(2,1)}, u32[]{:S(2)}) copy-start(bf16[768,256]{1,0:T(8,128)(2,1)} %k_ref.3) | copy-start | bytes 1179652
  17.6 49.0 %copy-start.10 = (bf16[256,768]{1,0:T(8,128)(2,1)}, bf16[256,768]{1,0:T(8,128)(2,1)S(1)}, u32[]{:S(2)}) copy-start(bf16[256,768]{1,0:T(8,128)(2,1)S(1)} %get-tuple-element.43.gat_ref.refs_4_) | copy-start | bytes 1179652
  24.9 20.9 %copy-start = (bf16[8,256,256]{2,1,0:T(8,128)(2,1)}, bf16[8,256,256]{2,1,0:T(8,128)(2,1)S(1)}, u32[]{:S(2)}) copy-start(bf16[8,256,256]{2,1,0:T(8,128)(2,1)S(1)} %all-to-all-done.got_ref) | copy-start | bytes 3145732
  26.5 19.3 %copy-start.25 = (bf16[256,768]{1,0:T(8,128)(2,1)S(1)}, bf16[256,768]{1,0:T(8,128)(2,1)}, u32[]{:S(2)}) copy-start(bf16[256,768]{1,0:T(8,128)(2,1)} %copy-done.24) | copy-start | bytes 1179652
  55.9 4.0 %copy-start.26 = (bf16[256,768]{1,0:T(8,128)(2,1)S(1)}, bf16[256,768]{1,0:T(8,128)(2,1)}, u32[]{:S(2)}) copy-start(bf16[256,768]{1,0:T(8,128)(2,1)} %copy-done.24) | copy-start | bytes 1179652
  55.9 14.8 %all-to-all-start.2 = ((f32[32,8,256]{2,1,0:T(8,128)}), f32[32,8,256]{2,1,0:T(8,128)S(1)}, u32[]{:S(2)}, u32[]{:S(2)}) async-start(f32[32,8,256]{2,1,0:T(8,128)} %bitcast.6), calls=%async_computation.2 | async-start | bytes 524288 | tf_op jit(solution)/shard_map/all_to_all | solution.py:344
  61.6 43.6 %collective-permute-start.5 = (bf16[1536,256]{1,0:T(8,128)(2,1)}, bf16[1536,256]{1,0:T(8,128)(2,1)S(1)}, u32[]{:S(2)}, u32[]{:S(2)}) collective-permute-start(bf16[1536,256]{1,0:T(8,128)(2,1)} %scatter2.1.after2_ref), channel_id=1, source_target_pairs={{0,4},{1,5},{2,6},{3,7},{4,0},{5,1},{6,2},{7,3},{8,12},{9,13},{10,... | collective-permute-start | bytes 2359304 | tf_op jit(solution)/shard_map/ppermute | solution.py:337
  65.1 40.1 %collective-permute-start.4 = (bf16[1536,256]{1,0:T(8,128)(2,1)}, bf16[1536,256]{1,0:T(8,128)(2,1)S(1)}, u32[]{:S(2)}, u32[]{:S(2)}) collective-permute-start(bf16[1536,256]{1,0:T(8,128)(2,1)} %scatter1.1.after1_ref), channel_id=1, source_target_pairs={{0,8},{1,9},{2,10},{3,11},{4,12},{5,13},{6,14},{7,15},{8,0},{9,1},... | collective-permute-start | bytes 2359304 | tf_op jit(solution)/shard_map/ppermute | solution.py:337
  68.3 41.2 %collective-permute-start.3 = (bf16[1536,256]{1,0:T(8,128)(2,1)}, bf16[1536,256]{1,0:T(8,128)(2,1)S(1)}, u32[]{:S(2)}, u32[]{:S(2)}) collective-permute-start(bf16[1536,256]{1,0:T(8,128)(2,1)} %scatter0.1.after0_ref), channel_id=1, source_target_pairs={{0,16},{1,17},{2,18},{3,19},{4,20},{5,21},{6,22},{7,23},{8,24},{9,... | collective-permute-start | bytes 2359304 | tf_op jit(solution)/shard_map/ppermute | solution.py:337
  70.8 4.3 %copy-start.9 = (bf16[768,256]{1,0:T(8,128)(2,1)S(1)}, bf16[768,256]{1,0:T(8,128)(2,1)}, u32[]{:S(2)}) copy-start(bf16[768,256]{1,0:T(8,128)(2,1)} %q_ref.5) | copy-start | bytes 1179652
  70.8 4.3 %copy-start.11 = (bf16[256,768]{1,0:T(8,128)(2,1)S(1)}, bf16[256,768]{1,0:T(8,128)(2,1)}, u32[]{:S(2)}) copy-start(bf16[256,768]{1,0:T(8,128)(2,1)} %copy-done.10) | copy-start | bytes 1179652
  71.5 40.0 %all-to-all-start.3 = ((f32[32,8,256]{2,1,0:T(8,128)}), f32[32,8,256]{2,1,0:T(8,128)}, u32[]{:S(2)}, u32[]{:S(2)}) async-start(f32[32,8,256]{2,1,0:T(8,128)} %broadcast_in_dim.2), calls=%async_computation.3 | async-start | bytes 524288 | tf_op jit(solution)/shard_map/all_to_all | solution.py:346
  77.7 1.1 copy-start.18
  105.2 4.3 %copy-start.1 = (bf16[1536,256]{1,0:T(8,128)(2,1)}, bf16[1536,256]{1,0:T(8,128)(2,1)S(1)}, u32[]{:S(2)}) copy-start(bf16[1536,256]{1,0:T(8,128)(2,1)S(1)} %collective-permute-done.5.refs_2_) | copy-start | bytes 2359300
  105.3 4.3 %copy-start.3 = (bf16[1536,256]{1,0:T(8,128)(2,1)}, bf16[1536,256]{1,0:T(8,128)(2,1)S(1)}, u32[]{:S(2)}) copy-start(bf16[1536,256]{1,0:T(8,128)(2,1)S(1)} %collective-permute-done.4.refs_1_) | copy-start | bytes 2359300
  111.5 19.0 %copy-start.2 = (bf16[1536,256]{1,0:T(8,128)(2,1)S(1)}, bf16[1536,256]{1,0:T(8,128)(2,1)}, u32[]{:S(2)}) copy-start(bf16[1536,256]{1,0:T(8,128)(2,1)} %copy-done.1) | copy-start | bytes 2359300
  111.5 19.0 %copy-start.4 = (bf16[1536,256]{1,0:T(8,128)(2,1)S(1)}, bf16[1536,256]{1,0:T(8,128)(2,1)}, u32[]{:S(2)}) copy-start(bf16[1536,256]{1,0:T(8,128)(2,1)} %copy-done.3) | copy-start | bytes 2359300
  111.5 19.0 %copy-start.6 = (bf16[1536,256]{1,0:T(8,128)(2,1)S(1)}, bf16[1536,256]{1,0:T(8,128)(2,1)}, u32[]{:S(2)}) copy-start(bf16[1536,256]{1,0:T(8,128)(2,1)} %copy-done.5) | copy-start | bytes 2359300
  111.5 19.0 %all-to-all-start.1 = ((bf16[8,256,256]{2,1,0:T(8,128)(2,1)}), bf16[8,256,256]{2,1,0:T(8,128)(2,1)S(1)}, u32[]{:S(2)}, u32[]{:S(2)}) async-start(bf16[8,256,256]{2,1,0:T(8,128)(2,1)} %after_terms.1), calls=%async_computation.1 | async-start | bytes 2097152 | tf_op jit(solution)/shard_map/all_to_all | solution.py:469
  131.2 1.1 copy-start.20
  132.3 1.1 copy-start.22
  (16 other events, 13.4 us)

commit v4 on v3

--- a/solution.py
+++ b/solution.py
@@ -17,7 +17,7 @@
 BF16 = jnp.bfloat16
 
 
-def params(mib=48):
+def params(mib):
     return pltpu.CompilerParams(vmem_limit_bytes=mib * 1024 * 1024)
 
 
@@ -144,10 +144,10 @@
 
 
 def merge_kernel(*refs, heads):
-    (bias_ref, ot_ref, m_ref, l_ref, gat_ref, gu_ref, w_ref) = refs[:7]
-    far = refs[7:19]
-    update_ref, term_ref, lse_ref, delta_ref, eq_ref = refs[19:24]
-    out = refs[24:]
+    (bias_ref, ot_ref, m_ref, l_ref, gat_ref, w_ref) = refs[:6]
+    far = refs[6:18]
+    update_ref, att_ref, lse_ref, delta_ref, eq_ref = refs[18:23]
+    out = refs[23:]
     feat = ot_ref.shape[0]
     width = feat // heads
     scale = width**-0.5
@@ -164,7 +164,7 @@
         mixed = mixed + spread(weights[e], width) * far[4 * e + 1][...].astype(F32)
     att = mixed.astype(BF16)
     update_ref[...] = dot(att, w_ref[...], 0, 0).astype(BF16)
-    term_ref[...] = dot(att, gu_ref[...])
+    att_ref[...] = att
     delta = head_sums(att.astype(F32) * gat_ref[...].astype(F32), heads)
     delta_ref[...] = delta
     lse_ref[...] = top * LOG2E + jnp.log2(total)
@@ -178,7 +178,11 @@
     eq_ref[...] = query
 
 
-def scatter_kernel(match_ref, qt_ref, gat_ref, ds_ref, wt_ref, placed_ref, *, heads):
+def weight_kernel(att_ref, gu_ref, after_ref, term_ref):
+    term_ref[...] = dot(att_ref[...], gu_ref[...])
+
+
+def scatter_kernel(match_ref, qt_ref, gat_ref, ds_ref, wt_ref, after_ref, placed_ref, *, heads):
     feat, nodes = qt_ref.shape
     width = feat // heads
     onehot = hot(match_ref[...], nodes)
@@ -320,7 +324,7 @@
     lax.fori_loop(0, home_ref.shape[0], body, 0)
 
 
-def call(kernel, name, ins, outs, args, scratch=(), estimate=None, **static):
+def call(kernel, name, ins, outs, args, scratch=(), estimate=None, mib=16, **static):
     return pl.pallas_call(
         functools.partial(kernel, **static),
         name=name,
@@ -328,7 +332,7 @@
         out_specs=[VMEM] * len(outs),
         out_shape=[jax.ShapeDtypeStruct(shape, dtype) for shape, dtype in outs],
         scratch_shapes=list(scratch),
-        compiler_params=params(),
+        compiler_params=params(mib),
         cost_estimate=estimate,
     )(*args)
 
@@ -394,6 +398,7 @@
             pltpu.VMEM((1, wide), F32),
         ],
         estimate=cost(tile_flops / 2, nodes * feat),
+        mib=16 + entries // 4,
         heads=heads, block=block,
     )
     rows = [matching[turn : turn + 1] for turn in range(3)]
@@ -407,28 +412,34 @@
             heads=heads,
         )
     merged = call(
-        merge_kernel, "merge", [VMEM] * 19,
+        merge_kernel, "merge", [VMEM] * 18,
         [
-            ((nodes, feat), BF16), ((feat, feat), F32), ((heads, nodes), F32),
+            ((nodes, feat), BF16), ((feat, nodes), BF16), ((heads, nodes), F32),
             ((heads, nodes), F32), ((feat, nodes), F32),
         ] + [((heads, nodes), F32)] * 6,
-        (expander_bias.reshape(heads, 1), ot, top, total, gat, grad_update, out_weight,
+        (expander_bias.reshape(heads, 1), ot, top, total, gat, out_weight,
          *far[0], *far[1], *far[2]),
         estimate=cost(4 * nodes * feat * feat, 24 * nodes * feat),
         heads=heads,
     )
-    update, weight_term, lse, delta, edge_query = merged[:5]
+    update, attended, lse, delta, edge_query = merged[:5]
     owned, ready = [], []
     for turn in range(3):
         (placed,) = call(
-            scatter_kernel, f"scatter{turn}", [VMEM] * 5,
+            scatter_kernel, f"scatter{turn}", [VMEM] * 5 + [ANY],
             [((2 * nodes, feat), BF16)],
-            (rows[turn], qt, gat, merged[5 + 2 * turn], merged[6 + 2 * turn]),
+            (rows[turn], qt, gat, merged[5 + 2 * turn], merged[6 + 2 * turn],
+             ready[-1] if ready else lse),
             estimate=cost(4 * nodes * nodes * feat, 10 * nodes * feat),
             heads=heads,
         )
         ready.append(placed)
         owned.append(from_partner(placed, axes, top_bit - 1 - turn))
+    (weight_term,) = call(
+        weight_kernel, "weight_term", [VMEM, VMEM, ANY], [((feat, feat), F32)],
+        (attended, grad_update, ready[-1]),
+        estimate=cost(2 * nodes * feat * feat, 4 * nodes * feat), mib=8,
+    )
     weight_grad = reduce_everywhere(weight_term, axes) * (nodes * devices) ** (-0.5)
     query_grad, own_k, own_v, back = call(
         bwd_kernel, "bwd_tiles", [SMEM, SMEM] + [VMEM] * 10 + [ANY] * 3,
@@ -455,6 +466,7 @@
             pltpu.VMEM((1, wide), F32),
         ],
         estimate=cost(tile_flops / 2, nodes * feat),
+        mib=22 + 3 * entries // 5,
         heads=heads, block=block,
     )
     back = pl.pallas_call(

time: 137 us -> 137 us (level)
  waiting for transfers between devices: 25.7 us -> 29.5 us
  Pallas kernels: 59.8 us -> 57.1 us
  local copies, waits for them, and re-layouts: 19.3 us -> 17.5 us
    all_to_all x1, waiting for transfers between devices: 0.01 us -> 4.84 us  [reduce_everywhere(): lax.all_to_all(parts, axes, split_axis=0, concat_axis=0, tiled=True)]
    ppermute x6, waiting for transfers between devices: 4.28 us -> 0.02 us  [from_partner(): lax.ppermute(array, axis, [(i, i ^ 1 << apart) for i in range(lax.axis_si...]
    pallas_call x12 -> x13, Pallas kernels: 59.8 us -> 57.1 us  [call(): pl.pallas_call(functools.partial(kernel, **static), name=name, in_specs=i...]
    all_to_all x1, waiting for transfers between devices: 1.1 us -> 2.93 us  [reduce_everywhere(): lax.all_to_all(copies, axes, split_axis=0, concat_axis=0, tiled=True)]
    all_to_all x1, waiting for transfers between devices: 6.67 us -> 8.06 us  [shards(): got = lax.all_to_all(sent, 'dom', split_axis=0, concat_axis=0, tiled=True)]
    unnamed x78 -> x66, local copies, waits for them, and re-layouts: 17.9 us -> 16.6 us
  transfers between devices with their start and end apart: 10 -> 10, of which waited for: 4 -> 4; matrix products, arithmetic and copies ran while one was open for 2% -> 3% of each run, Pallas kernels for 38% -> 33%
where the time goes in v4:
time: 137 us; the launch traced here: 136 us
  Pallas kernels  57.1 us (42%)
  waiting for transfers between devices  29.5 us (22%)
  starting transfers between devices  28.6 us (21%)
  local copies, waits for them, and re-layouts  17.5 us (13%)
  other arithmetic  2.66 us (2%)
    pallas_call x13, Pallas kernels, call(): pl.pallas_call(functools.partial(kernel, **static), name=name, in_specs=i...  57.1 us
    unnamed x66, local copies, waits for them, and re-layouts  16.6 us
    all_to_all x1, waiting for transfers between devices, shards(): home = lax.all_to_all(back, 'dom', split_axis=0, concat_axis=0, tiled=True)  13.7 us
    ppermute x6, starting transfers between devices, from_partner(): lax.ppermute(array, axis, [(i, i ^ 1 << apart) for i in range(lax.axis_si...  11.9 us
    all_to_all x1, waiting for transfers between devices, shards(): got = lax.all_to_all(sent, 'dom', split_axis=0, concat_axis=0, tiled=True)  8.06 us
    all_to_all x1, starting transfers between devices, shards(): got = lax.all_to_all(sent, 'dom', split_axis=0, concat_axis=0, tiled=True)  5.31 us
    all_to_all x1, waiting for transfers between devices, reduce_everywhere(): lax.all_to_all(parts, axes, split_axis=0, concat_axis=0, tiled=True)  4.84 us
    all_to_all x1, starting transfers between devices, reduce_everywhere(): lax.all_to_all(parts, axes, split_axis=0, concat_axis=0, tiled=True)  4.1 us
  transfers between devices with their start and end apart: 10, of which 4 were waited for; matrix products, arithmetic and copies ran while one was open for 3% of the time, Pallas kernels for 33%

profile of v4, /device:TPU:0, one launch (start us, length us, event | category | flops | bytes accessed | tf_op | source)
XLA Modules:
  0.0 136.2 jit_solution(7580622747840869851)
XLA Ops:
  0.6 1.1 constant_dynamic-update-slice_fusion.1
  2.4 1.6 %pick.1 = bf16[8,256,256]{2,1,0:T(8,128)(2,1)} custom-call(s32[8]{0:T(128)S(1)} %bitcast.18, bf16[1536,256]{1,0:T(8,128)(2,1)S(1)} %constant_dynamic-update-slice_fusion.both_ref), custom_call_target="tpu_custom_call" | custom-call | bytes 2097152 | tf_op jit(solution)/shard_map/pick/pallas_call | solution.py:328
  4.1 5.3 %all-to-all-start = ((bf16[8,256,256]{2,1,0:T(8,128)(2,1)}), bf16[8,256,256]{2,1,0:T(8,128)(2,1)S(1)}, u32[]{:S(2)}, u32[]{:S(2)}) async-start(bf16[8,256,256]{2,1,0:T(8,128)(2,1)} %pick.1), calls=%async_computation | async-start | bytes 2097152 | tf_op jit(solution)/shard_map/all_to_all | solution.py:380
  9.4 2.0 %collective-permute-start.2 = (bf16[1536,256]{1,0:T(8,128)(2,1)S(1)}, bf16[1536,256]{1,0:T(8,128)(2,1)}, u32[]{:S(2)}, u32[]{:S(2)}) collective-permute-start(bf16[1536,256]{1,0:T(8,128)(2,1)S(1)} %constant_dynamic-update-slice_fusion.both_ref), channel_id=1, source_target_pairs={{0,4},{1,5},{2,6},{3,7},{4,0},{5,1},{6,2},{7,3},{8,12},{9,13},{10,... | collective-permute-start | bytes 2359304 | tf_op jit(solution)/shard_map/ppermute | solution.py:341
  11.4 1.6 %collective-permute-start.1 = (bf16[1536,256]{1,0:T(8,128)(2,1)S(1)}, bf16[1536,256]{1,0:T(8,128)(2,1)}, u32[]{:S(2)}, u32[]{:S(2)}) collective-permute-start(bf16[1536,256]{1,0:T(8,128)(2,1)S(1)} %constant_dynamic-update-slice_fusion.both_ref), channel_id=1, source_target_pairs={{0,8},{1,9},{2,10},{3,11},{4,12},{5,13},{6,14},{7,15},{8,0},{9,1},... | collective-permute-start | bytes 2359304 | tf_op jit(solution)/shard_map/ppermute | solution.py:341
  13.0 2.6 %collective-permute-start = (bf16[1536,256]{1,0:T(8,128)(2,1)S(1)}, bf16[1536,256]{1,0:T(8,128)(2,1)}, u32[]{:S(2)}, u32[]{:S(2)}) collective-permute-start(bf16[1536,256]{1,0:T(8,128)(2,1)S(1)} %constant_dynamic-update-slice_fusion.both_ref), channel_id=1, source_target_pairs={{0,16},{1,17},{2,18},{3,19},{4,20},{5,21},{6,22},{7,23},{8,24},{9,... | collective-permute-start | bytes 2359304 | tf_op jit(solution)/shard_map/ppermute | solution.py:341
  16.9 8.1 %all-to-all-done.got_ref = bf16[8,256,256]{2,1,0:T(8,128)(2,1)S(1)} async-done(((bf16[8,256,256]{2,1,0:T(8,128)(2,1)}), bf16[8,256,256]{2,1,0:T(8,128)(2,1)S(1)}, u32[]{:S(2)}, u32[]{:S(2)}) %all-to-all-start) | async-done | bytes 1048608 | tf_op jit(solution)/shard_map/all_to_all | solution.py:380
  25.6 1.0 copy-done.7
  26.6 1.0 copy-done.10
  27.6 19.2 %fwd_tiles.1 = (f32[256,768]{1,0:T(8,128)S(1)}, f32[8,768]{1,0:T(8,128)S(1)}, f32[8,768]{1,0:T(8,128)S(1)}) custom-call(s32[6,8]{1,0:T(8,128)S(1)} %bitcast.16, s32[6]{0:T(128)S(1)} %bitcast.20, bf16[768,256]{1,0:T(8,128)(2,1)S(1)} %copy-done.5, bf16[768,256]{1,0:T(8,128)(2,1)S(1)} %copy-done.7, bf16[768,256]{1,0:T(8,128)(2,1)S(1)} %copy-done.10, ...), custom_call_target="tpu_custom_call" | custom-call | flops 1610612736 | bytes 196608 | tf_op jit(solution)/shard_map/fwd_tiles/pallas_call | solution.py:328
  46.8 2.1 %gather2.1 = (bf16[256,768]{1,0:T(8,128)(2,1)S(1)}, bf16[256,768]{1,0:T(8,128)(2,1)S(1)}, f32[8,768]{1,0:T(8,128)S(1)}, f32[8,768]{1,0:T(8,128)S(1)}) custom-call(s32[1,768]{1,0:T(1,128)S(1)} %get-tuple-element.75.match_ref, bf16[1536,256]{1,0:T(8,128)(2,1)} %collective-permute-done.2.moved_ref, bf16[256,768]{1,0:T(8,128)(2,1)S(1)} %get-tuple-element.44.qt_ref, ...), custom_call_target="tpu_custom_call" | custom-call | flops 603979776 | bytes 2359296 | tf_op jit(solution)/shard_map/gather2/pallas_call | solution.py:328
  49.0 2.1 %gather1.1 = (bf16[256,768]{1,0:T(8,128)(2,1)S(1)}, bf16[256,768]{1,0:T(8,128)(2,1)S(1)}, f32[8,768]{1,0:T(8,128)S(1)}, f32[8,768]{1,0:T(8,128)S(1)}) custom-call(s32[1,768]{1,0:T(1,128)S(1)} %get-tuple-element.77.match_ref, bf16[1536,256]{1,0:T(8,128)(2,1)} %collective-permute-done.1.moved_ref, bf16[256,768]{1,0:T(8,128)(2,1)S(1)} %get-tuple-element.44.qt_ref, ...), custom_call_target="tpu_custom_call" | custom-call | flops 603979776 | bytes 2359296 | tf_op jit(solution)/shard_map/gather1/pallas_call | solution.py:328
  51.1 2.1 %gather0.1 = (bf16[256,768]{1,0:T(8,128)(2,1)S(1)}, bf16[256,768]{1,0:T(8,128)(2,1)S(1)}, f32[8,768]{1,0:T(8,128)S(1)}, f32[8,768]{1,0:T(8,128)S(1)}) custom-call(s32[1,768]{1,0:T(1,128)S(1)} %get-tuple-element.76.match_ref, bf16[1536,256]{1,0:T(8,128)(2,1)} %collective-permute-done.moved_ref, bf16[256,768]{1,0:T(8,128)(2,1)S(1)} %get-tuple-element.44.qt_ref, ...), custom_call_target="tpu_custom_call" | custom-call | flops 603979776 | bytes 2359296 | tf_op jit(solution)/shard_map/gather0/pallas_call | solution.py:328
  53.3 1.9 %merge.1 = (bf16[768,256]{1,0:T(8,128)(2,1)}, bf16[256,768]{1,0:T(8,128)(2,1)S(1)}, f32[8,768]{1,0:T(8,128)S(1)}, f32[8,768]{1,0:T(8,128)S(1)}, f32[256,768]{1,0...) custom-call(f32[8,1]{1,0:T(8,128)S(1)} %copy.16.refs_0_, ...), custom_call_target="tpu_custom_call" | custom-call | flops 201326592 | bytes 4718592 | tf_op jit(solution)/shard_map/merge/pallas_call | solution.py:328
  59.7 4.1 %all-to-all-start.2 = ((f32[32,8,256]{2,1,0:T(8,128)}), f32[32,8,256]{2,1,0:T(8,128)}, u32[]{:S(2)}, u32[]{:S(2)}) async-start(f32[32,8,256]{2,1,0:T(8,128)} %bitcast.15), calls=%async_computation.2 | async-start | bytes 524288 | tf_op jit(solution)/shard_map/all_to_all | solution.py:348
  63.8 1.8 %collective-permute-start.5 = (bf16[1536,256]{1,0:T(8,128)(2,1)S(1)}, bf16[1536,256]{1,0:T(8,128)(2,1)}, u32[]{:S(2)}, u32[]{:S(2)}) collective-permute-start(bf16[1536,256]{1,0:T(8,128)(2,1)S(1)} %scatter2.1.after2_ref.after_ref), channel_id=1, source_target_pairs={{0,4},{1,5},{2,6},{3,7},{4,0},{5,1},{6,2},{7,3},{8,12},{9,13},{10,... | collective-permute-start | bytes 2359304 | tf_op jit(solution)/shard_map/ppermute | solution.py:341
  65.6 1.5 %collective-permute-start.4 = (bf16[1536,256]{1,0:T(8,128)(2,1)S(1)}, bf16[1536,256]{1,0:T(8,128)(2,1)}, u32[]{:S(2)}, u32[]{:S(2)}) collective-permute-start(bf16[1536,256]{1,0:T(8,128)(2,1)S(1)} %scatter1.1.after_ref.after1_ref), channel_id=1, source_target_pairs={{0,8},{1,9},{2,10},{3,11},{4,12},{5,13},{6,14},{7,15},{8,0},{9,1},... | collective-permute-start | bytes 2359304 | tf_op jit(solution)/shard_map/ppermute | solution.py:341
  67.1 2.4 %collective-permute-start.3 = (bf16[1536,256]{1,0:T(8,128)(2,1)}, bf16[1536,256]{1,0:T(8,128)(2,1)}, u32[]{:S(2)}, u32[]{:S(2)}) collective-permute-start(bf16[1536,256]{1,0:T(8,128)(2,1)} %copy-done.1), channel_id=1, source_target_pairs={{0,16},{1,17},{2,18},{3,19},{4,20},{5,21},{6,22},{7,23},{8,24},{9,... | collective-permute-start | bytes 2359304 | tf_op jit(solution)/shard_map/ppermute | solution.py:341
  69.5 4.8 %all-to-all-done.2 = f32[32,8,256]{2,1,0:T(8,128)} async-done(((f32[32,8,256]{2,1,0:T(8,128)}), f32[32,8,256]{2,1,0:T(8,128)}, u32[]{:S(2)}, u32[]{:S(2)}) %all-to-all-start.2) | async-done | bytes 262176 | tf_op jit(solution)/shard_map/all_to_all | solution.py:348
  76.1 3.6 %all-to-all-start.3 = ((f32[32,8,256]{2,1,0:T(8,128)}), f32[32,8,256]{2,1,0:T(8,128)}, u32[]{:S(2)}, u32[]{:S(2)}) async-start(f32[32,8,256]{2,1,0:T(8,128)} %broadcast_in_dim.2), calls=%async_computation.3 | async-start | bytes 524288 | tf_op jit(solution)/shard_map/all_to_all | solution.py:350
  80.4 1.1 copy-done.2
  81.5 1.0 copy-done.6
  82.5 1.0 copy-done.8
  83.5 1.0 copy-done.11
  84.5 1.1 copy-done.14
  86.6 21.6 %bwd_tiles.1 = (f32[768,256]{1,0:T(8,128)}, f32[768,256]{1,0:T(8,128)S(1)}, f32[768,256]{1,0:T(8,128)S(1)}, bf16[8,256,256]{2,1,0:T(8,128)(2,1)S(1)}) custom-call(s32[6,8]{1,0:T(8,128)S(1)} %bitcast.17, s32[6]{0:T(128)S(1)} %bitcast.21, bf16[768,256]{1,0:T(8,128)(2,1)S(1)} %copy-done.6, bf16[768,256]{1,0:T(8,128)(2,1)S(1)} %copy-done.8, ...), custom_call_target="tpu_custom_call" | custom-call | flops 1610612736 | bytes 196608 | tf_op jit(solution)/shard_map/bwd_tiles/pallas_call | solution.py:328
  108.2 1.0 copy-done
  111.0 2.9 %all-to-all-done.3 = f32[32,8,256]{2,1,0:T(8,128)} async-done(((f32[32,8,256]{2,1,0:T(8,128)}), f32[32,8,256]{2,1,0:T(8,128)}, u32[]{:S(2)}, u32[]{:S(2)}) %all-to-all-start.3) | async-done | bytes 262176 | tf_op jit(solution)/shard_map/all_to_all | solution.py:350
  113.9 3.7 %all-to-all-start.1 = ((bf16[8,256,256]{2,1,0:T(8,128)(2,1)}), bf16[8,256,256]{2,1,0:T(8,128)(2,1)S(1)}, u32[]{:S(2)}, u32[]{:S(2)}) async-start(bf16[8,256,256]{2,1,0:T(8,128)(2,1)} %after_terms.1), calls=%async_computation.1 | async-start | bytes 2097152 | tf_op jit(solution)/shard_map/all_to_all | solution.py:481
  117.6 1.7 %multiply_bitcast_fusion = f32[256,256]{1,0:T(8,128)} fusion(f32[32,8,256]{2,1,0:T(8,128)} %all-to-all-done.3), kind=kLoop, calls=%fused_computation | loop fusion | flops 65536 | bytes 524288 | tf_op jit(solution)/shard_map/mul | solution.py:443
  119.3 13.7 %all-to-all-done.1.home_ref = bf16[8,256,256]{2,1,0:T(8,128)(2,1)S(1)} async-done(((bf16[8,256,256]{2,1,0:T(8,128)(2,1)}), bf16[8,256,256]{2,1,0:T(8,128)(2,1)S(1)}, u32[]{:S(2)}, u32[]{:S(2)}) %all-to-all-start.1) | async-done | bytes 1048608 | tf_op jit(solution)/shard_map/all_to_all | solution.py:481
  133.0 3.3 %final.1 = (f32[768,256]{1,0:T(8,128)}, f32[768,256]{1,0:T(8,128)}) custom-call(s32[8]{0:T(128)S(1)} %bitcast.19, f32[768,256]{1,0:T(8,128)S(1)} %copy-done.16, f32[768,256]{1,0:T(8,128)S(1)} %copy-done.18, bf16[8,256,256]{2,1,0:T(8,128)(2,1)S(1)} %all-to-all-done.1.home_ref, bf16[1536,256]{1,0:T(8,128)(2,1)} %collective-permute-done.3.refs_0_, ...), custom_call_target="tpu_custom_call" | custom-call | bytes 7864320 | tf_op jit(solution)/shard_map/final/pallas_call | solution.py:328
  (74 shorter events, 12.3 us)
Async XLA Ops:
  0.6 1.1 copy-start.9
  4.1 11.5 %copy-start.31 = (f32[8]{0:T(128)S(1)}, f32[8]{0:T(128)}, u32[]{:S(2)}) copy-start(f32[8]{0:T(128)} %param.15) | copy-start | bytes 100
  4.1 11.6 %copy-start.3 = (bf16[768,256]{1,0:T(8,128)(2,1)S(1)}, bf16[768,256]{1,0:T(8,128)(2,1)}, u32[]{:S(2)}) copy-start(bf16[768,256]{1,0:T(8,128)(2,1)} %gu_ref.3) | copy-start | bytes 1179652
  4.1 11.6 %copy-start.5 = (bf16[768,256]{1,0:T(8,128)(2,1)S(1)}, bf16[768,256]{1,0:T(8,128)(2,1)}, u32[]{:S(2)}) copy-start(bf16[768,256]{1,0:T(8,128)(2,1)} %q_ref.5) | copy-start | bytes 1179652
  4.1 11.6 %copy-start.19 = (bf16[256,256]{1,0:T(8,128)(2,1)S(1)}, bf16[256,256]{1,0:T(8,128)(2,1)}, u32[]{:S(2)}) copy-start(bf16[256,256]{1,0:T(8,128)(2,1)} %refs_5_.1) | copy-start | bytes 393220
  4.1 20.8 %all-to-all-start = ((bf16[8,256,256]{2,1,0:T(8,128)(2,1)}), bf16[8,256,256]{2,1,0:T(8,128)(2,1)S(1)}, u32[]{:S(2)}, u32[]{:S(2)}) async-start(bf16[8,256,256]{2,1,0:T(8,128)(2,1)} %pick.1), calls=%async_computation | async-start | bytes 2097152 | tf_op jit(solution)/shard_map/all_to_all | solution.py:380
  9.4 6.3 %copy-start.30 = (s32[1,6,8]{2,0,1:T(1,128)S(1)}, s32[1,6,8]{2,0,1:T(1,128)}, u32[]{:S(2)}) copy-start(s32[1,6,8]{2,0,1:T(1,128)} %param.16) | copy-start | bytes 580
  9.4 37.4 %collective-permute-start.2 = (bf16[1536,256]{1,0:T(8,128)(2,1)S(1)}, bf16[1536,256]{1,0:T(8,128)(2,1)}, u32[]{:S(2)}, u32[]{:S(2)}) collective-permute-start(bf16[1536,256]{1,0:T(8,128)(2,1)S(1)} %constant_dynamic-update-slice_fusion.both_ref), channel_id=1, source_target_pairs={{0,4},{1,5},{2,6},{3,7},{4,0},{5,1},{6,2},{7,3},{8,12},{9,13},{10,... | collective-permute-start | bytes 2359304 | tf_op jit(solution)/shard_map/ppermute | solution.py:341
  11.4 37.5 %collective-permute-start.1 = (bf16[1536,256]{1,0:T(8,128)(2,1)S(1)}, bf16[1536,256]{1,0:T(8,128)(2,1)}, u32[]{:S(2)}, u32[]{:S(2)}) collective-permute-start(bf16[1536,256]{1,0:T(8,128)(2,1)S(1)} %constant_dynamic-update-slice_fusion.both_ref), channel_id=1, source_target_pairs={{0,8},{1,9},{2,10},{3,11},{4,12},{5,13},{6,14},{7,15},{8,0},{9,1},... | collective-permute-start | bytes 2359304 | tf_op jit(solution)/shard_map/ppermute | solution.py:341
  13.0 38.1 %collective-permute-start = (bf16[1536,256]{1,0:T(8,128)(2,1)S(1)}, bf16[1536,256]{1,0:T(8,128)(2,1)}, u32[]{:S(2)}, u32[]{:S(2)}) collective-permute-start(bf16[1536,256]{1,0:T(8,128)(2,1)S(1)} %constant_dynamic-update-slice_fusion.both_ref), channel_id=1, source_target_pairs={{0,16},{1,17},{2,18},{3,19},{4,20},{5,21},{6,22},{7,23},{8,24},{9,... | collective-permute-start | bytes 2359304 | tf_op jit(solution)/shard_map/ppermute | solution.py:341
  15.7 1.2 copy-start.29
  25.6 1.0 copy-start.7
  26.6 1.0 copy-start.10
  57.8 1.0 copy-start.4
  59.7 14.6 %all-to-all-start.2 = ((f32[32,8,256]{2,1,0:T(8,128)}), f32[32,8,256]{2,1,0:T(8,128)}, u32[]{:S(2)}, u32[]{:S(2)}) async-start(f32[32,8,256]{2,1,0:T(8,128)} %bitcast.15), calls=%async_computation.2 | async-start | bytes 524288 | tf_op jit(solution)/shard_map/all_to_all | solution.py:348
  63.8 47.1 %collective-permute-start.5 = (bf16[1536,256]{1,0:T(8,128)(2,1)S(1)}, bf16[1536,256]{1,0:T(8,128)(2,1)}, u32[]{:S(2)}, u32[]{:S(2)}) collective-permute-start(bf16[1536,256]{1,0:T(8,128)(2,1)S(1)} %scatter2.1.after2_ref.after_ref), channel_id=1, source_target_pairs={{0,4},{1,5},{2,6},{3,7},{4,0},{5,1},{6,2},{7,3},{8,12},{9,13},{10,... | collective-permute-start | bytes 2359304 | tf_op jit(solution)/shard_map/ppermute | solution.py:341
  65.6 45.4 %collective-permute-start.4 = (bf16[1536,256]{1,0:T(8,128)(2,1)S(1)}, bf16[1536,256]{1,0:T(8,128)(2,1)}, u32[]{:S(2)}, u32[]{:S(2)}) collective-permute-start(bf16[1536,256]{1,0:T(8,128)(2,1)S(1)} %scatter1.1.after_ref.after1_ref), channel_id=1, source_target_pairs={{0,8},{1,9},{2,10},{3,11},{4,12},{5,13},{6,14},{7,15},{8,0},{9,1},... | collective-permute-start | bytes 2359304 | tf_op jit(solution)/shard_map/ppermute | solution.py:341
  67.1 43.9 %collective-permute-start.3 = (bf16[1536,256]{1,0:T(8,128)(2,1)}, bf16[1536,256]{1,0:T(8,128)(2,1)}, u32[]{:S(2)}, u32[]{:S(2)}) collective-permute-start(bf16[1536,256]{1,0:T(8,128)(2,1)} %copy-done.1), channel_id=1, source_target_pairs={{0,16},{1,17},{2,18},{3,19},{4,20},{5,21},{6,22},{7,23},{8,24},{9,... | collective-permute-start | bytes 2359304 | tf_op jit(solution)/shard_map/ppermute | solution.py:341
  76.1 3.6 %copy-start.23 = (f32[8,768]{1,0:T(8,128)S(1)}, f32[8,768]{1,0:T(8,128)}, u32[]{:S(2)}) copy-start(f32[8,768]{1,0:T(8,128)} %copy-done.22) | copy-start | bytes 73732
  76.1 3.7 %copy-start.25 = (f32[8,768]{1,0:T(8,128)S(1)}, f32[8,768]{1,0:T(8,128)}, u32[]{:S(2)}) copy-start(f32[8,768]{1,0:T(8,128)} %copy-done.24) | copy-start | bytes 73732
  76.1 37.8 %all-to-all-start.3 = ((f32[32,8,256]{2,1,0:T(8,128)}), f32[32,8,256]{2,1,0:T(8,128)}, u32[]{:S(2)}, u32[]{:S(2)}) async-start(f32[32,8,256]{2,1,0:T(8,128)} %broadcast_in_dim.2), calls=%async_computation.3 | async-start | bytes 524288 | tf_op jit(solution)/shard_map/all_to_all | solution.py:350
  80.4 1.1 copy-start.2
  81.5 1.0 copy-start.6
  82.5 1.0 copy-start.8
  83.5 1.0 copy-start.11
  84.5 1.1 copy-start.14
  85.6 1.0 copy-start.21
  108.2 1.0 copy-start
  110.1 0.9 copy-start.17
  113.9 19.0 %copy-start.16 = (f32[768,256]{1,0:T(8,128)S(1)}, f32[768,256]{1,0:T(8,128)}, u32[]{:S(2)}) copy-start(f32[768,256]{1,0:T(8,128)} %copy-done.15) | copy-start | bytes 2359300
  113.9 19.0 %copy-start.18 = (f32[768,256]{1,0:T(8,128)S(1)}, f32[768,256]{1,0:T(8,128)}, u32[]{:S(2)}) copy-start(f32[768,256]{1,0:T(8,128)} %copy-done.17) | copy-start | bytes 2359300
  113.9 19.0 %all-to-all-start.1 = ((bf16[8,256,256]{2,1,0:T(8,128)(2,1)}), bf16[8,256,256]{2,1,0:T(8,128)(2,1)S(1)}, u32[]{:S(2)}, u32[]{:S(2)}) async-start(bf16[8,256,256]{2,1,0:T(8,128)(2,1)} %after_terms.1), calls=%async_computation.1 | async-start | bytes 2097152 | tf_op jit(solution)/shard_map/all_to_all | solution.py:481
  (10 other events, 7.7 us)

commit v5 on v3

--- a/solution.py
+++ b/solution.py
@@ -17,7 +17,7 @@
 BF16 = jnp.bfloat16
 
 
-def params(mib=48):
+def params(mib):
     return pltpu.CompilerParams(vmem_limit_bytes=mib * 1024 * 1024)
 
 
@@ -178,7 +178,7 @@
     eq_ref[...] = query
 
 
-def scatter_kernel(match_ref, qt_ref, gat_ref, ds_ref, wt_ref, placed_ref, *, heads):
+def scatter_kernel(match_ref, qt_ref, gat_ref, ds_ref, wt_ref, after_ref, placed_ref, *, heads):
     feat, nodes = qt_ref.shape
     width = feat // heads
     onehot = hot(match_ref[...], nodes)
@@ -320,15 +320,34 @@
     lax.fori_loop(0, home_ref.shape[0], body, 0)
 
 
-def call(kernel, name, ins, outs, args, scratch=(), estimate=None, **static):
+def origin(dims, step):
+    return (0,) * dims
+
+
+def call(kernel, name, ins, outs, args, scratch=(), estimate=None, mib=16, whole=False, **static):
+    if whole:
+        ins = [
+            pl.BlockSpec(
+                arg.shape, functools.partial(origin, arg.ndim), pipeline_mode=pl.Buffered(1)
+            )
+            if spec is VMEM
+            else spec
+            for spec, arg in zip(ins, args)
+        ]
+        out_specs = [
+            pl.BlockSpec(shape, functools.partial(origin, len(shape))) for shape, _ in outs
+        ]
+    else:
+        out_specs = [VMEM] * len(outs)
     return pl.pallas_call(
         functools.partial(kernel, **static),
         name=name,
+        grid=(1,) if whole else (),
         in_specs=ins,
-        out_specs=[VMEM] * len(outs),
+        out_specs=out_specs,
         out_shape=[jax.ShapeDtypeStruct(shape, dtype) for shape, dtype in outs],
         scratch_shapes=list(scratch),
-        compiler_params=params(),
+        compiler_params=params(mib),
         cost_estimate=estimate,
     )(*args)
 
@@ -394,6 +413,7 @@
             pltpu.VMEM((1, wide), F32),
         ],
         estimate=cost(tile_flops / 2, nodes * feat),
+        mib=20 + entries // 2, whole=True,
         heads=heads, block=block,
     )
     rows = [matching[turn : turn + 1] for turn in range(3)]
@@ -421,9 +441,10 @@
     owned, ready = [], []
     for turn in range(3):
         (placed,) = call(
-            scatter_kernel, f"scatter{turn}", [VMEM] * 5,
+            scatter_kernel, f"scatter{turn}", [VMEM] * 5 + [ANY],
             [((2 * nodes, feat), BF16)],
-            (rows[turn], qt, gat, merged[5 + 2 * turn], merged[6 + 2 * turn]),
+            (rows[turn], qt, gat, merged[5 + 2 * turn], merged[6 + 2 * turn],
+             ready[-1] if ready else lse),
             estimate=cost(4 * nodes * nodes * feat, 10 * nodes * feat),
             heads=heads,
         )
@@ -455,6 +476,7 @@
             pltpu.VMEM((1, wide), F32),
         ],
         estimate=cost(tile_flops / 2, nodes * feat),
+        mib=30 + 2 * entries // 3, whole=True,
         heads=heads, block=block,
     )
     back = pl.pallas_call(
@@ -472,7 +494,7 @@
         [((nodes, feat), F32), ((nodes, feat), F32)],
         (send_block, own_k, own_v, home, *owned),
         estimate=cost(0, 40 * nodes * feat),
-        block=block,
+        mib=24 + entries // 2, whole=True, block=block,
     )
     return update, query_grad, key_grad, value_grad, weight_grad
 

time: 137 us -> 139 us (1.015)
  Pallas kernels: 59.8 us -> 57.8 us
  local copies, waits for them, and re-layouts: 19.3 us -> 21.2 us
    pallas_call x12, Pallas kernels: 59.8 us -> 57.8 us  [call(): pl.pallas_call(functools.partial(kernel, **static), name=name, grid=(1,)...]
    unnamed x78, local copies, waits for them, and re-layouts: 17.9 us -> 19.8 us
  transfers between devices with their start and end apart: 10 -> 10, of which waited for: 4 -> 4; matrix products, arithmetic and copies ran while one was open for 2% -> 3% of each run, Pallas kernels for 38% -> 36%
where the time goes in v5:
time: 139 us; the launch traced here: 137 us
  Pallas kernels  57.8 us (42%)
  starting transfers between devices  28.4 us (20%)
  waiting for transfers between devices  26.3 us (19%)
  local copies, waits for them, and re-layouts  21.2 us (15%)
  other arithmetic  2.66 us (2%)
    pallas_call x12, Pallas kernels, call(): pl.pallas_call(functools.partial(kernel, **static), name=name, grid=(1,)...  57.8 us
    unnamed x78, local copies, waits for them, and re-layouts  19.8 us
    all_to_all x1, waiting for transfers between devices, shards(): home = lax.all_to_all(back, 'dom', split_axis=0, concat_axis=0, tiled=True)  13.7 us
    ppermute x6, starting transfers between devices, from_partner(): lax.ppermute(array, axis, [(i, i ^ 1 << apart) for i in range(lax.axis_si...  11.8 us
    all_to_all x1, waiting for transfers between devices, shards(): got = lax.all_to_all(sent, 'dom', split_axis=0, concat_axis=0, tiled=True)  7.44 us
    all_to_all x1, starting transfers between devices, shards(): got = lax.all_to_all(sent, 'dom', split_axis=0, concat_axis=0, tiled=True)  5.31 us
    all_to_all x1, starting transfers between devices, reduce_everywhere(): lax.all_to_all(parts, axes, split_axis=0, concat_axis=0, tiled=True)  4.1 us
    all_to_all x1, starting transfers between devices, shards(): home = lax.all_to_all(back, 'dom', split_axis=0, concat_axis=0, tiled=True)  3.69 us
  transfers between devices with their start and end apart: 10, of which 4 were waited for; matrix products, arithmetic and copies ran while one was open for 3% of the time, Pallas kernels for 36%

profile of v5, /device:TPU:0, one launch (start us, length us, event | category | flops | bytes accessed | tf_op | source)
XLA Modules:
  0.0 137.3 jit_solution(2591332156777045857)
XLA Ops:
  0.6 1.1 constant_dynamic-update-slice_fusion.1
  2.4 1.7 %pick.1 = bf16[8,256,256]{2,1,0:T(8,128)(2,1)} custom-call(s32[8]{0:T(128)S(1)} %bitcast.17, bf16[1536,256]{1,0:T(8,128)(2,1)S(1)} %constant_dynamic-update-slice_fusion.both_ref), custom_call_target="tpu_custom_call" | custom-call | bytes 2097152 | tf_op jit(solution)/shard_map/pick/pallas_call | solution.py:342
  4.1 5.3 %all-to-all-start = ((bf16[8,256,256]{2,1,0:T(8,128)(2,1)}), bf16[8,256,256]{2,1,0:T(8,128)(2,1)S(1)}, u32[]{:S(2)}, u32[]{:S(2)}) async-start(bf16[8,256,256]{2,1,0:T(8,128)(2,1)} %pick.1), calls=%async_computation | async-start | bytes 2097152 | tf_op jit(solution)/shard_map/all_to_all | solution.py:395
  9.4 2.0 %collective-permute-start.2 = (bf16[1536,256]{1,0:T(8,128)(2,1)S(1)}, bf16[1536,256]{1,0:T(8,128)(2,1)}, u32[]{:S(2)}, u32[]{:S(2)}) collective-permute-start(bf16[1536,256]{1,0:T(8,128)(2,1)S(1)} %constant_dynamic-update-slice_fusion.both_ref), channel_id=1, source_target_pairs={{0,4},{1,5},{2,6},{3,7},{4,0},{5,1},{6,2},{7,3},{8,12},{9,13},{10,... | collective-permute-start | bytes 2359304 | tf_op jit(solution)/shard_map/ppermute | solution.py:356
  11.5 1.6 %collective-permute-start.1 = (bf16[1536,256]{1,0:T(8,128)(2,1)S(1)}, bf16[1536,256]{1,0:T(8,128)(2,1)}, u32[]{:S(2)}, u32[]{:S(2)}) collective-permute-start(bf16[1536,256]{1,0:T(8,128)(2,1)S(1)} %constant_dynamic-update-slice_fusion.both_ref), channel_id=1, source_target_pairs={{0,8},{1,9},{2,10},{3,11},{4,12},{5,13},{6,14},{7,15},{8,0},{9,1},... | collective-permute-start | bytes 2359304 | tf_op jit(solution)/shard_map/ppermute | solution.py:356
  13.0 2.6 %collective-permute-start = (bf16[1536,256]{1,0:T(8,128)(2,1)S(1)}, bf16[1536,256]{1,0:T(8,128)(2,1)}, u32[]{:S(2)}, u32[]{:S(2)}) collective-permute-start(bf16[1536,256]{1,0:T(8,128)(2,1)S(1)} %constant_dynamic-update-slice_fusion.both_ref), channel_id=1, source_target_pairs={{0,16},{1,17},{2,18},{3,19},{4,20},{5,21},{6,22},{7,23},{8,24},{9,... | collective-permute-start | bytes 2359304 | tf_op jit(solution)/shard_map/ppermute | solution.py:356
  17.5 7.4 %all-to-all-done.got_ref = bf16[8,256,256]{2,1,0:T(8,128)(2,1)S(1)} async-done(((bf16[8,256,256]{2,1,0:T(8,128)(2,1)}), bf16[8,256,256]{2,1,0:T(8,128)(2,1)S(1)}, u32[]{:S(2)}, u32[]{:S(2)}) %all-to-all-start) | async-done | bytes 1048608 | tf_op jit(solution)/shard_map/all_to_all | solution.py:395
  25.6 1.0 copy-done.4
  26.6 1.0 copy-done.7
  27.6 19.2 %fwd_tiles.1 = (f32[256,768]{1,0:T(8,128)S(1)}, f32[8,768]{1,0:T(8,128)S(1)}, f32[8,768]{1,0:T(8,128)S(1)}) custom-call(s32[6,8]{1,0:T(8,128)S(1)} %bitcast.15, s32[6]{0:T(128)S(1)} %bitcast.19, bf16[768,256]{1,0:T(8,128)(2,1)S(1)} %copy-done.2, bf16[768,256]{1,0:T(8,128)(2,1)S(1)} %copy-done.4, bf16[768,256]{1,0:T(8,128)(2,1)S(1)} %copy-done.7, ...), custom_call_target="tpu_custom_call" | custom-call | flops 1610612736 | bytes 196608 | tf_op jit(solution)/shard_map/fwd_tiles/pallas_call | solution.py:342
  46.9 2.1 %gather2.1 = (bf16[256,768]{1,0:T(8,128)(2,1)S(1)}, bf16[256,768]{1,0:T(8,128)(2,1)S(1)}, f32[8,768]{1,0:T(8,128)S(1)}, f32[8,768]{1,0:T(8,128)S(1)}) custom-call(s32[1,768]{1,0:T(1,128)S(1)} %get-tuple-element.75.match_ref, bf16[1536,256]{1,0:T(8,128)(2,1)} %collective-permute-done.2.moved_ref, bf16[256,768]{1,0:T(8,128)(2,1)S(1)} %get-tuple-element.44.qt_ref, ...), custom_call_target="tpu_custom_call" | custom-call | flops 603979776 | bytes 2359296 | tf_op jit(solution)/shard_map/gather2/pallas_call | solution.py:342
  49.0 2.1 %gather1.1 = (bf16[256,768]{1,0:T(8,128)(2,1)S(1)}, bf16[256,768]{1,0:T(8,128)(2,1)S(1)}, f32[8,768]{1,0:T(8,128)S(1)}, f32[8,768]{1,0:T(8,128)S(1)}) custom-call(s32[1,768]{1,0:T(1,128)S(1)} %get-tuple-element.77.match_ref, bf16[1536,256]{1,0:T(8,128)(2,1)} %collective-permute-done.1.moved_ref, bf16[256,768]{1,0:T(8,128)(2,1)S(1)} %get-tuple-element.44.qt_ref, ...), custom_call_target="tpu_custom_call" | custom-call | flops 603979776 | bytes 2359296 | tf_op jit(solution)/shard_map/gather1/pallas_call | solution.py:342
  51.2 2.1 %gather0.1 = (bf16[256,768]{1,0:T(8,128)(2,1)S(1)}, bf16[256,768]{1,0:T(8,128)(2,1)S(1)}, f32[8,768]{1,0:T(8,128)S(1)}, f32[8,768]{1,0:T(8,128)S(1)}) custom-call(s32[1,768]{1,0:T(1,128)S(1)} %get-tuple-element.76.match_ref, bf16[1536,256]{1,0:T(8,128)(2,1)} %collective-permute-done.moved_ref, bf16[256,768]{1,0:T(8,128)(2,1)S(1)} %get-tuple-element.44.qt_ref, ...), custom_call_target="tpu_custom_call" | custom-call | flops 603979776 | bytes 2359296 | tf_op jit(solution)/shard_map/gather0/pallas_call | solution.py:342
  54.0 2.0 %merge.1 = (bf16[768,256]{1,0:T(8,128)(2,1)}, f32[256,256]{1,0:T(8,128)}, f32[8,768]{1,0:T(8,128)S(1)}, f32[8,768]{1,0:T(8,128)S(1)}, f32[256,768]{1,0:T(8,128)S...) custom-call(f32[8,1]{1,0:T(8,128)S(1)} %copy-done.20, ...), custom_call_target="tpu_custom_call" | custom-call | flops 201326592 | bytes 4718592 | tf_op jit(solution)/shard_map/merge/pallas_call | solution.py:342
  57.2 4.1 %all-to-all-start.2 = ((f32[32,8,256]{2,1,0:T(8,128)}), f32[32,8,256]{2,1,0:T(8,128)}, u32[]{:S(2)}, u32[]{:S(2)}) async-start(f32[32,8,256]{2,1,0:T(8,128)} %bitcast.6), calls=%async_computation.2 | async-start | bytes 524288 | tf_op jit(solution)/shard_map/all_to_all | solution.py:363
  66.5 1.7 %scatter2.1.after2_ref = bf16[1536,256]{1,0:T(8,128)(2,1)} custom-call(s32[1,768]{1,0:T(1,128)S(1)} %copy-done.22, bf16[256,768]{1,0:T(8,128)(2,1)S(1)} %get-tuple-element.44.qt_ref, bf16[256,768]{1,0:T(8,128)(2,1)S(1)} %get-tuple-element.43.gat_ref.refs_4_, f32[8,768]{1,0:T(8,128)S(1)} %get-tuple-element.66.ds_ref, f32[8,768]{1,0:T(8,128)S(1)} %get-tuple-element.67.wt_ref, ...), custom_call_target="tpu_custom_call" | custom-call | flops 603979776 | bytes 1966080 | tf_op jit(solution)/shard_map/scatter2/pallas_call | solution.py:342
  68.2 1.7 %collective-permute-start.5 = (bf16[1536,256]{1,0:T(8,128)(2,1)}, bf16[1536,256]{1,0:T(8,128)(2,1)}, u32[]{:S(2)}, u32[]{:S(2)}) collective-permute-start(bf16[1536,256]{1,0:T(8,128)(2,1)} %scatter2.1.after2_ref), channel_id=1, source_target_pairs={{0,4},{1,5},{2,6},{3,7},{4,0},{5,1},{6,2},{7,3},{8,12},{9,13},{10,... | collective-permute-start | bytes 2359304 | tf_op jit(solution)/shard_map/ppermute | solution.py:356
  69.9 1.5 %collective-permute-start.4 = (bf16[1536,256]{1,0:T(8,128)(2,1)S(1)}, bf16[1536,256]{1,0:T(8,128)(2,1)}, u32[]{:S(2)}, u32[]{:S(2)}) collective-permute-start(bf16[1536,256]{1,0:T(8,128)(2,1)S(1)} %scatter1.1.after_ref.after1_ref), channel_id=1, source_target_pairs={{0,8},{1,9},{2,10},{3,11},{4,12},{5,13},{6,14},{7,15},{8,0},{9,1},... | collective-permute-start | bytes 2359304 | tf_op jit(solution)/shard_map/ppermute | solution.py:356
  71.4 2.5 %collective-permute-start.3 = (bf16[1536,256]{1,0:T(8,128)(2,1)S(1)}, bf16[1536,256]{1,0:T(8,128)(2,1)}, u32[]{:S(2)}, u32[]{:S(2)}) collective-permute-start(bf16[1536,256]{1,0:T(8,128)(2,1)S(1)} %scatter0.1.after_ref.after0_ref), channel_id=1, source_target_pairs={{0,16},{1,17},{2,18},{3,19},{4,20},{5,21},{6,22},{7,23},{8,24},{9,... | collective-permute-start | bytes 2359304 | tf_op jit(solution)/shard_map/ppermute | solution.py:356
  75.5 3.5 %all-to-all-start.3 = ((f32[32,8,256]{2,1,0:T(8,128)}), f32[32,8,256]{2,1,0:T(8,128)}, u32[]{:S(2)}, u32[]{:S(2)}) async-start(f32[32,8,256]{2,1,0:T(8,128)} %broadcast_in_dim.2), calls=%async_computation.3 | async-start | bytes 524288 | tf_op jit(solution)/shard_map/all_to_all | solution.py:365
  79.7 1.0 copy-done.3
  81.7 1.0 copy-done.8
  82.7 1.1 copy-done.10
  83.8 1.0 copy-done.17
  84.8 21.6 %bwd_tiles.1 = (f32[768,256]{1,0:T(8,128)}, f32[768,256]{1,0:T(8,128)S(1)}, f32[768,256]{1,0:T(8,128)S(1)}, bf16[8,256,256]{2,1,0:T(8,128)(2,1)S(1)}) custom-call(s32[6,8]{1,0:T(8,128)S(1)} %bitcast.16, s32[6]{0:T(128)S(1)} %bitcast.20, bf16[768,256]{1,0:T(8,128)(2,1)S(1)} %copy-done.3, bf16[768,256]{1,0:T(8,128)(2,1)S(1)} %copy-done.5, ...), custom_call_target="tpu_custom_call" | custom-call | flops 1610612736 | bytes 196608 | tf_op jit(solution)/shard_map/bwd_tiles/pallas_call | solution.py:342
  106.4 1.0 copy-done
  109.2 3.3 %collective-permute-done.3.refs_0_ = bf16[1536,256]{1,0:T(8,128)(2,1)} collective-permute-done((bf16[1536,256]{1,0:T(8,128)(2,1)S(1)}, bf16[1536,256]{1,0:T(8,128)(2,1)}, u32[]{:S(2)}, u32[]{:S(2)}) %collective-permute-start.3) | collective-permute-done | bytes 786464 | tf_op jit(solution)/shard_map/ppermute | solution.py:356
  112.5 1.9 %all-to-all-done.3 = f32[32,8,256]{2,1,0:T(8,128)} async-done(((f32[32,8,256]{2,1,0:T(8,128)}), f32[32,8,256]{2,1,0:T(8,128)}, u32[]{:S(2)}, u32[]{:S(2)}) %all-to-all-start.3) | async-done | bytes 262176 | tf_op jit(solution)/shard_map/all_to_all | solution.py:365
  114.4 3.7 %all-to-all-start.1 = ((bf16[8,256,256]{2,1,0:T(8,128)(2,1)}), bf16[8,256,256]{2,1,0:T(8,128)(2,1)S(1)}, u32[]{:S(2)}, u32[]{:S(2)}) async-start(bf16[8,256,256]{2,1,0:T(8,128)(2,1)} %after_terms.1), calls=%async_computation.1 | async-start | bytes 2097152 | tf_op jit(solution)/shard_map/all_to_all | solution.py:491
  118.1 1.7 %multiply_bitcast_fusion = f32[256,256]{1,0:T(8,128)} fusion(f32[32,8,256]{2,1,0:T(8,128)} %all-to-all-done.3), kind=kLoop, calls=%fused_computation | loop fusion | flops 65536 | bytes 524288 | tf_op jit(solution)/shard_map/mul | solution.py:453
  119.8 13.7 %all-to-all-done.1.home_ref = bf16[8,256,256]{2,1,0:T(8,128)(2,1)S(1)} async-done(((bf16[8,256,256]{2,1,0:T(8,128)(2,1)}), bf16[8,256,256]{2,1,0:T(8,128)(2,1)S(1)}, u32[]{:S(2)}, u32[]{:S(2)}) %all-to-all-start.1) | async-done | bytes 1048608 | tf_op jit(solution)/shard_map/all_to_all | solution.py:491
  134.1 3.3 %final.1 = (f32[768,256]{1,0:T(8,128)}, f32[768,256]{1,0:T(8,128)}) custom-call(s32[8]{0:T(128)S(1)} %bitcast.18, f32[768,256]{1,0:T(8,128)S(1)} %copy-done.12, f32[768,256]{1,0:T(8,128)S(1)} %copy-done.14, bf16[8,256,256]{2,1,0:T(8,128)(2,1)S(1)} %all-to-all-done.1.home_ref, bf16[1536,256]{1,0:T(8,128)(2,1)} %collective-permute-done.3.refs_0_, ...), custom_call_target="tpu_custom_call" | custom-call | bytes 7864320 | tf_op jit(solution)/shard_map/final/pallas_call | solution.py:342
  (85 shorter events, 16.0 us)
Async XLA Ops:
  0.6 1.1 copy-start.6
  4.1 11.5 %copy-start.37 = (f32[8]{0:T(128)S(1)}, f32[8]{0:T(128)}, u32[]{:S(2)}) copy-start(f32[8]{0:T(128)} %param.15) | copy-start | bytes 100
  4.1 12.2 %copy-start.1 = (bf16[768,256]{1,0:T(8,128)(2,1)S(1)}, bf16[768,256]{1,0:T(8,128)(2,1)}, u32[]{:S(2)}) copy-start(bf16[768,256]{1,0:T(8,128)(2,1)} %refs_5_.1) | copy-start | bytes 1179652
  4.1 12.2 %copy-start.2 = (bf16[768,256]{1,0:T(8,128)(2,1)S(1)}, bf16[768,256]{1,0:T(8,128)(2,1)}, u32[]{:S(2)}) copy-start(bf16[768,256]{1,0:T(8,128)(2,1)} %q_ref.5) | copy-start | bytes 1179652
  4.1 12.2 %copy-start.15 = (bf16[256,256]{1,0:T(8,128)(2,1)S(1)}, bf16[256,256]{1,0:T(8,128)(2,1)}, u32[]{:S(2)}) copy-start(bf16[256,256]{1,0:T(8,128)(2,1)} %refs_6_.1) | copy-start | bytes 393220
  4.1 20.8 %all-to-all-start = ((bf16[8,256,256]{2,1,0:T(8,128)(2,1)}), bf16[8,256,256]{2,1,0:T(8,128)(2,1)S(1)}, u32[]{:S(2)}, u32[]{:S(2)}) async-start(bf16[8,256,256]{2,1,0:T(8,128)(2,1)} %pick.1), calls=%async_computation | async-start | bytes 2097152 | tf_op jit(solution)/shard_map/all_to_all | solution.py:395
  9.4 6.9 %copy-start.36 = (s32[1,6,8]{2,0,1:T(1,128)S(1)}, s32[1,6,8]{2,0,1:T(1,128)}, u32[]{:S(2)}) copy-start(s32[1,6,8]{2,0,1:T(1,128)} %param.16) | copy-start | bytes 580
  9.4 37.4 %collective-permute-start.2 = (bf16[1536,256]{1,0:T(8,128)(2,1)S(1)}, bf16[1536,256]{1,0:T(8,128)(2,1)}, u32[]{:S(2)}, u32[]{:S(2)}) collective-permute-start(bf16[1536,256]{1,0:T(8,128)(2,1)S(1)} %constant_dynamic-update-slice_fusion.both_ref), channel_id=1, source_target_pairs={{0,4},{1,5},{2,6},{3,7},{4,0},{5,1},{6,2},{7,3},{8,12},{9,13},{10,... | collective-permute-start | bytes 2359304 | tf_op jit(solution)/shard_map/ppermute | solution.py:356
  11.5 37.5 %collective-permute-start.1 = (bf16[1536,256]{1,0:T(8,128)(2,1)S(1)}, bf16[1536,256]{1,0:T(8,128)(2,1)}, u32[]{:S(2)}, u32[]{:S(2)}) collective-permute-start(bf16[1536,256]{1,0:T(8,128)(2,1)S(1)} %constant_dynamic-update-slice_fusion.both_ref), channel_id=1, source_target_pairs={{0,8},{1,9},{2,10},{3,11},{4,12},{5,13},{6,14},{7,15},{8,0},{9,1},... | collective-permute-start | bytes 2359304 | tf_op jit(solution)/shard_map/ppermute | solution.py:356
  13.0 38.1 %collective-permute-start = (bf16[1536,256]{1,0:T(8,128)(2,1)S(1)}, bf16[1536,256]{1,0:T(8,128)(2,1)}, u32[]{:S(2)}, u32[]{:S(2)}) collective-permute-start(bf16[1536,256]{1,0:T(8,128)(2,1)S(1)} %constant_dynamic-update-slice_fusion.both_ref), channel_id=1, source_target_pairs={{0,16},{1,17},{2,18},{3,19},{4,20},{5,21},{6,22},{7,23},{8,24},{9,... | collective-permute-start | bytes 2359304 | tf_op jit(solution)/shard_map/ppermute | solution.py:356
  16.3 8.6 %copy-start.18 = (s32[1,6,8]{2,1,0:T(8,128)}, s32[1,6,8]{2,1,0:T(8,128)S(1)}, u32[]{:S(2)}) copy-start(s32[1,6,8]{2,1,0:T(8,128)S(1)} %copy.19) | copy-start | bytes 580
  16.3 1.2 copy-start.35
  17.5 29.4 %copy-start.21 = (s32[1,768]{1,0:T(1,128)}, s32[1,768]{1,0:T(1,128)S(1)}, u32[]{:S(2)}) copy-start(s32[1,768]{1,0:T(1,128)S(1)} %get-tuple-element.75.match_ref) | copy-start | bytes 9220
  17.5 31.5 %copy-start.23 = (s32[1,768]{1,0:T(1,128)}, s32[1,768]{1,0:T(1,128)S(1)}, u32[]{:S(2)}) copy-start(s32[1,768]{1,0:T(1,128)S(1)} %get-tuple-element.77.match_ref) | copy-start | bytes 9220
  17.5 33.7 %copy-start.25 = (s32[1,768]{1,0:T(1,128)}, s32[1,768]{1,0:T(1,128)S(1)}, u32[]{:S(2)}) copy-start(s32[1,768]{1,0:T(1,128)S(1)} %get-tuple-element.76.match_ref) | copy-start | bytes 9220
  25.6 1.0 copy-start.4
  26.6 1.0 copy-start.7
  57.2 7.1 %copy-start.9 = (f32[256,768]{1,0:T(8,128)}, f32[256,768]{1,0:T(8,128)S(1)}, u32[]{:S(2)}) copy-start(f32[256,768]{1,0:T(8,128)S(1)} %get-tuple-element.61.eq_ref) | copy-start | bytes 2359300
  57.2 16.6 %all-to-all-start.2 = ((f32[32,8,256]{2,1,0:T(8,128)}), f32[32,8,256]{2,1,0:T(8,128)}, u32[]{:S(2)}, u32[]{:S(2)}) async-start(f32[32,8,256]{2,1,0:T(8,128)} %bitcast.6), calls=%async_computation.2 | async-start | bytes 524288 | tf_op jit(solution)/shard_map/all_to_all | solution.py:363
  68.2 41.0 %collective-permute-start.5 = (bf16[1536,256]{1,0:T(8,128)(2,1)}, bf16[1536,256]{1,0:T(8,128)(2,1)}, u32[]{:S(2)}, u32[]{:S(2)}) collective-permute-start(bf16[1536,256]{1,0:T(8,128)(2,1)} %scatter2.1.after2_ref), channel_id=1, source_target_pairs={{0,4},{1,5},{2,6},{3,7},{4,0},{5,1},{6,2},{7,3},{8,12},{9,13},{10,... | collective-permute-start | bytes 2359304 | tf_op jit(solution)/shard_map/ppermute | solution.py:356
  69.9 39.3 %collective-permute-start.4 = (bf16[1536,256]{1,0:T(8,128)(2,1)S(1)}, bf16[1536,256]{1,0:T(8,128)(2,1)}, u32[]{:S(2)}, u32[]{:S(2)}) collective-permute-start(bf16[1536,256]{1,0:T(8,128)(2,1)S(1)} %scatter1.1.after_ref.after1_ref), channel_id=1, source_target_pairs={{0,8},{1,9},{2,10},{3,11},{4,12},{5,13},{6,14},{7,15},{8,0},{9,1},... | collective-permute-start | bytes 2359304 | tf_op jit(solution)/shard_map/ppermute | solution.py:356
  71.4 41.1 %collective-permute-start.3 = (bf16[1536,256]{1,0:T(8,128)(2,1)S(1)}, bf16[1536,256]{1,0:T(8,128)(2,1)}, u32[]{:S(2)}, u32[]{:S(2)}) collective-permute-start(bf16[1536,256]{1,0:T(8,128)(2,1)S(1)} %scatter0.1.after_ref.after0_ref), channel_id=1, source_target_pairs={{0,16},{1,17},{2,18},{3,19},{4,20},{5,21},{6,22},{7,23},{8,24},{9,... | collective-permute-start | bytes 2359304 | tf_op jit(solution)/shard_map/ppermute | solution.py:356
  75.5 38.9 %all-to-all-start.3 = ((f32[32,8,256]{2,1,0:T(8,128)}), f32[32,8,256]{2,1,0:T(8,128)}, u32[]{:S(2)}, u32[]{:S(2)}) async-start(f32[32,8,256]{2,1,0:T(8,128)} %broadcast_in_dim.2), calls=%async_computation.3 | async-start | bytes 524288 | tf_op jit(solution)/shard_map/all_to_all | solution.py:365
  79.7 1.0 copy-start.3
  80.7 1.0 copy-start.5
  81.7 1.0 copy-start.8
  82.7 1.1 copy-start.10
  83.8 1.0 copy-start.17
  106.4 1.0 copy-start
  114.4 19.0 %copy-start.12 = (f32[768,256]{1,0:T(8,128)S(1)}, f32[768,256]{1,0:T(8,128)}, u32[]{:S(2)}) copy-start(f32[768,256]{1,0:T(8,128)} %copy-done.11) | copy-start | bytes 2359300
  114.4 19.0 %copy-start.14 = (f32[768,256]{1,0:T(8,128)S(1)}, f32[768,256]{1,0:T(8,128)}, u32[]{:S(2)}) copy-start(f32[768,256]{1,0:T(8,128)} %copy-done.13) | copy-start | bytes 2359300
  114.4 19.0 %all-to-all-start.1 = ((bf16[8,256,256]{2,1,0:T(8,128)(2,1)}), bf16[8,256,256]{2,1,0:T(8,128)(2,1)S(1)}, u32[]{:S(2)}, u32[]{:S(2)}) async-start(bf16[8,256,256]{2,1,0:T(8,128)(2,1)} %after_terms.1), calls=%async_computation.1 | async-start | bytes 2097152 | tf_op jit(solution)/shard_map/all_to_all | solution.py:491
  (16 other events, 11.2 us)

commit v6 on v5

--- a/solution.py
+++ b/solution.py
@@ -178,7 +178,7 @@
     eq_ref[...] = query
 
 
-def scatter_kernel(match_ref, qt_ref, gat_ref, ds_ref, wt_ref, after_ref, placed_ref, *, heads):
+def scatter_kernel(match_ref, qt_ref, gat_ref, ds_ref, wt_ref, placed_ref, *, heads):
     feat, nodes = qt_ref.shape
     width = feat // heads
     onehot = hot(match_ref[...], nodes)
@@ -324,7 +324,7 @@
     return (0,) * dims
 
 
-def call(kernel, name, ins, outs, args, scratch=(), estimate=None, mib=16, whole=False, **static):
+def call(kernel, name, ins, outs, args, scratch=(), estimate=None, mib=48, whole=False, **static):
     if whole:
         ins = [
             pl.BlockSpec(
@@ -413,7 +413,7 @@
             pltpu.VMEM((1, wide), F32),
         ],
         estimate=cost(tile_flops / 2, nodes * feat),
-        mib=20 + entries // 2, whole=True,
+        mib=60, whole=True,
         heads=heads, block=block,
     )
     rows = [matching[turn : turn + 1] for turn in range(3)]
@@ -441,10 +441,9 @@
     owned, ready = [], []
     for turn in range(3):
         (placed,) = call(
-            scatter_kernel, f"scatter{turn}", [VMEM] * 5 + [ANY],
+            scatter_kernel, f"scatter{turn}", [VMEM] * 5,
             [((2 * nodes, feat), BF16)],
-            (rows[turn], qt, gat, merged[5 + 2 * turn], merged[6 + 2 * turn],
-             ready[-1] if ready else lse),
+            (rows[turn], qt, gat, merged[5 + 2 * turn], merged[6 + 2 * turn]),
             estimate=cost(4 * nodes * nodes * feat, 10 * nodes * feat),
             heads=heads,
         )
@@ -476,7 +475,7 @@
             pltpu.VMEM((1, wide), F32),
         ],
         estimate=cost(tile_flops / 2, nodes * feat),
-        mib=30 + 2 * entries // 3, whole=True,
+        mib=60, whole=True,
         heads=heads, block=block,
     )
     back = pl.pallas_call(
@@ -494,7 +493,7 @@
         [((nodes, feat), F32), ((nodes, feat), F32)],
         (send_block, own_k, own_v, home, *owned),
         estimate=cost(0, 40 * nodes * feat),
-        mib=24 + entries // 2, whole=True, block=block,
+        mib=60, whole=True, block=block,
     )
     return update, query_grad, key_grad, value_grad, weight_grad
 

time: 139 us -> 137 us (0.986)
  local copies, waits for them, and re-layouts: 21.2 us -> 8.98 us
  waiting for transfers between devices: 26.3 us -> 34.1 us
  Pallas kernels: 57.8 us -> 62.4 us
    unnamed x78 -> x46, local copies, waits for them, and re-layouts: 19.8 us -> 8.15 us
    pallas_call x12, Pallas kernels: 57.8 us -> 62.4 us  [call(): pl.pallas_call(functools.partial(kernel, **static), name=name, grid=(1,)...]
    ppermute x6, waiting for transfers between devices: 3.32 us -> 7.6 us  [from_partner(): lax.ppermute(array, axis, [(i, i ^ 1 << apart) for i in range(lax.axis_si...]
    all_to_all x1, waiting for transfers between devices: 0.01 us -> 2.17 us  [reduce_everywhere(): lax.all_to_all(parts, axes, split_axis=0, concat_axis=0, tiled=True)]
  transfers between devices with their start and end apart: 10 -> 10, of which waited for: 4 -> 6; matrix products, arithmetic and copies ran while one was open for 3% -> 2% of each run, Pallas kernels for 36% -> 38%
where the time goes in v6:
time: 137 us
  Pallas kernels  62.4 us (46%)
  waiting for transfers between devices  34.1 us (25%)
  starting transfers between devices  28.6 us (21%)
  local copies, waits for them, and re-layouts  8.98 us (7%)
  other arithmetic  1.72 us (1%)
    pallas_call x12, Pallas kernels, call(): pl.pallas_call(functools.partial(kernel, **static), name=name, grid=(1,)...  62.4 us
    all_to_all x1, waiting for transfers between devices, shards(): home = lax.all_to_all(back, 'dom', split_axis=0, concat_axis=0, tiled=True)  14.6 us
    ppermute x6, starting transfers between devices, from_partner(): lax.ppermute(array, axis, [(i, i ^ 1 << apart) for i in range(lax.axis_si...  12.4 us
    unnamed x46, local copies, waits for them, and re-layouts  8.15 us
    all_to_all x1, waiting for transfers between devices, shards(): got = lax.all_to_all(sent, 'dom', split_axis=0, concat_axis=0, tiled=True)  7.62 us
    ppermute x6, waiting for transfers between devices, from_partner(): lax.ppermute(array, axis, [(i, i ^ 1 << apart) for i in range(lax.axis_si...  7.6 us
    all_to_all x1, starting transfers between devices, shards(): got = lax.all_to_all(sent, 'dom', split_axis=0, concat_axis=0, tiled=True)  5.31 us
    all_to_all x1, starting transfers between devices, reduce_everywhere(): lax.all_to_all(parts, axes, split_axis=0, concat_axis=0, tiled=True)  4.51 us
  transfers between devices with their start and end apart: 10, of which 6 were waited for; matrix products, arithmetic and copies ran while one was open for 2% of the time, Pallas kernels for 38%

profile of v6, /device:TPU:0, one launch (start us, length us, event | category | flops | bytes accessed | tf_op | source)
XLA Modules:
  0.0 136.7 jit_solution(154578472229731889)
XLA Ops:
  0.6 1.1 constant_dynamic-update-slice_fusion.1
  2.4 1.6 %pick.1 = bf16[8,256,256]{2,1,0:T(8,128)(2,1)} custom-call(s32[8]{0:T(128)S(1)} %bitcast.16, bf16[1536,256]{1,0:T(8,128)(2,1)S(1)} %constant_dynamic-update-slice_fusion.both_ref), custom_call_target="tpu_custom_call" | custom-call | bytes 2097152 | tf_op jit(solution)/shard_map/pick/pallas_call | solution.py:342
  4.1 5.3 %all-to-all-start = ((bf16[8,256,256]{2,1,0:T(8,128)(2,1)}), bf16[8,256,256]{2,1,0:T(8,128)(2,1)}, u32[]{:S(2)}, u32[]{:S(2)}) async-start(bf16[8,256,256]{2,1,0:T(8,128)(2,1)} %pick.1), calls=%async_computation | async-start | bytes 2097152 | tf_op jit(solution)/shard_map/all_to_all | solution.py:395
  9.4 2.1 %collective-permute-start.2 = (bf16[1536,256]{1,0:T(8,128)(2,1)S(1)}, bf16[1536,256]{1,0:T(8,128)(2,1)}, u32[]{:S(2)}, u32[]{:S(2)}) collective-permute-start(bf16[1536,256]{1,0:T(8,128)(2,1)S(1)} %constant_dynamic-update-slice_fusion.both_ref), channel_id=1, source_target_pairs={{0,4},{1,5},{2,6},{3,7},{4,0},{5,1},{6,2},{7,3},{8,12},{9,13},{10,... | collective-permute-start | bytes 2359304 | tf_op jit(solution)/shard_map/ppermute | solution.py:356
  11.5 1.9 %collective-permute-start.1 = (bf16[1536,256]{1,0:T(8,128)(2,1)S(1)}, bf16[1536,256]{1,0:T(8,128)(2,1)}, u32[]{:S(2)}, u32[]{:S(2)}) collective-permute-start(bf16[1536,256]{1,0:T(8,128)(2,1)S(1)} %constant_dynamic-update-slice_fusion.both_ref), channel_id=1, source_target_pairs={{0,8},{1,9},{2,10},{3,11},{4,12},{5,13},{6,14},{7,15},{8,0},{9,1},... | collective-permute-start | bytes 2359304 | tf_op jit(solution)/shard_map/ppermute | solution.py:356
  13.4 2.6 %collective-permute-start = (bf16[1536,256]{1,0:T(8,128)(2,1)S(1)}, bf16[1536,256]{1,0:T(8,128)(2,1)}, u32[]{:S(2)}, u32[]{:S(2)}) collective-permute-start(bf16[1536,256]{1,0:T(8,128)(2,1)S(1)} %constant_dynamic-update-slice_fusion.both_ref), channel_id=1, source_target_pairs={{0,16},{1,17},{2,18},{3,19},{4,20},{5,21},{6,22},{7,23},{8,24},{9,... | collective-permute-start | bytes 2359304 | tf_op jit(solution)/shard_map/ppermute | solution.py:356
  17.4 7.6 %all-to-all-done.got_ref = bf16[8,256,256]{2,1,0:T(8,128)(2,1)} async-done(((bf16[8,256,256]{2,1,0:T(8,128)(2,1)}), bf16[8,256,256]{2,1,0:T(8,128)(2,1)}, u32[]{:S(2)}, u32[]{:S(2)}) %all-to-all-start) | async-done | bytes 1048608 | tf_op jit(solution)/shard_map/all_to_all | solution.py:395
  25.0 21.1 %fwd_tiles.1 = (f32[256,768]{1,0:T(8,128)}, f32[8,768]{1,0:T(8,128)}, f32[8,768]{1,0:T(8,128)}) custom-call(s32[6,8]{1,0:T(8,128)} %bitcast.17, s32[6]{0:T(128)} %bitcast.19, bf16[768,256]{1,0:T(8,128)(2,1)} %q_ref.5, bf16[768,256]{1,0:T(8,128)(2,1)} %k_ref.3, bf16[768,256]{1,0:T(8,128)(2,1)} %v_ref.3, bf16[8,256,256]{2,1,0:T(8,128)(2,1)} %all-to-all-done.got_ref), custom_call_target="tpu_custom_call" | custom-call | flops 1610612736 | bytes 196608 | tf_op jit(solution)/shard_map/fwd_tiles/pallas_call | solution.py:342
  46.9 2.1 %gather2.1 = (bf16[256,768]{1,0:T(8,128)(2,1)S(1)}, bf16[256,768]{1,0:T(8,128)(2,1)S(1)}, f32[8,768]{1,0:T(8,128)S(1)}, f32[8,768]{1,0:T(8,128)S(1)}) custom-call(s32[1,768]{1,0:T(1,128)S(1)} %get-tuple-element.75.match_ref, bf16[1536,256]{1,0:T(8,128)(2,1)} %collective-permute-done.2.moved_ref, bf16[256,768]{1,0:T(8,128)(2,1)S(1)} %get-tuple-element.44.qt_ref, ...), custom_call_target="tpu_custom_call" | custom-call | flops 603979776 | bytes 2359296 | tf_op jit(solution)/shard_map/gather2/pallas_call | solution.py:342
  49.0 2.1 %gather1.1 = (bf16[256,768]{1,0:T(8,128)(2,1)S(1)}, bf16[256,768]{1,0:T(8,128)(2,1)S(1)}, f32[8,768]{1,0:T(8,128)S(1)}, f32[8,768]{1,0:T(8,128)S(1)}) custom-call(s32[1,768]{1,0:T(1,128)S(1)} %get-tuple-element.77.match_ref, bf16[1536,256]{1,0:T(8,128)(2,1)} %collective-permute-done.1.moved_ref, bf16[256,768]{1,0:T(8,128)(2,1)S(1)} %get-tuple-element.44.qt_ref, ...), custom_call_target="tpu_custom_call" | custom-call | flops 603979776 | bytes 2359296 | tf_op jit(solution)/shard_map/gather1/pallas_call | solution.py:342
  51.2 2.2 %gather0.1 = (bf16[256,768]{1,0:T(8,128)(2,1)S(1)}, bf16[256,768]{1,0:T(8,128)(2,1)S(1)}, f32[8,768]{1,0:T(8,128)S(1)}, f32[8,768]{1,0:T(8,128)S(1)}) custom-call(s32[1,768]{1,0:T(1,128)S(1)} %get-tuple-element.76.match_ref, bf16[1536,256]{1,0:T(8,128)(2,1)} %collective-permute-done.moved_ref, bf16[256,768]{1,0:T(8,128)(2,1)S(1)} %get-tuple-element.44.qt_ref, ...), custom_call_target="tpu_custom_call" | custom-call | flops 603979776 | bytes 2359296 | tf_op jit(solution)/shard_map/gather0/pallas_call | solution.py:342
  54.1 2.0 %merge.1 = (bf16[768,256]{1,0:T(8,128)(2,1)}, f32[256,256]{1,0:T(8,128)}, f32[8,768]{1,0:T(8,128)S(1)}, f32[8,768]{1,0:T(8,128)S(1)}, f32[256,768]{1,0:T(8,128)S...) custom-call(f32[8,1]{1,0:T(8,128)S(1)} %copy.16.refs_0_, ...), custom_call_target="tpu_custom_call" | custom-call | flops 201326592 | bytes 4718592 | tf_op jit(solution)/shard_map/merge/pallas_call | solution.py:342
  56.2 0.9 copy-done.3
  58.3 4.5 %all-to-all-start.2 = ((f32[32,8,256]{2,1,0:T(8,128)}), f32[32,8,256]{2,1,0:T(8,128)}, u32[]{:S(2)}, u32[]{:S(2)}) async-start(f32[32,8,256]{2,1,0:T(8,128)} %bitcast.6), calls=%async_computation.2 | async-start | bytes 524288 | tf_op jit(solution)/shard_map/all_to_all | solution.py:363
  62.8 0.8 scatter2.1.after2_ref
  63.6 1.8 %collective-permute-start.5 = (bf16[1536,256]{1,0:T(8,128)(2,1)S(1)}, bf16[1536,256]{1,0:T(8,128)(2,1)}, u32[]{:S(2)}, u32[]{:S(2)}) collective-permute-start(bf16[1536,256]{1,0:T(8,128)(2,1)S(1)} %scatter2.1.after2_ref), channel_id=1, source_target_pairs={{0,4},{1,5},{2,6},{3,7},{4,0},{5,1},{6,2},{7,3},{8,12},{9,13},{10,... | collective-permute-start | bytes 2359304 | tf_op jit(solution)/shard_map/ppermute | solution.py:356
  65.4 0.8 scatter1.1.after1_ref
  66.2 1.5 %collective-permute-start.4 = (bf16[1536,256]{1,0:T(8,128)(2,1)S(1)}, bf16[1536,256]{1,0:T(8,128)(2,1)}, u32[]{:S(2)}, u32[]{:S(2)}) collective-permute-start(bf16[1536,256]{1,0:T(8,128)(2,1)S(1)} %scatter1.1.after1_ref), channel_id=1, source_target_pairs={{0,8},{1,9},{2,10},{3,11},{4,12},{5,13},{6,14},{7,15},{8,0},{9,1},... | collective-permute-start | bytes 2359304 | tf_op jit(solution)/shard_map/ppermute | solution.py:356
  67.8 0.8 scatter0.1.after0_ref
  68.6 2.5 %collective-permute-start.3 = (bf16[1536,256]{1,0:T(8,128)(2,1)S(1)}, bf16[1536,256]{1,0:T(8,128)(2,1)S(1)}, u32[]{:S(2)}, u32[]{:S(2)}) collective-permute-start(bf16[1536,256]{1,0:T(8,128)(2,1)S(1)} %scatter0.1.after0_ref), channel_id=1, source_target_pairs={{0,16},{1,17},{2,18},{3,19},{4,20},{5,21},{6,22},{7,23},{8,24},{9,... | collective-permute-start | bytes 2359304 | tf_op jit(solution)/shard_map/ppermute | solution.py:356
  71.1 2.2 %all-to-all-done.2 = f32[32,8,256]{2,1,0:T(8,128)} async-done(((f32[32,8,256]{2,1,0:T(8,128)}), f32[32,8,256]{2,1,0:T(8,128)}, u32[]{:S(2)}, u32[]{:S(2)}) %all-to-all-start.2) | async-done | bytes 262176 | tf_op jit(solution)/shard_map/all_to_all | solution.py:363
  73.3 1.0 reduce_sum.9
  75.0 2.8 %all-to-all-start.3 = ((f32[32,8,256]{2,1,0:T(8,128)}), f32[32,8,256]{2,1,0:T(8,128)S(1)}, u32[]{:S(2)}, u32[]{:S(2)}) async-start(f32[32,8,256]{2,1,0:T(8,128)} %broadcast_in_dim.2), calls=%async_computation.3 | async-start | bytes 524288 | tf_op jit(solution)/shard_map/all_to_all | solution.py:365
  77.9 24.2 %bwd_tiles.1 = (f32[768,256]{1,0:T(8,128)}, f32[768,256]{1,0:T(8,128)}, f32[768,256]{1,0:T(8,128)}, bf16[8,256,256]{2,1,0:T(8,128)(2,1)}) custom-call(s32[6,8]{1,0:T(8,128)} %bitcast.18, s32[6]{0:T(128)} %bitcast.20, bf16[768,256]{1,0:T(8,128)(2,1)} %q_ref.5, bf16[768,256]{1,0:T(8,128)(2,1)} %k_ref.3, bf16[768,256]{1,0:T(8,128)(2,1)} %v_ref.3, ...), custom_call_target="tpu_custom_call" | custom-call | flops 1610612736 | bytes 196608 | tf_op jit(solution)/shard_map/bwd_tiles/pallas_call | solution.py:342
  102.1 2.1 %collective-permute-done.4.refs_1_ = bf16[1536,256]{1,0:T(8,128)(2,1)} collective-permute-done((bf16[1536,256]{1,0:T(8,128)(2,1)S(1)}, bf16[1536,256]{1,0:T(8,128)(2,1)}, u32[]{:S(2)}, u32[]{:S(2)}) %collective-permute-start.4) | collective-permute-done | bytes 786464 | tf_op jit(solution)/shard_map/ppermute | solution.py:356
  104.2 5.5 %collective-permute-done.3.refs_0_ = bf16[1536,256]{1,0:T(8,128)(2,1)S(1)} collective-permute-done((bf16[1536,256]{1,0:T(8,128)(2,1)S(1)}, bf16[1536,256]{1,0:T(8,128)(2,1)S(1)}, u32[]{:S(2)}, u32[]{:S(2)}) %collective-permute-start.3) | collective-permute-done | bytes 786464 | tf_op jit(solution)/shard_map/ppermute | solution.py:356
  109.7 0.9 copy-done.17
  110.6 2.1 %all-to-all-done.3 = f32[32,8,256]{2,1,0:T(8,128)S(1)} async-done(((f32[32,8,256]{2,1,0:T(8,128)}), f32[32,8,256]{2,1,0:T(8,128)S(1)}, u32[]{:S(2)}, u32[]{:S(2)}) %all-to-all-start.3) | async-done | bytes 262176 | tf_op jit(solution)/shard_map/all_to_all | solution.py:365
  112.8 3.6 %all-to-all-start.1 = ((bf16[8,256,256]{2,1,0:T(8,128)(2,1)}), bf16[8,256,256]{2,1,0:T(8,128)(2,1)S(1)}, u32[]{:S(2)}, u32[]{:S(2)}) async-start(bf16[8,256,256]{2,1,0:T(8,128)(2,1)} %after_terms.1), calls=%async_computation.1 | async-start | bytes 2097152 | tf_op jit(solution)/shard_map/all_to_all | solution.py:490
  117.1 14.6 %all-to-all-done.1.home_ref = bf16[8,256,256]{2,1,0:T(8,128)(2,1)S(1)} async-done(((bf16[8,256,256]{2,1,0:T(8,128)(2,1)}), bf16[8,256,256]{2,1,0:T(8,128)(2,1)S(1)}, u32[]{:S(2)}, u32[]{:S(2)}) %all-to-all-start.1) | async-done | bytes 1048608 | tf_op jit(solution)/shard_map/all_to_all | solution.py:490
  131.7 1.0 copy-done.16
  132.7 4.1 %final.1 = (f32[768,256]{1,0:T(8,128)}, f32[768,256]{1,0:T(8,128)}) custom-call(s32[8]{0:T(128)} %bitcast.15, f32[768,256]{1,0:T(8,128)} %get-tuple-element.69.dk_ref, f32[768,256]{1,0:T(8,128)} %get-tuple-element.70.dv_ref, bf16[8,256,256]{2,1,0:T(8,128)(2,1)} %copy-done.16, bf16[1536,256]{1,0:T(8,128)(2,1)} %copy-done.17, ...), custom_call_target="tpu_custom_call" | custom-call | bytes 7864320 | tf_op jit(solution)/shard_map/final/pallas_call | solution.py:342
  (53 shorter events, 6.3 us)
Async XLA Ops:
  0.6 1.1 copy-start.18
  1.8 0.7 copy-start.15
  4.1 11.9 %copy-start.21 = (f32[8]{0:T(128)S(1)}, f32[8]{0:T(128)}, u32[]{:S(2)}) copy-start(f32[8]{0:T(128)} %param.15) | copy-start | bytes 100
  4.1 12.6 %copy-start = (bf16[768,256]{1,0:T(8,128)(2,1)S(1)}, bf16[768,256]{1,0:T(8,128)(2,1)}, u32[]{:S(2)}) copy-start(bf16[768,256]{1,0:T(8,128)(2,1)} %refs_5_.1) | copy-start | bytes 1179652
  4.1 12.6 %copy-start.1 = (bf16[768,256]{1,0:T(8,128)(2,1)S(1)}, bf16[768,256]{1,0:T(8,128)(2,1)}, u32[]{:S(2)}) copy-start(bf16[768,256]{1,0:T(8,128)(2,1)} %q_ref.5) | copy-start | bytes 1179652
  4.1 12.6 %copy-start.8 = (bf16[256,256]{1,0:T(8,128)(2,1)S(1)}, bf16[256,256]{1,0:T(8,128)(2,1)}, u32[]{:S(2)}) copy-start(bf16[256,256]{1,0:T(8,128)(2,1)} %refs_6_.1) | copy-start | bytes 393220
  4.1 20.9 %all-to-all-start = ((bf16[8,256,256]{2,1,0:T(8,128)(2,1)}), bf16[8,256,256]{2,1,0:T(8,128)(2,1)}, u32[]{:S(2)}, u32[]{:S(2)}) async-start(bf16[8,256,256]{2,1,0:T(8,128)(2,1)} %pick.1), calls=%async_computation | async-start | bytes 2097152 | tf_op jit(solution)/shard_map/all_to_all | solution.py:395
  9.4 6.7 %copy-start.20 = (s32[1,6,8]{2,0,1:T(1,128)S(1)}, s32[1,6,8]{2,0,1:T(1,128)}, u32[]{:S(2)}) copy-start(s32[1,6,8]{2,0,1:T(1,128)} %param.16) | copy-start | bytes 580
  9.4 36.8 %collective-permute-start.2 = (bf16[1536,256]{1,0:T(8,128)(2,1)S(1)}, bf16[1536,256]{1,0:T(8,128)(2,1)}, u32[]{:S(2)}, u32[]{:S(2)}) collective-permute-start(bf16[1536,256]{1,0:T(8,128)(2,1)S(1)} %constant_dynamic-update-slice_fusion.both_ref), channel_id=1, source_target_pairs={{0,4},{1,5},{2,6},{3,7},{4,0},{5,1},{6,2},{7,3},{8,12},{9,13},{10,... | collective-permute-start | bytes 2359304 | tf_op jit(solution)/shard_map/ppermute | solution.py:356
  11.5 37.6 %collective-permute-start.1 = (bf16[1536,256]{1,0:T(8,128)(2,1)S(1)}, bf16[1536,256]{1,0:T(8,128)(2,1)}, u32[]{:S(2)}, u32[]{:S(2)}) collective-permute-start(bf16[1536,256]{1,0:T(8,128)(2,1)S(1)} %constant_dynamic-update-slice_fusion.both_ref), channel_id=1, source_target_pairs={{0,8},{1,9},{2,10},{3,11},{4,12},{5,13},{6,14},{7,15},{8,0},{9,1},... | collective-permute-start | bytes 2359304 | tf_op jit(solution)/shard_map/ppermute | solution.py:356
  13.4 37.8 %collective-permute-start = (bf16[1536,256]{1,0:T(8,128)(2,1)S(1)}, bf16[1536,256]{1,0:T(8,128)(2,1)}, u32[]{:S(2)}, u32[]{:S(2)}) collective-permute-start(bf16[1536,256]{1,0:T(8,128)(2,1)S(1)} %constant_dynamic-update-slice_fusion.both_ref), channel_id=1, source_target_pairs={{0,16},{1,17},{2,18},{3,19},{4,20},{5,21},{6,22},{7,23},{8,24},{9,... | collective-permute-start | bytes 2359304 | tf_op jit(solution)/shard_map/ppermute | solution.py:356
  16.7 0.7 copy-start.19
  17.4 28.8 %copy-start.10 = (bf16[768,256]{1,0:T(8,128)(2,1)}, bf16[768,256]{1,0:T(8,128)(2,1)S(1)}, u32[]{:S(2)}) copy-start(bf16[768,256]{1,0:T(8,128)(2,1)S(1)} %get-tuple-element.58.ga_ref) | copy-start | bytes 1179652
  17.4 50.4 %copy-start.2 = (bf16[256,768]{1,0:T(8,128)(2,1)}, bf16[256,768]{1,0:T(8,128)(2,1)S(1)}, u32[]{:S(2)}) copy-start(bf16[256,768]{1,0:T(8,128)(2,1)S(1)} %get-tuple-element.43.gat_ref.refs_4_) | copy-start | bytes 1179652
  17.4 50.4 %copy-start.9 = (bf16[256,768]{1,0:T(8,128)(2,1)}, bf16[256,768]{1,0:T(8,128)(2,1)S(1)}, u32[]{:S(2)}) copy-start(bf16[256,768]{1,0:T(8,128)(2,1)S(1)} %get-tuple-element.44.qt_ref) | copy-start | bytes 1179652
  46.1 0.7 copy-start.13
  51.2 2.2 %copy-start.5 = (f32[256,768]{1,0:T(8,128)S(1)}, f32[256,768]{1,0:T(8,128)}, u32[]{:S(2)}) copy-start(f32[256,768]{1,0:T(8,128)} %get-tuple-element.40.refs_1_) | copy-start | bytes 2359300
  53.4 0.7 copy-start.14
  56.2 0.9 copy-start.3
  57.1 0.6 copy-start.11
  57.7 0.6 copy-start.12
  58.3 15.0 %all-to-all-start.2 = ((f32[32,8,256]{2,1,0:T(8,128)}), f32[32,8,256]{2,1,0:T(8,128)}, u32[]{:S(2)}, u32[]{:S(2)}) async-start(f32[32,8,256]{2,1,0:T(8,128)} %bitcast.6), calls=%async_computation.2 | async-start | bytes 524288 | tf_op jit(solution)/shard_map/all_to_all | solution.py:363
  63.6 2.6 %copy-start.4 = (bf16[1536,256]{1,0:T(8,128)(2,1)}, bf16[1536,256]{1,0:T(8,128)(2,1)S(1)}, u32[]{:S(2)}) copy-start(bf16[1536,256]{1,0:T(8,128)(2,1)S(1)} %scatter2.1.after2_ref) | copy-start | bytes 2359300
  63.6 38.5 %collective-permute-start.5 = (bf16[1536,256]{1,0:T(8,128)(2,1)S(1)}, bf16[1536,256]{1,0:T(8,128)(2,1)}, u32[]{:S(2)}, u32[]{:S(2)}) collective-permute-start(bf16[1536,256]{1,0:T(8,128)(2,1)S(1)} %scatter2.1.after2_ref), channel_id=1, source_target_pairs={{0,4},{1,5},{2,6},{3,7},{4,0},{5,1},{6,2},{7,3},{8,12},{9,13},{10,... | collective-permute-start | bytes 2359304 | tf_op jit(solution)/shard_map/ppermute | solution.py:356
  66.2 2.4 %copy-start.6 = (bf16[1536,256]{1,0:T(8,128)(2,1)}, bf16[1536,256]{1,0:T(8,128)(2,1)S(1)}, u32[]{:S(2)}) copy-start(bf16[1536,256]{1,0:T(8,128)(2,1)S(1)} %scatter1.1.after1_ref) | copy-start | bytes 2359300
  66.2 38.0 %collective-permute-start.4 = (bf16[1536,256]{1,0:T(8,128)(2,1)S(1)}, bf16[1536,256]{1,0:T(8,128)(2,1)}, u32[]{:S(2)}, u32[]{:S(2)}) collective-permute-start(bf16[1536,256]{1,0:T(8,128)(2,1)S(1)} %scatter1.1.after1_ref), channel_id=1, source_target_pairs={{0,8},{1,9},{2,10},{3,11},{4,12},{5,13},{6,14},{7,15},{8,0},{9,1},... | collective-permute-start | bytes 2359304 | tf_op jit(solution)/shard_map/ppermute | solution.py:356
  68.6 9.2 %copy-start.7 = (bf16[1536,256]{1,0:T(8,128)(2,1)}, bf16[1536,256]{1,0:T(8,128)(2,1)S(1)}, u32[]{:S(2)}) copy-start(bf16[1536,256]{1,0:T(8,128)(2,1)S(1)} %scatter0.1.after0_ref) | copy-start | bytes 2359300
  68.6 41.1 %collective-permute-start.3 = (bf16[1536,256]{1,0:T(8,128)(2,1)S(1)}, bf16[1536,256]{1,0:T(8,128)(2,1)S(1)}, u32[]{:S(2)}, u32[]{:S(2)}) collective-permute-start(bf16[1536,256]{1,0:T(8,128)(2,1)S(1)} %scatter0.1.after0_ref), channel_id=1, source_target_pairs={{0,16},{1,17},{2,18},{3,19},{4,20},{5,21},{6,22},{7,23},{8,24},{9,... | collective-permute-start | bytes 2359304 | tf_op jit(solution)/shard_map/ppermute | solution.py:356
  75.0 37.7 %all-to-all-start.3 = ((f32[32,8,256]{2,1,0:T(8,128)}), f32[32,8,256]{2,1,0:T(8,128)S(1)}, u32[]{:S(2)}, u32[]{:S(2)}) async-start(f32[32,8,256]{2,1,0:T(8,128)} %broadcast_in_dim.2), calls=%async_computation.3 | async-start | bytes 524288 | tf_op jit(solution)/shard_map/all_to_all | solution.py:365
  109.7 0.9 copy-start.17
  112.8 18.9 %all-to-all-start.1 = ((bf16[8,256,256]{2,1,0:T(8,128)(2,1)}), bf16[8,256,256]{2,1,0:T(8,128)(2,1)S(1)}, u32[]{:S(2)}, u32[]{:S(2)}) async-start(bf16[8,256,256]{2,1,0:T(8,128)(2,1)} %after_terms.1), calls=%async_computation.1 | async-start | bytes 2097152 | tf_op jit(solution)/shard_map/all_to_all | solution.py:490
  131.7 1.0 copy-start.16
